TPU v7x, 32 devices: a whole 2x2x4 slice. The times are simulated.
32 devices in a mesh: ctx: 8 (over z, x), head: 4 (over y, core).
Axes of the slice: x: 2, y: 2, z: 4, core: 2. Of those that a mesh axis runs over, the one named last changes fastest.
Arguments:
- queries: bfloat16 [64, 8192], P('ctx', 'head'), may hold values from -16 to 16
- keys: bfloat16 [262144, 8, 128], P('ctx', 'head'), may hold values from -16 to 16
- values: bfloat16 [262144, 8, 128], P('ctx', 'head'), may hold values from -4 to 4
- offsets: int32 [8], P('ctx'), may hold values from 0 to 229376, as said below
- lengths: int32 [64], replicated, may hold values from 131072 to 262144
- residual: bfloat16 [64, 5120], P(None, 'ctx'), may hold values from -2 to 2
- wo: bfloat16 [8192, 5120], P('head', 'ctx'), may hold values from -0.0625 to 0.0625
- norm_gain: float32 [5120], P('ctx'), may hold values from 0.1 to 1.9
- w_gate: bfloat16 [5120, 25600], P('ctx', 'head'), may hold values from -0.078125 to 0.078125
- w_up: bfloat16 [5120, 25600], P('ctx', 'head'), may hold values from -0.078125 to 0.078125
- w_down: bfloat16 [25600, 5120], P('head', 'ctx'), may hold values from -0.0390625 to 0.0390625
Outputs:
- attended: bfloat16 [64, 8192], P('ctx', 'head')
- stream: bfloat16 [64, 5120], P(None, 'ctx')
- ffn_out: bfloat16 [64, 5120], P('head', 'ctx')
Inputs may be any that keep to these rules, and one draw needn't show every extreme that they name: offsets holds each of 0, 32768, ..., 229376 once.
All inputs are finite; a program needn't handle non-finite values.
Results may differ from a plain program's by a relative error of at most 0.02.
Values may be sent and summed in bfloat16 or wider, within the bound.
No kernel may reach another device: no remote copies, remote signals or barrier semaphores. Data moves between devices by JAX's collectives and lax.ppermute only.
A program may use at most 128 MiB of HBM per device.

v0:
```python
import math

import jax
import jax.numpy as jnp
from jax import lax
from jax.sharding import PartitionSpec as P

D = 5120


masked_score = -1e30
epsilon = 1e-06


def activate(gate, upward, square_total):
    scale = lax.rsqrt(square_total / D + epsilon)[:, None]
    return (jax.nn.silu(scale * gate) * (scale * upward)).astype(jnp.bfloat16)


def local(queries, keys, values, offsets, lengths, residual, wo, norm_gain, w_gate, w_up, w_down):
    head_size = keys.shape[2]
    kv_local = keys.shape[1]
    rows_local = queries.shape[0]
    everyone = lax.all_gather(queries, "ctx", axis=0, tiled=True)
    batch = everyone.shape[0]
    groups = everyone.shape[1] // (kv_local * head_size)
    query_heads = everyone.reshape(batch, kv_local, groups, head_size)
    query_heads = query_heads.transpose(1, 0, 2, 3).reshape(kv_local, batch * groups, head_size)
    row_limit = jnp.repeat(lengths, groups)
    inverse_root = 1.0 / math.sqrt(head_size)
    span = keys.shape[0]
    block = min(2048, span)
    turns = span // block
    shard_begin = offsets[0]

    def visit(carry, block_index):
        row_high, row_total, row_acc = carry
        first_slot = block_index * block
        key_block = lax.dynamic_slice_in_dim(keys, first_slot, block, 0)
        value_block = lax.dynamic_slice_in_dim(values, first_slot, block, 0)
        scores = (
            jnp.einsum("hrd,khd->hrk", query_heads, key_block, preferred_element_type=jnp.float32)
            * inverse_root
        )
        position = shard_begin + first_slot + jnp.arange(block, dtype=jnp.int32)
        scores = jnp.where(position[None, None, :] < row_limit[None, :, None], scores, masked_score)
        new_high = jnp.maximum(row_high, jnp.max(scores, axis=2))
        weights = jnp.exp(scores - new_high[:, :, None])
        rescale = jnp.exp(row_high - new_high)
        row_total = row_total * rescale + jnp.sum(weights, axis=2)
        update = jnp.einsum(
            "hrk,khd->hrd",
            weights.astype(jnp.bfloat16),
            value_block,
            preferred_element_type=jnp.float32,
        )
        row_acc = row_acc * rescale[:, :, None] + update
        return ((new_high, row_total, row_acc), None)

    start_high = jnp.full((kv_local, batch * groups), masked_score, jnp.float32)
    start_total = jnp.zeros((kv_local, batch * groups), jnp.float32)
    start_acc = jnp.zeros((kv_local, batch * groups, head_size), jnp.float32)
    (row_high, row_total, row_acc), _ = lax.scan(
        visit, (start_high, start_total, start_acc), jnp.arange(turns, dtype=jnp.int32)
    )
    heads_local = kv_local * groups
    row_high = (
        row_high.reshape(kv_local, batch, groups).transpose(1, 0, 2).reshape(batch, heads_local)
    )
    row_total = (
        row_total.reshape(kv_local, batch, groups).transpose(1, 0, 2).reshape(batch, heads_local)
    )
    row_acc = (
        row_acc.reshape(kv_local, batch, groups, head_size)
        .transpose(1, 0, 2, 3)
        .reshape(batch, heads_local, head_size)
    )
    part_acc = lax.all_to_all(row_acc, "ctx", split_axis=0, concat_axis=0, tiled=True)
    part_high = lax.all_to_all(row_high, "ctx", split_axis=0, concat_axis=0, tiled=True)
    part_total = lax.all_to_all(row_total, "ctx", split_axis=0, concat_axis=0, tiled=True)
    sources = part_acc.shape[0] // rows_local
    part_acc = part_acc.reshape(sources, rows_local, part_acc.shape[1], part_acc.shape[2])
    part_high = part_high.reshape(sources, rows_local, part_high.shape[1])
    part_total = part_total.reshape(sources, rows_local, part_total.shape[1])
    top_score = jnp.max(part_high, axis=0)
    rescale = jnp.exp(part_high - top_score[None])
    denominator = jnp.sum(part_total * rescale, axis=0)
    numerator = jnp.sum(part_acc * rescale[:, :, :, None], axis=0)
    merged = (numerator / denominator[:, :, None]).astype(jnp.bfloat16)
    attended = merged.reshape(rows_local, heads_local * head_size)
    projected = jnp.dot(
        lax.all_gather(attended, "ctx", axis=0, tiled=True), wo, preferred_element_type=jnp.float32
    )
    mixed = lax.psum(projected, "head")
    combined = residual.astype(jnp.float32) + mixed
    stream = combined.astype(jnp.bfloat16)
    squares = jnp.sum(combined * combined, axis=1)
    normed = (combined * norm_gain).astype(jnp.bfloat16)
    gate_part = jnp.dot(normed, w_gate, preferred_element_type=jnp.float32)
    up_part = jnp.dot(normed, w_up, preferred_element_type=jnp.float32)
    square_total = lax.psum(squares, "ctx")
    gate, upward = lax.psum((gate_part, up_part), "ctx")
    hidden = activate(gate, upward, square_total)
    ffn_out = lax.psum_scatter(
        jnp.dot(hidden, w_down, preferred_element_type=jnp.float32),
        "head",
        scatter_dimension=0,
        tiled=True,
    ).astype(jnp.bfloat16)
    return (attended, stream, ffn_out)


def solution(mesh):
    return jax.shard_map(
        local,
        mesh=mesh,
        in_specs=(
            P("ctx", "head"),
            P("ctx", "head", None),
            P("ctx", "head", None),
            P("ctx"),
            P(),
            P(None, "ctx"),
            P("head", "ctx"),
            P("ctx"),
            P("ctx", "head"),
            P("ctx", "head"),
            P("head", "ctx"),
        ),
        out_specs=(P("ctx", "head"), P(None, "ctx"), P("head", "ctx")),
        check_vma=False,
    )
```

profile of v0, /device:TPU:0, one launch (start us, length us, event | category | flops | bytes accessed | tf_op | source)
XLA Modules:
  0.0 727.9 jit_solution(1557931857765369294)
XLA Ops:
  7.2 32.9 %all_gather.6 = bf16[64,2048]{1,0:T(8,128)(2,1)S(1)} all-gather(bf16[8,2048]{1,0:T(8,128)(2,1)} %param.13), channel_id=1, replica_groups=mesh['ctx'=8,'head'=4] {'ctx'}, dimensions={0}, use_global_device_ids=true | all-gather | bytes 294912 | tf_op jit(solution)/shard_map/all_gather | solution.py:24
  40.2 407.4 %while.15 = (s32[]{:T(128)}, f32[2,512]{1,0:T(2,128)S(1)}, f32[2,512]{1,0:T(2,128)S(1)}, f32[2,512,128]{2,1,0:T(8,128)S(1)}, s32[16]{0:T(128)S(1)}, /*index=5*/s...) while((s32[]{:T(128)}, f32[2,512]{1,0:T(2,128)S(1)}, ...), condition=%wide.region_3.4_spmd.clone, body=%wide.region_0.3_spmd.clone.sunk | while | flops 1098259456 | bytes 78996016 | solution.py:63
  48.5 6.4 fusion.47
  54.9 4.8 fusion.49
  74.0 6.4 fusion.47
  80.4 4.8 fusion.49
  99.4 6.4 fusion.47
  124.9 6.4 fusion.47
  150.4 6.4 fusion.47
  175.8 6.4 fusion.47
  201.3 6.4 fusion.47
  226.7 6.4 fusion.47
  252.2 6.4 fusion.47
  277.6 6.4 fusion.47
  303.1 6.4 fusion.47
  328.5 6.4 fusion.47
  354.0 6.4 fusion.47
  379.4 6.4 fusion.47
  404.9 6.4 fusion.47
  430.3 6.4 fusion.47
  448.5 5.5 all-to-all-start.1
  455.0 5.5 all-to-all-done.1
  464.6 5.6 all-to-all-done.2
  475.8 8.3 %all-to-all-done = f32[64,16,128]{2,1,0:T(8,128)S(1)} async-done(((f32[64,16,128]{2,1,0:T(8,128)}), f32[64,16,128]{2,1,0:T(8,128)S(1)}, u32[]{:S(2)}, u32[]{:S(2)}) %all-to-all-start) | async-done | bytes 524320 | tf_op jit(solution)/shard_map/all_to_all | solution.py:78
  484.4 30.7 %all_gather.7 = bf16[64,2048]{1,0:T(8,128)(2,1)S(1)} all-gather(bf16[8,2048]{1,0:T(8,128)(2,1)S(1)} %bitcast.60), channel_id=1, replica_groups=mesh['ctx'=8,'head'=4] {'ctx'}, dimensions={0}, use_global_device_ids=true | all-gather | bytes 294912 | tf_op jit(solution)/shard_map/all_gather | solution.py:92
  516.5 30.9 %all-reduce.4.cloned.1.call-done = f32[64,640]{1,0:T(8,128)} async-done(((f32[64,640]{1,0:T(8,128)}), f32[64,640]{1,0:T(8,128)}) %all-reduce.4.cloned.1.call-update) | async-done | bytes 163856 | tf_op jit(solution)/shard_map/psum | solution.py:94
  549.1 5.8 fusion.25
  554.9 5.8 fusion.26
  560.8 22.2 %psum.29 = f32[64]{0:T(128)S(1)} all-reduce(f32[64]{0:T(128)S(1)} %get-tuple-element.166), channel_id=1, replica_groups=mesh['ctx'=8,'head'=4] {'ctx'}, use_global_device_ids=true, to_apply=%region_9.10 | all-reduce | flops 64 | bytes 512 | tf_op jit(solution)/shard_map/psum | solution.py:101
  583.0 111.6 %all-reduce.6.cloned.1.call-done = (f32[64,6400]{1,0:T(8,128)}, f32[64,6400]{1,0:T(8,128)}) async-done(((f32[64,6400]{1,0:T(8,128)}, f32[64,6400]{1,0:T(8,128)}), (f32[64,6400]{1,0:T(8,128)}, f32[64,6400]{1,0:T(8,128)})) %all-reduce.6.cloned.1.call-update) | async-done | bytes 3276816 | tf_op jit(solution)/shard_map/psum | solution.py:102
  694.6 6.5 fusion.18
  701.1 18.8 %reduce-scatter.2.cloned.1.call-done = f32[16,640]{1,0:T(8,128)} async-done(((f32[64,640]{1,0:T(8,128)}), f32[16,640]{1,0:T(8,128)}) %reduce-scatter.2.cloned.1.call-update) | async-done | bytes 40976 | tf_op jit(solution)/shard_map/reduce_scatter | solution.py:104
  (315 shorter events, 289.8 us)
Async XLA Ops:
  7.2 508.0 %copy-start = (bf16[2048,640]{1,0:T(8,128)(2,1)S(1)}, bf16[2048,640]{1,0:T(8,128)(2,1)}, u32[]{:S(2)}) copy-start(bf16[2048,640]{1,0:T(8,128)(2,1)} %param.19) | copy-start | bytes 7864324
  40.2 507.2 %copy-start.5 = (bf16[64,640]{1,0:T(8,128)(2,1)S(1)}, bf16[64,640]{1,0:T(8,128)(2,1)}, u32[]{:S(2)}) copy-start(bf16[64,640]{1,0:T(8,128)(2,1)} %param.18) | copy-start | bytes 245764
  40.2 507.2 %copy-start.6 = (f32[640]{0:T(1024)S(1)}, f32[640]{0:T(1024)}, u32[]{:S(2)}) copy-start(f32[640]{0:T(1024)} %param.20) | copy-start | bytes 7684
  54.9 6.4 copy-start.3
  80.4 6.1 copy-start.1
  80.4 6.4 copy-start.3
  105.8 6.4 copy-start.3
  131.3 6.4 copy-start.3
  156.8 6.4 copy-start.3
  182.2 6.4 copy-start.3
  207.7 6.4 copy-start.3
  233.1 6.1 copy-start.1
  233.1 6.4 copy-start.3
  258.6 6.1 copy-start.1
  258.6 6.4 copy-start.3
  284.0 6.1 copy-start.1
  284.0 6.4 copy-start.3
  309.5 6.1 copy-start.1
  309.5 6.4 copy-start.3
  334.9 6.1 copy-start.1
  334.9 6.4 copy-start.3
  360.4 6.4 copy-start.3
  385.8 6.4 copy-start.3
  411.3 6.4 copy-start.3
  436.7 6.4 copy-start.3
  448.5 11.9 %all-to-all-start.1 = ((f32[8,1,128]{2,1,0:T(1,128)}), f32[8,1,128]{2,1,0:T(1,128)S(1)}, u32[]{:S(2)}, u32[]{:S(2)}) async-start(f32[8,1,128]{2,1,0:T(1,128)} %reshape.104), calls=%async_computation.1 | async-start | bytes 8192 | tf_op jit(solution)/shard_map/all_to_all | solution.py:79
  460.4 9.8 %all-to-all-start.2 = ((f32[8,1,128]{2,1,0:T(1,128)}), f32[8,1,128]{2,1,0:T(1,128)S(1)}, u32[]{:S(2)}, u32[]{:S(2)}) async-start(f32[8,1,128]{2,1,0:T(1,128)} %reshape.106), calls=%async_computation.2 | async-start | bytes 8192 | tf_op jit(solution)/shard_map/all_to_all | solution.py:80
  470.2 13.9 %all-to-all-start = ((f32[64,16,128]{2,1,0:T(8,128)}), f32[64,16,128]{2,1,0:T(8,128)S(1)}, u32[]{:S(2)}, u32[]{:S(2)}) async-start(f32[64,16,128]{2,1,0:T(8,128)} %copy_bitcast_fusion), calls=%async_computation | async-start | bytes 1048576 | tf_op jit(solution)/shard_map/all_to_all | solution.py:78
  473.7 73.7 %all-reduce.4.cloned.1.call-start = ((), (), s32[]{:S(2)}) async-start(), calls=%async_computation.4 | async-start | bytes 327680 | tf_op jit(solution)/shard_map/psum | solution.py:94
  484.4 70.5 %copy-start.4 = (bf16[1,8,16,128]{3,1,2,0:T(8,128)(2,1)}, bf16[1,8,16,128]{3,1,2,0:T(8,128)(2,1)S(1)}, u32[]{:S(2)}) copy-start(bf16[1,8,16,128]{3,1,2,0:T(8,128)(2,1)S(1)} %copy.61) | copy-start | bytes 98308
  516.4 178.2 %all-reduce.6.cloned.1.call-start = ((), (), s32[]{:S(2)}) async-start(), calls=%async_computation.6 | async-start | bytes 6553600 | tf_op jit(solution)/shard_map/psum | solution.py:102
  560.7 159.3 %reduce-scatter.2.cloned.1.call-start = ((), (), s32[]{:S(2)}) async-start(), calls=%async_computation.5 | async-start | bytes 204800 | tf_op jit(solution)/shard_map/reduce_scatter | solution.py:104
  (26 other events, 77.1 us)
Sparse Core Ops, SparseCore 0:
  516.5 30.8 all-reduce.3
  560.9 133.6 all-reduce.5
  701.3 18.6 reduce-scatter.1
where the time goes:
time: 731 us; the launch traced here: 728 us
  matrix products  193 us (26%)
  waiting for transfers between devices  181 us (25%)
  local copies, waits for them, and re-layouts  126 us (17%)
  other arithmetic  94 us (13%)
  blocking collectives  85.8 us (12%)
  loops' own time  22 us (3%)
  between operations  13.9 us (2%)
  starting transfers between devices  12.5 us (2%)
    psum x1, waiting for transfers between devices, local(): gate, upward = lax.psum((gate_part, up_part), 'ctx')  112 us
    dot_general x16, matrix products, visit(): jnp.einsum('hrd,khd->hrk', query_heads, key_block, preferred_element_type...  102 us
    reduce_sum x16, other arithmetic, visit(): row_total = row_total * rescale + jnp.sum(weights, axis=2)  76.5 us
    dot_general x16, matrix products, visit(): jnp.einsum('hrk,khd->hrd', weights.astype(jnp.bfloat16), value_block, pre...  71.6 us
    dynamic_slice x16, local copies, waits for them, and re-layouts, visit(): value_block = lax.dynamic_slice_in_dim(values, first_slot, block, 0)  59.4 us
    while x112, local copies, waits for them, and re-layouts  40.4 us
    all_gather x1, blocking collectives, local(): everyone = lax.all_gather(queries, 'ctx', axis=0, tiled=True)  32.9 us
    psum x1, waiting for transfers between devices, local(): mixed = lax.psum(projected, 'head')  30.9 us
  transfers between devices with their start and end apart: 6, of which 6 were waited for; matrix products, arithmetic and copies ran while one was open for 1% of the time, Pallas kernels for 0%

commit v1 on v0

v1 whole, which is shorter than its diff:
```python
import functools
import math

import jax
import jax.numpy as jnp
from jax import lax
from jax.experimental import pallas as pl
from jax.experimental.pallas import tpu as pltpu
from jax.sharding import PartitionSpec as P

hidden_score = -1e30
lowest_base = -65536.0
largest_sum = 2.0**115
epsilon = 1e-06
lane = 128


def split_heads(block, kv_local, head_size):
    flat = block.reshape(block.shape[0], kv_local * head_size)
    return [flat[:, h * head_size : (h + 1) * head_size] for h in range(kv_local)]


def hidden_slots(first_slot, count, limits):
    slot = lax.broadcasted_iota(jnp.int32, (count, limits.shape[1]), 0) + first_slot
    return jnp.where(slot < limits, 0.0, 1.0).astype(jnp.bfloat16)


def scores_of(key_block, hidden, query_cols):
    return jnp.dot(
        jnp.concatenate([key_block, hidden], axis=1), query_cols, preferred_element_type=jnp.float32
    )


def weighted_values(value_block, weights):
    return lax.dot_general(
        value_block,
        weights.astype(jnp.bfloat16),
        (((0,), (0,)), ((), ())),
        preferred_element_type=jnp.float32,
    )


def sublane_sums(weights):
    return jnp.sum(weights.reshape(weights.shape[0] // 8, 8, weights.shape[1]), axis=0)


def attention_kernel(
    query_ref,
    limit_ref,
    key_ref,
    value_ref,
    all_keys,
    all_values,
    out_ref,
    query_cols,
    base_ref,
    acc_ref,
    total_ref,
    spare_keys,
    spare_values,
    copy_sems,
    *,
    kv_local,
    groups,
    sources,
    factor,
):
    step = pl.program_id(0)
    batch = query_ref.shape[0]
    head_size = key_ref.shape[2]
    block = key_ref.shape[0]
    columns = batch * groups
    extra = limit_ref.shape[1]
    limits = limit_ref[...]

    @pl.when(step == 0)
    def start():
        row = lax.broadcasted_iota(jnp.int32, (extra, columns), 0)
        column = lax.broadcasted_iota(jnp.int32, (extra, columns), 1)
        mask_rows = jnp.where(lax.rem(column, batch) == row, hidden_score, 0.0)
        probe = min(512, block)
        hidden = hidden_slots(0, probe, limits)
        first_keys = split_heads(key_ref[pl.ds(0, probe)], kv_local, head_size)
        for h in range(kv_local):
            rows = [
                query_ref[:, (h * groups + g) * head_size : (h * groups + g + 1) * head_size]
                for g in range(groups)
            ]
            turned = jnp.concatenate(rows, axis=0).astype(jnp.float32).T
            query_cols[h, :head_size] = turned.astype(jnp.bfloat16)
            query_cols[h, head_size:] = mask_rows.astype(jnp.bfloat16)
            top = jnp.max(
                scores_of(first_keys[h], hidden, query_cols[h]), axis=0, keepdims=True
            )
            base = jnp.maximum(top, lowest_base).astype(jnp.bfloat16).astype(jnp.float32)
            base_ref[h] = base
            query_cols[h, head_size:] = jnp.where(row == batch, -base, mask_rows).astype(
                jnp.bfloat16
            )
        acc_ref[...] = jnp.zeros_like(acc_ref)
        total_ref[...] = jnp.zeros_like(total_ref)

    hidden = hidden_slots(step * block, block, limits)
    keys = split_heads(key_ref[...], kv_local, head_size)
    values = split_heads(value_ref[...], kv_local, head_size)
    for h in range(kv_local):
        weights = jnp.exp2(scores_of(keys[h], hidden, query_cols[h]) * factor)
        total_ref[h] += sublane_sums(weights)
        acc_ref[h] += weighted_values(values[h], weights)

    @pl.when(step == pl.num_programs(0) - 1)
    def finish():
        @pl.when(jnp.logical_not(jnp.max(total_ref[...]) <= largest_sum))
        def redo():
            piece = spare_keys.shape[0]
            for h in range(kv_local):
                row = lax.broadcasted_iota(jnp.int32, (extra, columns), 0)
                old = query_cols[h, head_size:].astype(jnp.float32)
                query_cols[h, head_size:] = jnp.where(row == batch, 0.0, old).astype(jnp.bfloat16)
            base_ref[...] = jnp.full_like(base_ref, lowest_base)
            acc_ref[...] = jnp.zeros_like(acc_ref)
            total_ref[...] = jnp.zeros_like(total_ref)

            def visit(turn, carry):
                first = turn * piece
                here = pl.ds(first, piece)
                get_keys = pltpu.make_async_copy(all_keys.at[here], spare_keys, copy_sems.at[0])
                get_values = pltpu.make_async_copy(
                    all_values.at[here], spare_values, copy_sems.at[1]
                )
                get_keys.start()
                get_values.start()
                get_keys.wait()
                get_values.wait()
                hidden = hidden_slots(first, piece, limits)
                keys = split_heads(spare_keys[...], kv_local, head_size)
                values = split_heads(spare_values[...], kv_local, head_size)
                for h in range(kv_local):
                    scores = scores_of(keys[h], hidden, query_cols[h])
                    old = base_ref[h]
                    new = jnp.maximum(old, jnp.max(scores, axis=0, keepdims=True))
                    rescale = jnp.exp2((old - new) * factor)
                    weights = jnp.exp2((scores - new) * factor)
                    base_ref[h] = new
                    total_ref[h] = total_ref[h] * rescale + sublane_sums(weights)
                    acc_ref[h] = acc_ref[h] * rescale + weighted_values(values[h], weights)
                return carry

            lax.fori_loop(0, all_keys.shape[0] // piece, visit, 0)

        rows_local = batch // sources
        stat_row = lax.broadcasted_iota(jnp.int32, (head_size, columns), 0)
        stats = jnp.zeros((head_size, columns), jnp.float32)
        for h in range(kv_local):
            total = jnp.sum(total_ref[h], axis=0, keepdims=True)
            seen = total > 0.0
            safe = jnp.where(seen, total, 1.0)
            height = jnp.where(seen, base_ref[h] * factor + jnp.log2(safe), hidden_score)
            for piece in range(3):
                part = height.astype(jnp.bfloat16).astype(jnp.float32)
                stats = jnp.where(stat_row == 3 * h + piece, part, stats)
                height = height - part
            mean = (acc_ref[h] * (1.0 / safe)).T.astype(jnp.bfloat16)
            for c in range(sources):
                for g in range(groups):
                    out_ref[c, h, g * rows_local : (g + 1) * rows_local] = mean[
                        g * batch + c * rows_local : g * batch + (c + 1) * rows_local
                    ]
        stats = stats.T.astype(jnp.bfloat16)
        for c in range(sources):
            for g in range(groups):
                out_ref[c, kv_local, g * rows_local : (g + 1) * rows_local] = stats[
                    g * batch + c * rows_local : g * batch + (c + 1) * rows_local
                ]


def attention(queries, limits, keys, values, sources, groups):
    span, kv_local, head_size = keys.shape
    batch = queries.shape[0]
    columns = batch * groups
    block = math.gcd(4096, span)
    piece = math.gcd(1024, span)
    extra = limits.shape[1]
    whole = lambda *shape: pl.BlockSpec(shape, lambda j: (0,) * len(shape))
    part = pl.BlockSpec((block, kv_local, head_size), lambda j: (j, 0, 0))
    out = (sources, kv_local + 1, columns // sources, head_size)
    return pl.pallas_call(
        functools.partial(
            attention_kernel,
            kv_local=kv_local,
            groups=groups,
            sources=sources,
            factor=math.log2(math.e) / math.sqrt(head_size),
        ),
        grid=(span // block,),
        in_specs=[
            whole(batch, queries.shape[1]),
            whole(1, extra),
            part,
            part,
            pl.BlockSpec(memory_space=pl.ANY),
            pl.BlockSpec(memory_space=pl.ANY),
        ],
        out_specs=whole(*out),
        out_shape=jax.ShapeDtypeStruct(out, jnp.bfloat16),
        scratch_shapes=[
            pltpu.VMEM((kv_local, head_size + extra, columns), jnp.bfloat16),
            pltpu.VMEM((kv_local, 1, columns), jnp.float32),
            pltpu.VMEM((kv_local, head_size, columns), jnp.float32),
            pltpu.VMEM((kv_local, 8, columns), jnp.float32),
            pltpu.VMEM((piece, kv_local, head_size), jnp.bfloat16),
            pltpu.VMEM((piece, kv_local, head_size), jnp.bfloat16),
            pltpu.SemaphoreType.DMA((2,)),
        ],
        compiler_params=pltpu.CompilerParams(
            dimension_semantics=("arbitrary",), vmem_limit_bytes=48 * 2**20
        ),
        cost_estimate=pl.CostEstimate(
            flops=4 * span * columns * kv_local * head_size,
            bytes_accessed=4 * span * kv_local * head_size,
            transcendentals=span * columns * kv_local,
        ),
    )(queries, limits, keys, values, keys, values)


def merge_kernel(part_ref, out_ref, *, kv_local, groups):
    sources, _, rows, head_size = part_ref.shape
    rows_local = rows // groups
    for h in range(kv_local):
        heights = []
        for c in range(sources):
            stats = part_ref[c, kv_local].astype(jnp.float32)
            heights.append(
                stats[:, 3 * h : 3 * h + 1]
                + stats[:, 3 * h + 1 : 3 * h + 2]
                + stats[:, 3 * h + 2 : 3 * h + 3]
            )
        top = functools.reduce(jnp.maximum, heights)
        shares = [jnp.exp2(height - top) for height in heights]
        whole = sum(shares)
        mean = sum(
            share * part_ref[c, h].astype(jnp.float32) for c, share in enumerate(shares)
        ) / whole
        for g in range(groups):
            out_ref[:, (h * groups + g) * head_size : (h * groups + g + 1) * head_size] = mean[
                g * rows_local : (g + 1) * rows_local
            ].astype(jnp.bfloat16)


def merge(parts, kv_local, groups):
    rows_local = parts.shape[2] // groups
    return pl.pallas_call(
        functools.partial(merge_kernel, kv_local=kv_local, groups=groups),
        out_shape=jax.ShapeDtypeStruct(
            (rows_local, kv_local * groups * parts.shape[3]), jnp.bfloat16
        ),
    )(parts)


def gather_rows(block, sources):
    copies = jnp.broadcast_to(block[None], (sources,) + block.shape)
    gathered = lax.all_to_all(copies, "ctx", split_axis=0, concat_axis=0)
    return gathered.reshape((sources * block.shape[0],) + block.shape[1:])


def swap(block, axis, size, bit):
    return lax.ppermute(block, axis, [(i, i ^ bit) for i in range(size)])


def sum_over_head(block, size):
    bit = 1
    while bit < size:
        block = block + swap(block, "head", size, bit)
        bit *= 2
    return block


def scatter_sum_over_head(block, size):
    me = lax.axis_index("head")
    bit = size // 2
    while bit >= 1:
        halves = block.reshape((2, block.shape[0] // 2) + block.shape[1:])
        side = lax.rem(me // bit, 2)
        keep = lax.dynamic_index_in_dim(halves, side, 0, keepdims=False)
        give = lax.dynamic_index_in_dim(halves, 1 - side, 0, keepdims=False)
        block = keep + swap(give, "head", size, bit)
        bit //= 2
    return block


def three_parts(column):
    parts = []
    for _ in range(3):
        part = column.astype(jnp.bfloat16)
        parts.append(part)
        column = column - part.astype(jnp.float32)
    return jnp.stack(parts, axis=-1)


def local_step(sources, heads):
    def local(
        queries, keys, values, offsets, lengths, residual, wo, norm_gain, w_gate, w_up, w_down
    ):
        head_size = keys.shape[2]
        kv_local = keys.shape[1]
        rows_local = queries.shape[0]
        groups = queries.shape[1] // (kv_local * head_size)
        batch = lengths.shape[0]
        width = residual.shape[1] * sources
        everyone = gather_rows(queries, sources)
        extra = -(-(batch + 1) // lane) * lane
        limits = jnp.full((extra,), jnp.iinfo(jnp.int32).max, jnp.int32)
        limits = limits.at[:batch].set(lengths - offsets[0]).at[batch].set(-1)
        parts = attention(everyone, limits[None], keys, values, sources, groups)
        parts = lax.all_to_all(parts, "ctx", split_axis=0, concat_axis=0)
        attended = merge(parts, kv_local, groups)
        projected = jnp.dot(
            gather_rows(attended, sources), wo, preferred_element_type=jnp.float32
        )
        combined = residual.astype(jnp.float32) + sum_over_head(projected, heads)
        stream = combined.astype(jnp.bfloat16)
        squares = three_parts(jnp.sum(combined * combined, axis=1))
        normed = (combined * norm_gain).astype(jnp.bfloat16)
        gate_part = jnp.dot(normed, w_gate, preferred_element_type=jnp.float32)
        up_part = jnp.dot(normed, w_up, preferred_element_type=jnp.float32)
        hidden_units = w_gate.shape[1]
        terms = jnp.concatenate(
            [
                gate_part.astype(jnp.bfloat16),
                up_part.astype(jnp.bfloat16),
                jnp.pad(squares, ((0, 0), (0, lane - squares.shape[1]))),
            ],
            axis=1,
        )
        terms = lax.all_to_all(
            terms.reshape(sources, rows_local, -1), "ctx", split_axis=0, concat_axis=0
        )
        terms = jnp.sum(terms.astype(jnp.float32), axis=0)
        square_total = jnp.sum(terms[:, 2 * hidden_units : 2 * hidden_units + 3], axis=1)
        scale = lax.rsqrt(square_total / width + epsilon)[:, None]
        gate = scale * terms[:, :hidden_units]
        upward = scale * terms[:, hidden_units : 2 * hidden_units]
        hidden = (jax.nn.silu(gate) * upward).astype(jnp.bfloat16)
        down = jnp.dot(
            gather_rows(hidden, sources), w_down, preferred_element_type=jnp.float32
        )
        ffn_out = scatter_sum_over_head(down, heads).astype(jnp.bfloat16)
        return (attended, stream, ffn_out)

    return local


def solution(mesh):
    return jax.shard_map(
        local_step(mesh.shape["ctx"], mesh.shape["head"]),
        mesh=mesh,
        in_specs=(
            P("ctx", "head"),
            P("ctx", "head", None),
            P("ctx", "head", None),
            P("ctx"),
            P(),
            P(None, "ctx"),
            P("head", "ctx"),
            P("ctx"),
            P("ctx", "head"),
            P("ctx", "head"),
            P("head", "ctx"),
        ),
        out_specs=(P("ctx", "head"), P(None, "ctx"), P("head", "ctx")),
        check_vma=False,
    )
```

time: 731 us -> 319 us (0.44)
  matrix products: 193 us -> 14.6 us
  waiting for transfers between devices: 181 us -> 38.7 us
  local copies, waits for them, and re-layouts: 126 us -> 4.26 us
  blocking collectives: 85.8 us -> 194 us
  other arithmetic: 94 us -> 4.52 us
  Pallas kernels: 0 us -> 47.7 us
  loops' own time: 22 us -> 0 us
  between operations: 13.9 us -> 1.48 us
    all_to_all x0 -> x3, blocking collectives: none -> 194 us  [the longest x1 142 us: local(): parts = lax.all_to_all(parts, 'ctx', split_axis=0, concat_axis=0)]
    dot_general x34 -> x2, matrix products: 182 us -> 5.49 us  [the longest x1 4.96 us: local(): jnp.dot(gather_rows(hidden, sources), w_down, preferred_element_type=jnp....]
    psum x2 -> x0, waiting for transfers between devices: 143 us -> none  [the longest x1 112 us: local(): gate, upward = lax.psum((gate_part, up_part), 'ctx')]
    reduce_sum x19 -> x3, other arithmetic: 78.4 us -> 0.48 us  [the longest x1 0.23 us: local(): terms = jnp.sum(terms.astype(jnp.float32), axis=0)]
    dynamic_slice x32 -> x0, local copies, waits for them, and re-layouts: 68.8 us -> none  [the longest x16 59.4 us: visit(): value_block = lax.dynamic_slice_in_dim(values, first_slot, block, 0)]
    all_gather x2 -> x0, blocking collectives: 63.6 us -> none  [the longest x1 32.9 us: local(): everyone = lax.all_gather(queries, 'ctx', axis=0, tiled=True)]
    pallas_call x0 -> x2, Pallas kernels: none -> 47.7 us  [the longest x1 45.6 us: attention(): pl.pallas_call(functools.partial(attention_kernel, kv_local=kv_local, gro...]
    while x112 -> x0, local copies, waits for them, and re-layouts: 40.4 us -> none
  transfers between devices with their start and end apart: 6 -> 6, of which waited for: 6 -> 5; matrix products, arithmetic and copies ran while one was open for 1% -> 1% of each run, Pallas kernels for 0% -> 0%
where the time goes in v1:
time: 319 us; the launch traced here: 317 us
  blocking collectives  194 us (61%)
  Pallas kernels  47.7 us (15%)
  waiting for transfers between devices  38.7 us (12%)
  matrix products  14.6 us (5%)
  starting transfers between devices  11.7 us (4%)
  other arithmetic  4.52 us (1%)
  local copies, waits for them, and re-layouts  4.26 us (1%)
    all_to_all x1, blocking collectives, local(): parts = lax.all_to_all(parts, 'ctx', split_axis=0, concat_axis=0)  142 us
    pallas_call x1, Pallas kernels, attention(): pl.pallas_call(functools.partial(attention_kernel, kv_local=kv_local, gro...  45.6 us
    all_to_all x1, blocking collectives, local(): lax.all_to_all(terms.reshape(sources, rows_local, -1), 'ctx', split_axis=...  41.5 us
    all_to_all x2, waiting for transfers between devices, gather_rows(): gathered = lax.all_to_all(copies, 'ctx', split_axis=0, concat_axis=0)  27.4 us
    ppermute x4, waiting for transfers between devices, swap(): return lax.ppermute(block, axis, [(i, i ^ bit) for i in range(size)])  11.3 us
    all_to_all x1, blocking collectives, gather_rows(): gathered = lax.all_to_all(copies, 'ctx', split_axis=0, concat_axis=0)  11.1 us
    all_to_all x2, starting transfers between devices, gather_rows(): gathered = lax.all_to_all(copies, 'ctx', split_axis=0, concat_axis=0)  10.8 us
  transfers between devices with their start and end apart: 6, of which 5 were waited for; matrix products, arithmetic and copies ran while one was open for 1% of the time, Pallas kernels for 0%

profile of v1, /device:TPU:0, one launch (start us, length us, event | category | flops | bytes accessed | tf_op | source)
XLA Modules:
  0.0 317.5 jit_solution(7897817653808717563)
XLA Ops:
  0.6 1.6 broadcast_in_dim.8
  2.3 7.3 %all-to-all-start = ((bf16[8,8,2048]{2,1,0:T(8,128)(2,1)}), bf16[8,8,2048]{2,1,0:T(8,128)(2,1)S(1)}, u32[]{:S(2)}, u32[]{:S(2)}) async-start(bf16[8,8,2048]{2,1,0:T(8,128)(2,1)} %broadcast_in_dim.8), calls=%async_computation | async-start | bytes 524288 | tf_op jit(solution)/shard_map/all_to_all | solution.py:262
  10.2 0.7 broadcast_subtract_fusion
  10.8 0.1 scatter.9.limit_ref
  10.9 7.5 %all-to-all-done = bf16[8,8,2048]{2,1,0:T(8,128)(2,1)S(1)} async-done(((bf16[8,8,2048]{2,1,0:T(8,128)(2,1)}), bf16[8,8,2048]{2,1,0:T(8,128)(2,1)S(1)}, u32[]{:S(2)}, u32[]{:S(2)}) %all-to-all-start) | async-done | bytes 262176 | tf_op jit(solution)/shard_map/all_to_all | solution.py:262
  18.4 45.6 %shard_map.130 = bf16[8,3,64,128]{3,2,1,0:T(8,128)(2,1)S(1)} custom-call(bf16[64,2048]{1,0:T(8,128)(2,1)S(1)} %bitcast.42, s32[1,128]{1,0:T(1,128)S(1)} %scatter.9.limit_ref, bf16[32768,2,128]{2,1,0:T(2,128)(2,1)} %all_keys.1, bf16[32768,2,128]{2,1,0:T(2,128)(2,1)} %all_values.1, bf16[32768,2,128]{2,1,0:T(2,128)(2,1)} %all_keys.1, ...), custom_call_target="tpu_custom_call" | custom-call | flops 17179869184 | bytes 33554432 | tf_op jit(solution)/shard_map/pallas_call | solution.py:187
  64.0 141.8 %all_to_all.25.part_ref = bf16[8,3,64,128]{3,2,1,0:T(8,128)(2,1)} all-to-all(bf16[8,3,64,128]{3,2,1,0:T(8,128)(2,1)S(1)} %shard_map.130), channel_id=1, replica_groups=mesh['ctx'=8,'head'=4] {'ctx'}, dimensions={0} | all-to-all | bytes 786432 | tf_op jit(solution)/shard_map/all_to_all | solution.py:315
  205.9 2.2 shard_map.131
  208.0 0.8 broadcast_in_dim.10
  208.8 11.1 %all_to_all.26 = bf16[8,8,2048]{2,1,0:T(8,128)(2,1)S(1)} all-to-all(bf16[8,8,2048]{2,1,0:T(8,128)(2,1)S(1)} %broadcast_in_dim.10), channel_id=1, replica_groups=mesh['ctx'=8,'head'=4] {'ctx'}, dimensions={0} | all-to-all | bytes 524288 | tf_op jit(solution)/shard_map/all_to_all | solution.py:262
  219.9 0.5 fusion.5
  220.5 1.4 collective-permute-done
  222.0 6.2 %collective-permute-done.1 = f32[64,640]{1,0:T(8,128)S(1)} collective-permute-done((f32[64,640]{1,0:T(8,128)S(1)}, f32[64,640]{1,0:T(8,128)S(1)}, u32[]{:S(2)}, u32[]{:S(2)}) %collective-permute-start.1) | collective-permute-done | bytes 163872 | tf_op jit(solution)/shard_map/ppermute | solution.py:267
  228.2 0.1 multiply_reduce_fusion
  228.4 0.1 copy.16
  228.5 4.6 %convolution_convert_fusion = bf16[64,6400]{1,0:T(8,128)(2,1)S(1)} fusion(bf16[640,6400]{1,0:T(8,128)(2,1)} %param.24, f32[64,640]{1,0:T(8,128)S(1)} %get-tuple-element.28, f32[640]{0:T(1024)S(1)} %copy-done.4), kind=kOutput, calls=%fused_computation.2 | convolution fusion | flops 524779520 | bytes 9177600 | tf_op jit(solution)/shard_map/dot_general | solution.py:325
  233.1 4.6 %convolution_convert_fusion.1 = bf16[64,6400]{1,0:T(8,128)(2,1)S(1)} fusion(bf16[640,6400]{1,0:T(8,128)(2,1)} %param.23, f32[64,640]{1,0:T(8,128)S(1)} %get-tuple-element.28, f32[640]{0:T(1024)S(1)} %copy-done.4), kind=kOutput, calls=%fused_computation.3 | convolution fusion | flops 524779520 | bytes 9177600 | tf_op jit(solution)/shard_map/dot_general | solution.py:324
  237.6 0.1 fusion.4
  237.8 41.5 %all_to_all.27 = bf16[8,8,12928]{2,1,0:T(8,128)(2,1)S(1)} all-to-all(bf16[8,8,12928]{2,1,0:T(8,128)(2,1)S(1)} %fusion.4), channel_id=1, replica_groups=mesh['ctx'=8,'head'=4] {'ctx'}, dimensions={0} | all-to-all | bytes 3309568 | tf_op jit(solution)/shard_map/all_to_all | solution.py:335
  279.3 0.2 convert_reduce_fusion
  279.5 0.1 slice_reduce_fusion
  279.7 0.1 fusion.8
  279.8 0.9 broadcast_in_dim.11
  280.8 3.5 %all-to-all-start.4 = ((bf16[8,8,6400]{2,1,0:T(8,128)(2,1)}), bf16[8,8,6400]{2,1,0:T(8,128)(2,1)S(1)}, u32[]{:S(2)}, u32[]{:S(2)}) async-start(bf16[8,8,6400]{2,1,0:T(8,128)(2,1)} %broadcast_in_dim.11), calls=%async_computation.4 | async-start | bytes 1638400 | tf_op jit(solution)/shard_map/all_to_all | solution.py:262
  284.3 19.9 %all-to-all-done.4 = bf16[8,8,6400]{2,1,0:T(8,128)(2,1)S(1)} async-done(((bf16[8,8,6400]{2,1,0:T(8,128)(2,1)}), bf16[8,8,6400]{2,1,0:T(8,128)(2,1)S(1)}, u32[]{:S(2)}, u32[]{:S(2)}) %all-to-all-start.4) | async-done | bytes 819232 | tf_op jit(solution)/shard_map/all_to_all | solution.py:262
  304.2 5.0 %fusion = f32[2,32,640]{2,1,0:T(8,128)S(1)} fusion(bf16[2,32,6400]{2,1,0:T(8,128)(2,1)S(1)} %bitcast.43, bf16[6400,640]{1,0:T(8,128)(2,1)} %param.25), kind=kOutput, calls=%fused_computation | convolution fusion | flops 524288000 | bytes 9175040 | tf_op jit(solution)/shard_map/dot_general | solution.py:344
  309.2 0.6 copy-done.3
  309.9 0.7 collective-permute-start.2
  310.6 3.7 %collective-permute-done.2 = f32[32,640]{1,0:T(8,128)S(1)} collective-permute-done((f32[32,640]{1,0:T(8,128)S(1)}, f32[32,640]{1,0:T(8,128)S(1)}, u32[]{:S(2)}, u32[]{:S(2)}) %collective-permute-start.2) | collective-permute-done | bytes 81952 | tf_op jit(solution)/shard_map/ppermute | solution.py:267
  314.3 0.9 bitcast_add_fusion
  315.3 1.6 convert_element_type.93
  316.9 0.6 fusion.9
  (23 shorter events, 0.3 us)
Async XLA Ops:
  0.6 219.2 %copy-start = (bf16[2048,640]{1,0:T(8,128)(2,1)S(1)}, bf16[2048,640]{1,0:T(8,128)(2,1)}, u32[]{:S(2)}) copy-start(bf16[2048,640]{1,0:T(8,128)(2,1)} %param.21) | copy-start | bytes 7864324
  2.3 16.2 %all-to-all-start = ((bf16[8,8,2048]{2,1,0:T(8,128)(2,1)}), bf16[8,8,2048]{2,1,0:T(8,128)(2,1)S(1)}, u32[]{:S(2)}, u32[]{:S(2)}) async-start(bf16[8,8,2048]{2,1,0:T(8,128)(2,1)} %broadcast_in_dim.8), calls=%async_computation | async-start | bytes 524288 | tf_op jit(solution)/shard_map/all_to_all | solution.py:262
  64.0 164.2 %copy-start.5 = (bf16[64,640]{1,0:T(8,128)(2,1)S(1)}, bf16[64,640]{1,0:T(8,128)(2,1)}, u32[]{:S(2)}) copy-start(bf16[64,640]{1,0:T(8,128)(2,1)} %param.20) | copy-start | bytes 245764
  64.0 164.5 %copy-start.4 = (f32[640]{0:T(1024)S(1)}, f32[640]{0:T(1024)}, u32[]{:S(2)}) copy-start(f32[640]{0:T(1024)} %param.22) | copy-start | bytes 7684
  220.4 1.5 collective-permute-start
  221.9 6.3 %collective-permute-start.1 = (f32[64,640]{1,0:T(8,128)S(1)}, f32[64,640]{1,0:T(8,128)S(1)}, u32[]{:S(2)}, u32[]{:S(2)}) collective-permute-start(f32[64,640]{1,0:T(8,128)S(1)} %add.52), channel_id=1, source_target_pairs={{0,2},{1,3},{2,0},{3,1},{4,6},{5,7},{6,4},{7,5},{8,10},{9,11},{10,... | collective-permute-start | bytes 491528 | tf_op jit(solution)/shard_map/ppermute | solution.py:267
  228.3 4.7 %copy-start.2 = (f32[64,640]{1,0:T(8,128)}, f32[64,640]{1,0:T(8,128)S(1)}, u32[]{:S(2)}) copy-start(f32[64,640]{1,0:T(8,128)S(1)} %get-tuple-element.28) | copy-start | bytes 491524
  280.8 23.5 %all-to-all-start.4 = ((bf16[8,8,6400]{2,1,0:T(8,128)(2,1)}), bf16[8,8,6400]{2,1,0:T(8,128)(2,1)S(1)}, u32[]{:S(2)}, u32[]{:S(2)}) async-start(bf16[8,8,6400]{2,1,0:T(8,128)(2,1)} %broadcast_in_dim.11), calls=%async_computation.4 | async-start | bytes 1638400 | tf_op jit(solution)/shard_map/all_to_all | solution.py:262
  304.2 13.3 %copy-start.1 = (bf16[2048,640]{1,0:T(8,128)(2,1)S(1)}, bf16[2048,640]{1,0:T(8,128)(2,1)}, u32[]{:S(2)}) copy-start(bf16[2048,640]{1,0:T(8,128)(2,1)} %param.21) | copy-start | bytes 7864324
  309.2 0.7 copy-start.3
  309.9 4.4 %collective-permute-start.2 = (f32[32,640]{1,0:T(8,128)S(1)}, f32[32,640]{1,0:T(8,128)S(1)}, u32[]{:S(2)}, u32[]{:S(2)}) collective-permute-start(f32[32,640]{1,0:T(8,128)S(1)} %dynamic-slice_bitcast_fusion), channel_id=1, source_target_pairs={{0,2},{1,3},{2,0},{3,1},{4,6},{5,7},{6,4},{7,5},{8,10},{9,11},{10,... | collective-permute-start | bytes 245768 | tf_op jit(solution)/shard_map/ppermute | solution.py:267
  315.2 1.7 collective-permute-start.3

commit v2 on v1

v2 whole, which is shorter than its diff:
```python
import functools
import math

import jax
import jax.numpy as jnp
from jax import lax
from jax.experimental import pallas as pl
from jax.experimental.pallas import tpu as pltpu
from jax.sharding import PartitionSpec as P

hidden_score = -1e30
lowest_base = -65536.0
largest_sum = 2.0**115
epsilon = 1e-06
lane = 128
stat_rows = 16
attention_vmem = 32 * 2**20
most_vmem = 56 * 2**20
small_vmem = 8 * 2**20


def split_heads(block, kv_local, head_size):
    flat = block.reshape(block.shape[0], kv_local * head_size)
    return [flat[:, h * head_size : (h + 1) * head_size] for h in range(kv_local)]


def hidden_slots(first_slot, count, limits):
    slot = lax.broadcasted_iota(jnp.int32, (count, limits.shape[1]), 0) + first_slot
    return jnp.where(slot < limits, 0.0, 1.0).astype(jnp.bfloat16)


def scores_of(key_block, hidden, query_cols):
    return jnp.dot(
        jnp.concatenate([key_block, hidden], axis=1), query_cols, preferred_element_type=jnp.float32
    )


def weighted_values(value_block, weights):
    return lax.dot_general(
        value_block,
        weights.astype(jnp.bfloat16),
        (((0,), (0,)), ((), ())),
        preferred_element_type=jnp.float32,
    )


def sublane_sums(weights):
    return jnp.sum(weights.reshape(weights.shape[0] // 8, 8, weights.shape[1]), axis=0)


def query_kernel(query_ref, limit_ref, key_ref, cols_ref, base_ref, *, kv_local, groups):
    batch = query_ref.shape[0]
    head_size = key_ref.shape[2]
    columns = batch * groups
    extra = limit_ref.shape[1]
    row = lax.broadcasted_iota(jnp.int32, (extra, columns), 0)
    column = lax.broadcasted_iota(jnp.int32, (extra, columns), 1)
    mask_rows = jnp.where(lax.rem(column, batch) == row, hidden_score, 0.0)
    hidden = hidden_slots(0, key_ref.shape[0], limit_ref[...])
    keys = split_heads(key_ref[...], kv_local, head_size)
    for h in range(kv_local):
        rows = [
            query_ref[:, (h * groups + g) * head_size : (h * groups + g + 1) * head_size]
            for g in range(groups)
        ]
        turned = jnp.concatenate(rows, axis=0).astype(jnp.float32).T
        cols_ref[h, :head_size] = turned.astype(jnp.bfloat16)
        cols_ref[h, head_size:] = mask_rows.astype(jnp.bfloat16)
        top = jnp.max(scores_of(keys[h], hidden, cols_ref[h]), axis=0, keepdims=True)
        base = jnp.maximum(top, lowest_base).astype(jnp.bfloat16).astype(jnp.float32)
        base_ref[h] = base
        cols_ref[h, head_size:] = jnp.where(row == batch, -base, mask_rows).astype(jnp.bfloat16)


def attention_kernel(
    query_cols,
    first_base,
    limit_ref,
    key_ref,
    value_ref,
    all_keys,
    all_values,
    *rest,
    kv_local,
    groups,
    sources,
    factor,
    carried,
):
    weights_in, rest = rest[:carried], rest[carried:]
    out_ref, weights_out, rest = rest[0], rest[1 : 1 + carried], rest[1 + carried :]
    (
    base_ref,
    acc_ref,
    total_ref,
    plain_cols,
    spare_keys,
    spare_values,
    copy_sems,
    weight_sems,
    ) = rest
    step = pl.program_id(0)
    head_size = key_ref.shape[2]
    block = key_ref.shape[0]
    columns = query_cols.shape[2]
    batch = columns // groups
    extra = limit_ref.shape[1]
    limits = limit_ref[...]
    steps = all_keys.shape[0] // block

    turns = [
        max(t for t in range(1, steps + 1) if weight.shape[0] % (16 * t) == 0)
        for weight in weights_in
    ]

    def weight_copies(index, turn):
        rows = weights_in[index].shape[0] // turns[index]
        here = pl.ds(pl.multiple_of(turn * rows, 16), rows)
        return pltpu.make_async_copy(
            weights_in[index].at[here], weights_out[index].at[here], weight_sems.at[index, turn]
        )

    for index in range(carried):
        pl.when(step < turns[index])(weight_copies(index, step).start)

    @pl.when(step == 0)
    def start():
        base_ref[...] = first_base[...]
        acc_ref[...] = jnp.zeros_like(acc_ref)
        total_ref[...] = jnp.zeros_like(total_ref)

    hidden = hidden_slots(step * block, block, limits)
    keys = split_heads(key_ref[...], kv_local, head_size)
    values = split_heads(value_ref[...], kv_local, head_size)
    for h in range(kv_local):
        weights = jnp.exp2(scores_of(keys[h], hidden, query_cols[h]) * factor)
        total_ref[h] += sublane_sums(weights)
        acc_ref[h] += weighted_values(values[h], weights)

    @pl.when(step == pl.num_programs(0) - 1)
    def finish():
        @pl.when(jnp.logical_not(jnp.max(total_ref[...]) <= largest_sum))
        def redo():
            piece = spare_keys.shape[0]
            row = lax.broadcasted_iota(jnp.int32, (head_size + extra, columns), 0)
            for h in range(kv_local):
                old = query_cols[h].astype(jnp.float32)
                plain_cols[h] = jnp.where(row == head_size + batch, 0.0, old).astype(jnp.bfloat16)
            base_ref[...] = jnp.full_like(base_ref, lowest_base)
            acc_ref[...] = jnp.zeros_like(acc_ref)
            total_ref[...] = jnp.zeros_like(total_ref)

            def visit(turn, carry):
                first = turn * piece
                here = pl.ds(first, piece)
                get_keys = pltpu.make_async_copy(all_keys.at[here], spare_keys, copy_sems.at[0])
                get_values = pltpu.make_async_copy(
                    all_values.at[here], spare_values, copy_sems.at[1]
                )
                get_keys.start()
                get_values.start()
                get_keys.wait()
                get_values.wait()
                hidden = hidden_slots(first, piece, limits)
                keys = split_heads(spare_keys[...], kv_local, head_size)
                values = split_heads(spare_values[...], kv_local, head_size)
                for h in range(kv_local):
                    scores = scores_of(keys[h], hidden, plain_cols[h])
                    old = base_ref[h]
                    new = jnp.maximum(old, jnp.max(scores, axis=0, keepdims=True))
                    rescale = jnp.exp2((old - new) * factor)
                    weights = jnp.exp2((scores - new) * factor)
                    base_ref[h] = new
                    total_ref[h] = total_ref[h] * rescale + sublane_sums(weights)
                    acc_ref[h] = acc_ref[h] * rescale + weighted_values(values[h], weights)
                return carry

            lax.fori_loop(0, all_keys.shape[0] // piece, visit, 0)

        for index in range(carried):
            for turn in range(turns[index]):
                weight_copies(index, turn).wait()
        rows_local = batch // sources
        rows = groups * rows_local
        stats = jnp.zeros((stat_rows, columns), jnp.float32)
        stat_row = lax.broadcasted_iota(jnp.int32, (stat_rows, columns), 0)
        for h in range(kv_local):
            total = jnp.sum(total_ref[h], axis=0, keepdims=True)
            seen = total > 0.0
            safe = jnp.where(seen, total, 1.0)
            height = jnp.where(seen, base_ref[h] * factor + jnp.log2(safe), hidden_score)
            for piece in range(3):
                part = height.astype(jnp.bfloat16).astype(jnp.float32)
                stats = jnp.where(stat_row == 3 * h + piece, part, stats)
                height = height - part
            mean = (acc_ref[h] * (1.0 / safe)).T.astype(jnp.bfloat16)
            for c in range(sources):
                for g in range(groups):
                    out_ref[c, h * rows + g * rows_local : h * rows + (g + 1) * rows_local] = mean[
                        g * batch + c * rows_local : g * batch + (c + 1) * rows_local
                    ]
        here = lax.broadcasted_iota(jnp.int32, (columns, columns), 0)
        there = lax.broadcasted_iota(jnp.int32, (columns, columns), 1)
        source, place = lax.div(there, rows), lax.rem(there, rows)
        origin = lax.div(place, rows_local) * batch + source * rows_local + lax.rem(place, rows_local)
        stats = jnp.dot(
            stats.astype(jnp.bfloat16),
            jnp.where(here == origin, 1.0, 0.0).astype(jnp.bfloat16),
            preferred_element_type=jnp.float32,
        )
        for c in range(sources):
            out_ref[c, kv_local * rows :, :rows] = stats[:, c * rows : (c + 1) * rows].astype(
                jnp.bfloat16
            )


def attention(queries, limits, keys, values, sources, groups, weights=()):
    span, kv_local, head_size = keys.shape
    batch = queries.shape[0]
    columns = batch * groups
    block = math.gcd(4096, span)
    piece = math.gcd(1024, span)
    extra = limits.shape[1]
    whole = lambda *shape: pl.BlockSpec(shape, lambda j: (0,) * len(shape))
    part = pl.BlockSpec((block, kv_local, head_size), lambda j: (j, 0, 0))
    out = (sources, kv_local * columns // sources + stat_rows, head_size)
    depth = head_size + extra
    probe = math.gcd(512, span)
    query_cols, base = pl.pallas_call(
        functools.partial(query_kernel, kv_local=kv_local, groups=groups),
        grid=(1,),
        in_specs=[
            whole(batch, queries.shape[1]),
            whole(1, extra),
            pl.BlockSpec((probe, kv_local, head_size), lambda j: (0, 0, 0)),
        ],
        out_specs=[whole(kv_local, depth, columns), whole(kv_local, 1, columns)],
        out_shape=[
            jax.ShapeDtypeStruct((kv_local, depth, columns), jnp.bfloat16),
            jax.ShapeDtypeStruct((kv_local, 1, columns), jnp.float32),
        ],
        compiler_params=pltpu.CompilerParams(vmem_limit_bytes=most_vmem),
    )(queries, limits, keys)
    return pl.pallas_call(
        functools.partial(
            attention_kernel,
            kv_local=kv_local,
            groups=groups,
            sources=sources,
            factor=math.log2(math.e) / math.sqrt(head_size),
            carried=len(weights),
        ),
        grid=(span // block,),
        in_specs=[
            whole(kv_local, depth, columns),
            whole(kv_local, 1, columns),
            whole(1, extra),
            part,
            part,
            pl.BlockSpec(memory_space=pl.ANY),
            pl.BlockSpec(memory_space=pl.ANY),
        ]
        + [pl.BlockSpec(memory_space=pl.ANY)] * len(weights),
        out_specs=[whole(*out)] + [pl.BlockSpec(memory_space=pltpu.VMEM)] * len(weights),
        out_shape=[jax.ShapeDtypeStruct(out, jnp.bfloat16)]
        + [pltpu.VMEM(weight.shape, weight.dtype) for weight in weights],
        scratch_shapes=[
            pltpu.VMEM((kv_local, 1, columns), jnp.float32),
            pltpu.VMEM((kv_local, head_size, columns), jnp.float32),
            pltpu.VMEM((kv_local, 8, columns), jnp.float32),
            pltpu.VMEM((kv_local, head_size + extra, columns), jnp.bfloat16),
            pltpu.VMEM((piece, kv_local, head_size), jnp.bfloat16),
            pltpu.VMEM((piece, kv_local, head_size), jnp.bfloat16),
            pltpu.SemaphoreType.DMA((2,)),
            pltpu.SemaphoreType.DMA((len(weights), span // block)),
        ],
        compiler_params=pltpu.CompilerParams(
            dimension_semantics=("arbitrary",), vmem_limit_bytes=attention_vmem
        ),
        cost_estimate=pl.CostEstimate(
            flops=4 * span * columns * kv_local * head_size,
            bytes_accessed=4 * span * kv_local * head_size,
            transcendentals=span * columns * kv_local,
        ),
    )(query_cols, base, limits, keys, values, keys, values, *weights)


def merge_kernel(part_ref, out_ref, copies_ref, *, kv_local, groups):
    sources, depth, head_size = part_ref.shape
    rows = (depth - stat_rows) // kv_local
    rows_local = rows // groups
    stats = part_ref[:, kv_local * rows :].astype(jnp.float32)
    stats = stats.reshape(sources * stat_rows, head_size).T
    for h in range(kv_local):
        heights = []
        for c in range(sources):
            first = c * stat_rows + 3 * h
            heights.append(
                stats[:rows, first : first + 1]
                + stats[:rows, first + 1 : first + 2]
                + stats[:rows, first + 2 : first + 3]
            )
        top = functools.reduce(jnp.maximum, heights)
        shares = [jnp.exp2(height - top) for height in heights]
        whole = sum(shares)
        mean = (
            sum(
                share * part_ref[c, h * rows : (h + 1) * rows].astype(jnp.float32)
                for c, share in enumerate(shares)
            )
            / whole
        )
        for g in range(groups):
            out_ref[:, (h * groups + g) * head_size : (h * groups + g + 1) * head_size] = mean[
                g * rows_local : (g + 1) * rows_local
            ].astype(jnp.bfloat16)
    copies_ref[...] = jnp.broadcast_to(out_ref[...][None], copies_ref.shape)


def merge(parts, kv_local, groups):
    sources, depth, head_size = parts.shape
    rows_local = (depth - stat_rows) // kv_local // groups
    width = kv_local * groups * head_size
    return pl.pallas_call(
        functools.partial(merge_kernel, kv_local=kv_local, groups=groups),
        out_shape=[
            jax.ShapeDtypeStruct((rows_local, width), jnp.bfloat16),
            jax.ShapeDtypeStruct((sources, rows_local, width), jnp.bfloat16),
        ],
        compiler_params=pltpu.CompilerParams(vmem_limit_bytes=small_vmem),
    )(parts)


def terms_kernel(
    mixed_ref, residual_ref, gain_ref, gate_ref, up_ref, *rest, first, block, offset, sources
):
    if first:
        stream_ref, rest = rest[0], rest[1:]
    keep_ref, give_ref, normed = rest
    step = pl.program_id(0)
    upper = lax.rem(lax.axis_index("ctx"), 2) == 1
    rows_local = keep_ref.shape[1]

    def put(place, terms):
        for pair in range(sources // 2):
            begin = 2 * pair * rows_local
            low = terms[begin : begin + rows_local]
            high = terms[begin + rows_local : begin + 2 * rows_local]
            keep_ref[pair, :, place] = jnp.where(upper, high, low).astype(jnp.bfloat16)
            give_ref[pair, :, place] = jnp.where(upper, low, high).astype(jnp.bfloat16)

    @pl.when(step == 0)
    def start():
        combined = residual_ref[...].astype(jnp.float32) + mixed_ref[...]
        normed[...] = (combined * gain_ref[...]).astype(jnp.bfloat16)
        if first:
            stream_ref[...] = combined.astype(jnp.bfloat16)
            left = jnp.sum(combined * combined, axis=1, keepdims=True)
            spot = lax.broadcasted_iota(jnp.int32, (combined.shape[0], lane), 1)
            parts = jnp.zeros(spot.shape, jnp.float32)
            for piece in range(3):
                part = left.astype(jnp.bfloat16).astype(jnp.float32)
                parts = jnp.where(spot == piece, part, parts)
                left = left - part
            put(pl.ds(keep_ref.shape[2] - lane, lane), parts)

    begin = pl.multiple_of(step * 2 * block, lane)
    here = pl.ds(pl.multiple_of((step + offset) * block, lane), block)
    for place, weight_ref in ((begin, gate_ref), (begin + block, up_ref)):
        put(
            pl.ds(place, block),
            jnp.dot(normed[...], weight_ref[:, here], preferred_element_type=jnp.float32),
        )


def gate_and_up(mixed, residual, gain, w_gate, w_up, block, begin, end, sources):
    first = begin == 0
    rows, depth = residual.shape
    count = end - begin
    half = (sources // 2, rows // sources, 2 * block * count + (lane if first else 0))
    whole = lambda *shape: pl.BlockSpec(shape, lambda j: (0,) * len(shape))
    out_shape = [jax.ShapeDtypeStruct(half, jnp.bfloat16)] * 2
    out_specs = [whole(*half)] * 2
    if first:
        out_shape.insert(0, jax.ShapeDtypeStruct((rows, depth), jnp.bfloat16))
        out_specs.insert(0, whole(rows, depth))
    return pl.pallas_call(
        functools.partial(
            terms_kernel, first=first, block=block, offset=begin, sources=sources
        ),
        grid=(count,),
        in_specs=[
            whole(rows, depth),
            whole(rows, depth),
            whole(1, depth),
            pl.BlockSpec(memory_space=pltpu.VMEM),
            pl.BlockSpec(memory_space=pltpu.VMEM),
        ],
        out_specs=out_specs,
        out_shape=out_shape,
        scratch_shapes=[pltpu.VMEM((rows, depth), jnp.bfloat16)],
        compiler_params=pltpu.CompilerParams(
            dimension_semantics=("arbitrary",), vmem_limit_bytes=small_vmem
        ),
        cost_estimate=pl.CostEstimate(
            flops=4 * rows * depth * block * count,
            bytes_accessed=4 * depth * block * count,
            transcendentals=0,
        ),
    )(mixed, residual, gain[None], w_gate, w_up)


def hidden_kernel(terms_ref, copies_ref, *, block, counts, width):
    terms = [terms_ref[c].astype(jnp.float32) for c in range(terms_ref.shape[0])]
    terms = sum(terms)
    last = 2 * block * counts[0]
    square_total = terms[:, last : last + 1] + terms[:, last + 1 : last + 2]
    square_total = square_total + terms[:, last + 2 : last + 3]
    scale = lax.rsqrt(square_total / width + epsilon)
    place = 0
    begin = 0
    for index, count in enumerate(counts):
        for _ in range(count):
            gate = scale * terms[:, begin : begin + block]
            upward = scale * terms[:, begin + block : begin + 2 * block]
            hidden = (gate / (1.0 + jnp.exp(-gate)) * upward).astype(jnp.bfloat16)
            for c in range(copies_ref.shape[0]):
                copies_ref[c, :, place : place + block] = hidden
            place += block
            begin += 2 * block
        if index == 0:
            begin += lane


def hidden_copies(terms, block, counts, width, sources):
    shape = (sources, terms.shape[1], block * sum(counts))
    return pl.pallas_call(
        functools.partial(hidden_kernel, block=block, counts=counts, width=width),
        out_shape=jax.ShapeDtypeStruct(shape, jnp.bfloat16),
        compiler_params=pltpu.CompilerParams(vmem_limit_bytes=small_vmem),
    )(terms)


def give_half(total, keep_ref, give_ref, bit):
    upper = lax.rem(lax.div(lax.axis_index("head"), bit), 2) == 1
    half = keep_ref.shape[0]
    low, high = total[:half], total[half:]
    keep_ref[...] = jnp.where(upper, high, low)
    give_ref[...] = jnp.where(upper, low, high).astype(give_ref.dtype)


def halves(rows, columns, bit):
    sent = jnp.bfloat16 if bit > 1 else jnp.float32
    return [
        jax.ShapeDtypeStruct((rows // 2, columns), jnp.float32),
        jax.ShapeDtypeStruct((rows // 2, columns), sent),
    ]


def down_kernel(hidden_ref, weight_ref, keep_ref, give_ref, total_ref, *, bit):
    step = pl.program_id(0)

    @pl.when(step == 0)
    def start():
        total_ref[...] = jnp.zeros_like(total_ref)

    block = hidden_ref.shape[1]
    here = pl.ds(pl.multiple_of(step * block, lane), block)
    total_ref[...] += jnp.dot(
        hidden_ref[...], weight_ref[here], preferred_element_type=jnp.float32
    )

    @pl.when(step == pl.num_programs(0) - 1)
    def finish():
        give_half(total_ref[...], keep_ref, give_ref, bit)


def down(hidden, w_down, block, bit):
    rows, depth = hidden.shape
    columns = w_down.shape[1]
    out = halves(rows, columns, bit)
    return pl.pallas_call(
        functools.partial(down_kernel, bit=bit),
        grid=(depth // block,),
        in_specs=[
            pl.BlockSpec((rows, block), lambda j: (0, j)),
            pl.BlockSpec(memory_space=pltpu.VMEM),
        ],
        out_specs=[pl.BlockSpec(part.shape, lambda j: (0, 0)) for part in out],
        out_shape=out,
        scratch_shapes=[pltpu.VMEM((rows, columns), jnp.float32)],
        compiler_params=pltpu.CompilerParams(
            dimension_semantics=("arbitrary",), vmem_limit_bytes=small_vmem
        ),
        cost_estimate=pl.CostEstimate(
            flops=2 * rows * depth * columns, bytes_accessed=2 * depth * columns, transcendentals=0
        ),
    )(hidden, w_down)


def add_kernel(mine_ref, theirs_ref, keep_ref, give_ref, *, bit):
    give_half(mine_ref[...] + theirs_ref[...].astype(jnp.float32), keep_ref, give_ref, bit)


def add_and_split(mine, theirs, bit):
    return pl.pallas_call(
        functools.partial(add_kernel, bit=bit),
        out_shape=halves(*mine.shape, bit),
        compiler_params=pltpu.CompilerParams(vmem_limit_bytes=small_vmem),
    )(mine, theirs)


def spread(copies):
    gathered = lax.all_to_all(copies, "ctx", split_axis=0, concat_axis=0)
    return gathered.reshape((-1,) + copies.shape[2:])


def swap(block, axis, size, bit):
    return lax.ppermute(block, axis, [(i, i ^ bit) for i in range(size)])


def sum_over_head(block, size):
    bit = 1
    while bit < size:
        if bit > 1:
            block = block.astype(jnp.bfloat16)
        block = block.astype(jnp.float32) + swap(block, "head", size, bit).astype(jnp.float32)
        bit *= 2
    return block


def down_and_scatter(hidden, w_down, block, size):
    bit = size // 2
    keep, give = down(hidden, w_down, block, bit)
    while bit > 1:
        theirs = swap(give, "head", size, bit)
        bit //= 2
        keep, give = add_and_split(keep, theirs, bit)
    return keep + swap(give, "head", size, bit)


def local_step(sources, heads):
    def local(
        queries, keys, values, offsets, lengths, residual, wo, norm_gain, w_gate, w_up, w_down
    ):
        head_size = keys.shape[2]
        kv_local = keys.shape[1]
        rows_local = queries.shape[0]
        groups = queries.shape[1] // (kv_local * head_size)
        batch = lengths.shape[0]
        width = residual.shape[1] * sources
        everyone = spread(jnp.broadcast_to(queries[None], (sources,) + queries.shape))
        extra = -(-(batch + 1) // lane) * lane
        column = jnp.arange(extra, dtype=jnp.int32)
        limits = jnp.where(
            column < batch,
            jnp.pad(lengths, (0, extra - batch)) - offsets[0],
            jnp.where(column == batch, -1, jnp.iinfo(jnp.int32).max),
        )
        parts, w_gate, w_up, w_down = attention(
            everyone, limits[None], keys, values, sources, groups, (w_gate, w_up, w_down)
        )
        parts = lax.all_to_all(parts, "ctx", split_axis=0, concat_axis=0)
        attended, copies = merge(parts, kv_local, groups)
        projected = jnp.dot(spread(copies), wo, preferred_element_type=jnp.float32)
        mixed = sum_over_head(projected, heads)
        units = w_gate.shape[1]
        block = math.gcd(units, 640)
        blocks = units // block
        cuts = (0, (blocks + 1) // 2, blocks)
        counts = tuple(end - begin for begin, end in zip(cuts, cuts[1:]))
        terms = []
        for begin, end in zip(cuts, cuts[1:]):
            outs = gate_and_up(
                mixed, residual, norm_gain, w_gate, w_up, block, begin, end, sources
            )
            if begin == 0:
                stream = outs[0]
            keep, give = outs[-2:]
            theirs = swap(give, "ctx", sources, 1)
            terms.append(
                (keep.astype(jnp.float32) + theirs.astype(jnp.float32)).astype(jnp.bfloat16)
            )
        terms = lax.all_to_all(
            jnp.concatenate(terms, axis=2),
            "ctx",
            split_axis=0,
            concat_axis=0,
            axis_index_groups=[[c for c in range(sources) if c % 2 == s] for s in range(2)],
        )
        hidden = spread(hidden_copies(terms, block, counts, width, sources))
        ffn_out = down_and_scatter(hidden, w_down, block, heads)
        return (attended, stream, ffn_out.astype(jnp.bfloat16))

    return local


def solution(mesh):
    return jax.shard_map(
        local_step(mesh.shape["ctx"], mesh.shape["head"]),
        mesh=mesh,
        in_specs=(
            P("ctx", "head"),
            P("ctx", "head", None),
            P("ctx", "head", None),
            P("ctx"),
            P(),
            P(None, "ctx"),
            P("head", "ctx"),
            P("ctx"),
            P("ctx", "head"),
            P("ctx", "head"),
            P("head", "ctx"),
        ),
        out_specs=(P("ctx", "head"), P(None, "ctx"), P("head", "ctx")),
        check_vma=False,
    )
```

time: 319 us -> 291 us (0.912); the launches traced: 317 us -> 293 us
  starting transfers between devices: 11.7 us -> 142 us
  blocking collectives: 194 us -> 69.8 us
  matrix products: 14.6 us -> 0.54 us
  waiting for transfers between devices: 38.7 us -> 30.5 us
  Pallas kernels: 47.7 us -> 43.7 us
    ppermute x4 -> x6, starting transfers between devices: 0.95 us -> 135 us  [swap(): return lax.ppermute(block, axis, [(i, i ^ bit) for i in range(size)])]
    all_to_all x1, blocking collectives: 142 us -> 12.4 us  [local(): parts = lax.all_to_all(parts, 'ctx', split_axis=0, concat_axis=0)]
    all_to_all x2 -> x1, waiting for transfers between devices: 27.4 us -> 7.09 us  [spread(): gathered = lax.all_to_all(copies, 'ctx', split_axis=0, concat_axis=0)]
    dot_general x4 -> x1, matrix products: 14.6 us -> 0.54 us  [local(): projected = jnp.dot(spread(copies), wo, preferred_element_type=jnp.float32)]
    pallas_call x1, Pallas kernels: 45.6 us -> 32.3 us  [attention(): pl.pallas_call(functools.partial(attention_kernel, kv_local=kv_local, gro...]
    ppermute x4 -> x6, waiting for transfers between devices: 11.3 us -> 23.4 us  [swap(): return lax.ppermute(block, axis, [(i, i ^ bit) for i in range(size)])]
    pallas_call x0 -> x6, Pallas kernels: none -> 10.1 us  [the longest x2 4.48 us: gate_and_up(): pl.pallas_call(functools.partial(terms_kernel, first=first, block=block,...]
    all_to_all x2 -> x3, blocking collectives: 52.6 us -> 57.5 us  [the longest x2 34.9 us: spread(): gathered = lax.all_to_all(copies, 'ctx', split_axis=0, concat_axis=0)]
  transfers between devices with their start and end apart: 6 -> 7, of which waited for: 5 -> 7; matrix products, arithmetic and copies ran while one was open for 1% -> 0% of each run, Pallas kernels for 0% -> 1%
where the time goes in v2:
time: 291 us; the launch traced here: 293 us
  starting transfers between devices  142 us (49%)
  blocking collectives  69.8 us (24%)
  Pallas kernels  43.7 us (15%)
  waiting for transfers between devices  30.5 us (10%)
    ppermute x6, starting transfers between devices, swap(): return lax.ppermute(block, axis, [(i, i ^ bit) for i in range(size)])  135 us
    all_to_all x2, blocking collectives, spread(): gathered = lax.all_to_all(copies, 'ctx', split_axis=0, concat_axis=0)  34.9 us
    pallas_call x1, Pallas kernels, attention(): pl.pallas_call(functools.partial(attention_kernel, kv_local=kv_local, gro...  32.3 us
    ppermute x6, waiting for transfers between devices, swap(): return lax.ppermute(block, axis, [(i, i ^ bit) for i in range(size)])  23.4 us
    all_to_all x1, blocking collectives, local(): lax.all_to_all(jnp.concatenate(terms, axis=2), 'ctx', split_axis=0, conca...  22.5 us
    all_to_all x1, blocking collectives, local(): parts = lax.all_to_all(parts, 'ctx', split_axis=0, concat_axis=0)  12.4 us
    all_to_all x1, starting transfers between devices, spread(): gathered = lax.all_to_all(copies, 'ctx', split_axis=0, concat_axis=0)  7.25 us
    all_to_all x1, waiting for transfers between devices, spread(): gathered = lax.all_to_all(copies, 'ctx', split_axis=0, concat_axis=0)  7.09 us
  transfers between devices with their start and end apart: 7, of which 7 were waited for; matrix products, arithmetic and copies ran while one was open for 0% of the time, Pallas kernels for 1%

profile of v2, /device:TPU:0, one launch (start us, length us, event | category | flops | bytes accessed | tf_op | source)
XLA Modules:
  0.0 292.8 jit_solution(17752796623247616325)
XLA Ops:
  0.6 1.6 broadcast_in_dim.21
  2.3 7.3 %all-to-all-start = ((bf16[8,8,2048]{2,1,0:T(8,128)(2,1)}), bf16[8,8,2048]{2,1,0:T(8,128)(2,1)S(1)}, u32[]{:S(2)}, u32[]{:S(2)}) async-start(bf16[8,8,2048]{2,1,0:T(8,128)(2,1)} %broadcast_in_dim.21), calls=%async_computation | async-start | bytes 524288 | tf_op jit(solution)/shard_map/all_to_all | solution.py:514
  10.2 1.2 fusion.2.limit_ref
  11.4 7.1 %all-to-all-done = bf16[8,8,2048]{2,1,0:T(8,128)(2,1)S(1)} async-done(((bf16[8,8,2048]{2,1,0:T(8,128)(2,1)}), bf16[8,8,2048]{2,1,0:T(8,128)(2,1)S(1)}, u32[]{:S(2)}, u32[]{:S(2)}) %all-to-all-start) | async-done | bytes 262176 | tf_op jit(solution)/shard_map/all_to_all | solution.py:514
  18.5 0.7 copy-done.2
  19.1 2.4 shard_map.130
  21.6 32.3 %shard_map.131 = (bf16[8,144,128]{2,1,0:T(8,128)(2,1)}, bf16[640,6400]{1,0:T(8,128)(2,1)S(1)}, bf16[640,6400]{1,0:T(8,128)(2,1)S(1)}, bf16[6400,640]{1,0:T(8,128)(2,1)S(1)}) custom-call(bf16[2,256,512]{2,1,0:T(8,128)(2,1)} %get-tuple-element.20.query_cols, f32[2,1,512]{2,1,0:T(1,128)} %get-tuple-element.21.first_base, s32[1,128]{1,0:T(1,128)} %fusion.2.limit_ref, ...), custom_call_target="tpu_custom_call" | custom-call | flops 17179869184 | bytes 33554432 | tf_op jit(solution)/shard_map/pallas_call | solution.py:244
  53.9 12.4 %all_to_all.25.part_ref = bf16[8,144,128]{2,1,0:T(8,128)(2,1)S(1)} all-to-all(bf16[8,144,128]{2,1,0:T(8,128)(2,1)} %get-tuple-element.22), channel_id=1, replica_groups=mesh['ctx'=8,'head'=4] {'ctx'}, dimensions={0} | all-to-all | bytes 589824 | tf_op jit(solution)/shard_map/all_to_all | solution.py:563
  66.3 1.3 shard_map.132
  67.5 10.7 %all_to_all.26 = bf16[8,8,2048]{2,1,0:T(8,128)(2,1)S(1)} all-to-all(bf16[8,8,2048]{2,1,0:T(8,128)(2,1)S(1)} %get-tuple-element.24), channel_id=1, replica_groups=mesh['ctx'=8,'head'=4] {'ctx'}, dimensions={0} | all-to-all | bytes 524288 | tf_op jit(solution)/shard_map/all_to_all | solution.py:514
  78.2 0.5 fusion
  78.8 125.1 %collective-permute-start = (f32[64,640]{1,0:T(8,128)S(1)}, f32[64,640]{1,0:T(8,128)S(1)}, u32[]{:S(2)}, u32[]{:S(2)}) collective-permute-start(f32[64,640]{1,0:T(8,128)S(1)} %fusion), channel_id=1, source_target_pairs={{0,1},{1,0},{2,3},{3,2},{4,5},{5,4},{6,7},{7,6},{8,9},{9,8},{10,11... | collective-permute-start | bytes 491528 | tf_op jit(solution)/shard_map/ppermute | solution.py:519
  203.8 1.0 collective-permute-done
  204.9 6.8 %collective-permute-start.1 = (bf16[64,640]{1,0:T(8,128)(2,1)S(1)}, bf16[64,640]{1,0:T(8,128)(2,1)S(1)}, u32[]{:S(2)}, u32[]{:S(2)}) collective-permute-start(bf16[64,640]{1,0:T(8,128)(2,1)S(1)} %add_convert_fusion.2), channel_id=1, source_target_pairs={{0,2},{1,3},{2,0},{3,1},{4,6},{5,7},{6,4},{7,5},{8,10},{9,11},{10,... | collective-permute-start | bytes 245768 | tf_op jit(solution)/shard_map/ppermute | solution.py:519
  211.7 2.7 collective-permute-done.1
  214.5 2.1 shard_map.134
  216.6 1.4 collective-permute-start.3
  218.0 2.4 shard_map.133
  220.4 0.7 collective-permute-start.2
  221.1 7.9 %collective-permute-done.3 = bf16[4,8,6400]{2,1,0:T(8,128)(2,1)S(1)} collective-permute-done((bf16[4,8,6400]{2,1,0:T(8,128)(2,1)S(1)}, bf16[4,8,6400]{2,1,0:T(8,128)(2,1)S(1)}, u32[]{:S(2)}, u32[]{:S(2)}) %collective-permute-start.3) | collective-permute-done | bytes 409632 | tf_op jit(solution)/shard_map/ppermute | solution.py:519
  229.0 0.1 add_convert_fusion.1
  229.1 7.5 %collective-permute-done.2 = bf16[4,8,6528]{2,1,0:T(8,128)(2,1)S(1)} collective-permute-done((bf16[4,8,6528]{2,1,0:T(8,128)(2,1)S(1)}, bf16[4,8,6528]{2,1,0:T(8,128)(2,1)S(1)}, u32[]{:S(2)}, u32[]{:S(2)}) %collective-permute-start.2) | collective-permute-done | bytes 417824 | tf_op jit(solution)/shard_map/ppermute | solution.py:519
  236.6 0.1 add_convert_fusion
  236.8 22.5 %all_to_all.27.terms_ref = bf16[4,8,12928]{2,1,0:T(8,128)(2,1)S(1)} all-to-all(bf16[4,8,12928]{2,1,0:T(8,128)(2,1)S(1)} %pad_maximum_fusion), channel_id=1, replica_groups={{0,8,16,24},{4,12,20,28},{1,9,17,25},{5,13,21,29},{2,10,18,26},{6,14,22..., dimensions={0} | all-to-all | bytes 1654784 | tf_op jit(solution)/shard_map/all_to_all | solution.py:584
  259.3 0.3 shard_map.135
  259.6 24.2 %all_to_all.28 = bf16[8,8,6400]{2,1,0:T(8,128)(2,1)S(1)} all-to-all(bf16[8,8,6400]{2,1,0:T(8,128)(2,1)S(1)} %shard_map.135), channel_id=1, replica_groups=mesh['ctx'=8,'head'=4] {'ctx'}, dimensions={0} | all-to-all | bytes 1638400 | tf_op jit(solution)/shard_map/all_to_all | solution.py:514
  283.8 3.0 %shard_map.136 = (f32[32,640]{1,0:T(8,128)S(1)}, bf16[32,640]{1,0:T(8,128)(2,1)S(1)}) custom-call(bf16[64,6400]{1,0:T(8,128)(2,1)S(1)} %bitcast.10, bf16[6400,640]{1,0:T(8,128)(2,1)S(1)} %get-tuple-element.32.weight_ref), custom_call_target="tpu_custom_call" | custom-call | flops 524288000 | bytes 8192000 | tf_op jit(solution)/shard_map/pallas_call | solution.py:482
  286.8 1.0 collective-permute-start.4
  287.8 3.0 %collective-permute-done.4.theirs_ref = bf16[32,640]{1,0:T(8,128)(2,1)S(1)} collective-permute-done((bf16[32,640]{1,0:T(8,128)(2,1)S(1)}, bf16[32,640]{1,0:T(8,128)(2,1)S(1)}, u32[]{:S(2)}, u32[]{:S(2)}) %collective-permute-start.4) | collective-permute-done | bytes 40992 | tf_op jit(solution)/shard_map/ppermute | solution.py:519
  290.9 0.1 collective-permute-start.5
  290.9 1.2 collective-permute-done.5
  292.1 0.6 add_convert_fusion.3
  (12 shorter events, 0.1 us)
Async XLA Ops:
  0.6 77.6 %copy-start = (bf16[2048,640]{1,0:T(8,128)(2,1)S(1)}, bf16[2048,640]{1,0:T(8,128)(2,1)}, u32[]{:S(2)}) copy-start(bf16[2048,640]{1,0:T(8,128)(2,1)} %param.17) | copy-start | bytes 7864324
  2.3 16.2 %all-to-all-start = ((bf16[8,8,2048]{2,1,0:T(8,128)(2,1)}), bf16[8,8,2048]{2,1,0:T(8,128)(2,1)S(1)}, u32[]{:S(2)}, u32[]{:S(2)}) async-start(bf16[8,8,2048]{2,1,0:T(8,128)(2,1)} %broadcast_in_dim.21), calls=%async_computation | async-start | bytes 524288 | tf_op jit(solution)/shard_map/all_to_all | solution.py:514
  18.4 0.7 copy-start.2
  21.5 190.2 %copy-start.3 = (f32[640]{0:T(1024)S(1)}, f32[640]{0:T(1024)}, u32[]{:S(2)}) copy-start(f32[640]{0:T(1024)} %param.18) | copy-start | bytes 7684
  21.5 192.9 %copy-start.1 = (bf16[64,640]{1,0:T(8,128)(2,1)S(1)}, bf16[64,640]{1,0:T(8,128)(2,1)}, u32[]{:S(2)}) copy-start(bf16[64,640]{1,0:T(8,128)(2,1)} %residual_ref.3) | copy-start | bytes 245764
  78.8 126.1 %collective-permute-start = (f32[64,640]{1,0:T(8,128)S(1)}, f32[64,640]{1,0:T(8,128)S(1)}, u32[]{:S(2)}, u32[]{:S(2)}) collective-permute-start(f32[64,640]{1,0:T(8,128)S(1)} %fusion), channel_id=1, source_target_pairs={{0,1},{1,0},{2,3},{3,2},{4,5},{5,4},{6,7},{7,6},{8,9},{9,8},{10,11... | collective-permute-start | bytes 491528 | tf_op jit(solution)/shard_map/ppermute | solution.py:519
  204.9 9.6 %collective-permute-start.1 = (bf16[64,640]{1,0:T(8,128)(2,1)S(1)}, bf16[64,640]{1,0:T(8,128)(2,1)S(1)}, u32[]{:S(2)}, u32[]{:S(2)}) collective-permute-start(bf16[64,640]{1,0:T(8,128)(2,1)S(1)} %add_convert_fusion.2), channel_id=1, source_target_pairs={{0,2},{1,3},{2,0},{3,1},{4,6},{5,7},{6,4},{7,5},{8,10},{9,11},{10,... | collective-permute-start | bytes 245768 | tf_op jit(solution)/shard_map/ppermute | solution.py:519
  216.6 12.4 %collective-permute-start.3 = (bf16[4,8,6400]{2,1,0:T(8,128)(2,1)S(1)}, bf16[4,8,6400]{2,1,0:T(8,128)(2,1)S(1)}, u32[]{:S(2)}, u32[]{:S(2)}) collective-permute-start(bf16[4,8,6400]{2,1,0:T(8,128)(2,1)S(1)} %get-tuple-element.31), channel_id=1, source_target_pairs={{0,4},{4,0},{8,12},{12,8},{16,20},{20,16},{24,28},{28,24},{1,5},{5... | collective-permute-start | bytes 1228808 | tf_op jit(solution)/shard_map/ppermute | solution.py:519
  220.4 16.2 %collective-permute-start.2 = (bf16[4,8,6528]{2,1,0:T(8,128)(2,1)S(1)}, bf16[4,8,6528]{2,1,0:T(8,128)(2,1)S(1)}, u32[]{:S(2)}, u32[]{:S(2)}) collective-permute-start(bf16[4,8,6528]{2,1,0:T(8,128)(2,1)S(1)} %get-tuple-element.29), channel_id=1, source_target_pairs={{0,4},{4,0},{8,12},{12,8},{16,20},{20,16},{24,28},{28,24},{1,5},{5... | collective-permute-start | bytes 1253384 | tf_op jit(solution)/shard_map/ppermute | solution.py:519
  286.8 4.1 %collective-permute-start.4 = (bf16[32,640]{1,0:T(8,128)(2,1)S(1)}, bf16[32,640]{1,0:T(8,128)(2,1)S(1)}, u32[]{:S(2)}, u32[]{:S(2)}) collective-permute-start(bf16[32,640]{1,0:T(8,128)(2,1)S(1)} %get-tuple-element.34), channel_id=1, source_target_pairs={{0,2},{1,3},{2,0},{3,1},{4,6},{5,7},{6,4},{7,5},{8,10},{9,11},{10,... | collective-permute-start | bytes 122888 | tf_op jit(solution)/shard_map/ppermute | solution.py:519
  290.9 1.3 collective-permute-start.5

commit v3 on v2

--- a/solution.py
+++ b/solution.py
@@ -48,7 +48,18 @@
     return jnp.sum(weights.reshape(weights.shape[0] // 8, 8, weights.shape[1]), axis=0)
 
 
-def query_kernel(query_ref, limit_ref, key_ref, cols_ref, base_ref, *, kv_local, groups):
+def query_kernel(*refs, kv_local, groups, pieces):
+    piece_refs, (limit_ref, key_ref, cols_ref, base_ref, query_ref) = refs[:pieces], refs[pieces:]
+    me = lax.axis_index("ctx")
+    upper = lax.rem(me, 2) == 1
+    pair_rows = piece_refs[0].shape[0]
+    half = pair_rows // 2
+    for distance, piece_ref in enumerate(piece_refs):
+        piece = piece_ref[...].astype(jnp.float32)
+        low = jnp.where(upper, piece[half:], piece[:half])
+        high = jnp.where(upper, piece[:half], piece[half:])
+        place = pl.multiple_of(lax.bitwise_xor(lax.div(me, 2), distance) * pair_rows, pair_rows)
+        query_ref[pl.ds(place, pair_rows)] = jnp.concatenate([low, high], axis=0)
     batch = query_ref.shape[0]
     head_size = key_ref.shape[2]
     columns = batch * groups
@@ -63,7 +74,7 @@
             query_ref[:, (h * groups + g) * head_size : (h * groups + g + 1) * head_size]
             for g in range(groups)
         ]
-        turned = jnp.concatenate(rows, axis=0).astype(jnp.float32).T
+        turned = jnp.concatenate(rows, axis=0).T
         cols_ref[h, :head_size] = turned.astype(jnp.bfloat16)
         cols_ref[h, head_size:] = mask_rows.astype(jnp.bfloat16)
         top = jnp.max(scores_of(keys[h], hidden, cols_ref[h]), axis=0, keepdims=True)
@@ -214,9 +225,9 @@
             )
 
 
-def attention(queries, limits, keys, values, sources, groups, weights=()):
+def attention(pieces, limits, keys, values, sources, groups, weights=()):
     span, kv_local, head_size = keys.shape
-    batch = queries.shape[0]
+    batch = len(pieces) * pieces[0].shape[0]
     columns = batch * groups
     block = math.gcd(4096, span)
     piece = math.gcd(1024, span)
@@ -227,10 +238,12 @@
     depth = head_size + extra
     probe = math.gcd(512, span)
     query_cols, base = pl.pallas_call(
-        functools.partial(query_kernel, kv_local=kv_local, groups=groups),
+        functools.partial(
+            query_kernel, kv_local=kv_local, groups=groups, pieces=len(pieces)
+        ),
         grid=(1,),
         in_specs=[
-            whole(batch, queries.shape[1]),
+            *[whole(*piece.shape) for piece in pieces],
             whole(1, extra),
             pl.BlockSpec((probe, kv_local, head_size), lambda j: (0, 0, 0)),
         ],
@@ -239,8 +252,9 @@
             jax.ShapeDtypeStruct((kv_local, depth, columns), jnp.bfloat16),
             jax.ShapeDtypeStruct((kv_local, 1, columns), jnp.float32),
         ],
+        scratch_shapes=[pltpu.VMEM((batch, pieces[0].shape[1]), jnp.float32)],
         compiler_params=pltpu.CompilerParams(vmem_limit_bytes=most_vmem),
-    )(queries, limits, keys)
+    )(*pieces, limits, keys)
     return pl.pallas_call(
         functools.partial(
             attention_kernel,
@@ -355,14 +369,14 @@
         normed[...] = (combined * gain_ref[...]).astype(jnp.bfloat16)
         if first:
             stream_ref[...] = combined.astype(jnp.bfloat16)
-            left = jnp.sum(combined * combined, axis=1, keepdims=True)
-            spot = lax.broadcasted_iota(jnp.int32, (combined.shape[0], lane), 1)
-            parts = jnp.zeros(spot.shape, jnp.float32)
-            for piece in range(3):
-                part = left.astype(jnp.bfloat16).astype(jnp.float32)
-                parts = jnp.where(spot == piece, part, parts)
-                left = left - part
-            put(pl.ds(keep_ref.shape[2] - lane, lane), parts)
+        left = jnp.sum(combined * combined, axis=1, keepdims=True)
+        spot = lax.broadcasted_iota(jnp.int32, (combined.shape[0], lane), 1)
+        parts = jnp.zeros(spot.shape, jnp.float32)
+        for piece in range(3):
+            part = left.astype(jnp.bfloat16).astype(jnp.float32)
+            parts = jnp.where(spot == piece, part, parts)
+            left = left - part
+        put(pl.ds(keep_ref.shape[2] - lane, lane), parts)
 
     begin = pl.multiple_of(step * 2 * block, lane)
     here = pl.ds(pl.multiple_of((step + offset) * block, lane), block)
@@ -377,7 +391,7 @@
     first = begin == 0
     rows, depth = residual.shape
     count = end - begin
-    half = (sources // 2, rows // sources, 2 * block * count + (lane if first else 0))
+    half = (sources // 2, rows // sources, 2 * block * count + lane)
     whole = lambda *shape: pl.BlockSpec(shape, lambda j: (0,) * len(shape))
     out_shape = [jax.ShapeDtypeStruct(half, jnp.bfloat16)] * 2
     out_specs = [whole(*half)] * 2
@@ -410,35 +424,43 @@
     )(mixed, residual, gain[None], w_gate, w_up)
 
 
-def hidden_kernel(terms_ref, copies_ref, *, block, counts, width):
-    terms = [terms_ref[c].astype(jnp.float32) for c in range(terms_ref.shape[0])]
-    terms = sum(terms)
-    last = 2 * block * counts[0]
+def pair_kernel(keep_ref, theirs_ref, *out_refs):
+    mine = lax.div(lax.axis_index("ctx"), 2)
+    for distance, out_ref in enumerate(out_refs):
+        pair = lax.bitwise_xor(mine, distance)
+        total = keep_ref[pair].astype(jnp.float32) + theirs_ref[pair].astype(jnp.float32)
+        out_ref[...] = total.astype(jnp.bfloat16)
+
+
+def pair_sums(keep, theirs):
+    return pl.pallas_call(
+        pair_kernel,
+        out_shape=[jax.ShapeDtypeStruct(keep.shape[1:], jnp.bfloat16)] * keep.shape[0],
+        compiler_params=pltpu.CompilerParams(vmem_limit_bytes=small_vmem),
+    )(keep, theirs)
+
+
+def hidden_kernel(*refs, block, width):
+    out_ref = refs[-1]
+    terms = sum(part[...].astype(jnp.float32) for part in refs[:-1])
+    last = terms.shape[1] - lane
     square_total = terms[:, last : last + 1] + terms[:, last + 1 : last + 2]
     square_total = square_total + terms[:, last + 2 : last + 3]
     scale = lax.rsqrt(square_total / width + epsilon)
-    place = 0
-    begin = 0
-    for index, count in enumerate(counts):
-        for _ in range(count):
-            gate = scale * terms[:, begin : begin + block]
-            upward = scale * terms[:, begin + block : begin + 2 * block]
-            hidden = (gate / (1.0 + jnp.exp(-gate)) * upward).astype(jnp.bfloat16)
-            for c in range(copies_ref.shape[0]):
-                copies_ref[c, :, place : place + block] = hidden
-            place += block
-            begin += 2 * block
-        if index == 0:
-            begin += lane
-
-
-def hidden_copies(terms, block, counts, width, sources):
-    shape = (sources, terms.shape[1], block * sum(counts))
+    for begin in range(0, last, 2 * block):
+        gate = scale * terms[:, begin : begin + block]
+        upward = scale * terms[:, begin + block : begin + 2 * block]
+        hidden = gate / (1.0 + jnp.exp(-gate)) * upward
+        out_ref[:, begin // 2 : begin // 2 + block] = hidden.astype(jnp.bfloat16)
+
+
+def hidden_units(parts, block, width):
+    shape = (parts[0].shape[0], (parts[0].shape[1] - lane) // 2)
     return pl.pallas_call(
-        functools.partial(hidden_kernel, block=block, counts=counts, width=width),
+        functools.partial(hidden_kernel, block=block, width=width),
         out_shape=jax.ShapeDtypeStruct(shape, jnp.bfloat16),
         compiler_params=pltpu.CompilerParams(vmem_limit_bytes=small_vmem),
-    )(terms)
+    )(*parts)
 
 
 def give_half(total, keep_ref, give_ref, bit):
@@ -457,45 +479,81 @@
     ]
 
 
-def down_kernel(hidden_ref, weight_ref, keep_ref, give_ref, total_ref, *, bit):
+def down_kernel(mine_ref, theirs_ref, weight_ref, *refs, offset, started, finished, rows_local, bit):
+    if started:
+        before_ref, refs = refs[0], refs[1:]
+    if finished:
+        keep_ref, give_ref, total_ref, ordered_ref = refs
+    else:
+        (total_ref,) = refs
     step = pl.program_id(0)
 
     @pl.when(step == 0)
     def start():
-        total_ref[...] = jnp.zeros_like(total_ref)
-
-    block = hidden_ref.shape[1]
-    here = pl.ds(pl.multiple_of(step * block, lane), block)
+        total_ref[...] = before_ref[...] if started else jnp.zeros_like(total_ref)
+
+    block = mine_ref.shape[1]
+    here = pl.ds(pl.multiple_of((step + offset) * block, lane), block)
     total_ref[...] += jnp.dot(
-        hidden_ref[...], weight_ref[here], preferred_element_type=jnp.float32
+        jnp.concatenate([mine_ref[...], theirs_ref[...]], axis=0),
+        weight_ref[here],
+        preferred_element_type=jnp.float32,
     )
 
-    @pl.when(step == pl.num_programs(0) - 1)
-    def finish():
-        give_half(total_ref[...], keep_ref, give_ref, bit)
-
-
-def down(hidden, w_down, block, bit):
-    rows, depth = hidden.shape
-    columns = w_down.shape[1]
-    out = halves(rows, columns, bit)
+    if finished:
+
+        @pl.when(step == pl.num_programs(0) - 1)
+        def finish():
+            me = lax.axis_index("ctx")
+            pairs = ordered_ref.shape[0] // 2
+            for other in range(2):
+                side = lax.bitwise_xor(lax.rem(me, 2), other)
+                for distance in range(pairs):
+                    pair = lax.bitwise_xor(lax.div(me, 2), distance)
+                    begin = (other * pairs + distance) * rows_local
+                    ordered_ref[2 * pair + side] = total_ref[begin : begin + rows_local]
+            give_half(ordered_ref[...].reshape(total_ref.shape), keep_ref, give_ref, bit)
+
+
+def down(mine, theirs, w_down, before, block, begin, finished, rows_local, bit):
+    half, depth = mine.shape
+    rows, columns = 2 * half, w_down.shape[1]
+    operands = [mine, theirs, w_down]
+    in_specs = [pl.BlockSpec((half, block), lambda j: (0, j))] * 2
+    in_specs.append(pl.BlockSpec(memory_space=pltpu.VMEM))
+    if before is not None:
+        operands.append(before)
+        in_specs.append(pl.BlockSpec((rows, columns), lambda j: (0, 0)))
+    if finished:
+        out = halves(rows, columns, bit)
+        scratch = [
+            pltpu.VMEM((rows, columns), jnp.float32),
+            pltpu.VMEM((rows // rows_local, rows_local, columns), jnp.float32),
+        ]
+    else:
+        out = [jax.ShapeDtypeStruct((rows, columns), jnp.float32)]
+        scratch = []
     return pl.pallas_call(
-        functools.partial(down_kernel, bit=bit),
+        functools.partial(
+            down_kernel,
+            offset=begin,
+            started=before is not None,
+            finished=finished,
+            rows_local=rows_local,
+            bit=bit,
+        ),
         grid=(depth // block,),
-        in_specs=[
-            pl.BlockSpec((rows, block), lambda j: (0, j)),
-            pl.BlockSpec(memory_space=pltpu.VMEM),
-        ],
+        in_specs=in_specs,
         out_specs=[pl.BlockSpec(part.shape, lambda j: (0, 0)) for part in out],
         out_shape=out,
-        scratch_shapes=[pltpu.VMEM((rows, columns), jnp.float32)],
+        scratch_shapes=scratch,
         compiler_params=pltpu.CompilerParams(
             dimension_semantics=("arbitrary",), vmem_limit_bytes=small_vmem
         ),
         cost_estimate=pl.CostEstimate(
             flops=2 * rows * depth * columns, bytes_accessed=2 * depth * columns, transcendentals=0
         ),
-    )(hidden, w_down)
+    )(*operands)
 
 
 def add_kernel(mine_ref, theirs_ref, keep_ref, give_ref, *, bit):
@@ -529,9 +587,8 @@
     return block
 
 
-def down_and_scatter(hidden, w_down, block, size):
+def scatter_over_head(keep, give, size):
     bit = size // 2
-    keep, give = down(hidden, w_down, block, bit)
     while bit > 1:
         theirs = swap(give, "head", size, bit)
         bit //= 2
@@ -549,7 +606,8 @@
         groups = queries.shape[1] // (kv_local * head_size)
         batch = lengths.shape[0]
         width = residual.shape[1] * sources
-        everyone = spread(jnp.broadcast_to(queries[None], (sources,) + queries.shape))
+        pair = jnp.concatenate([queries, swap(queries, "ctx", sources, 1)], axis=0)
+        pieces = [pair] + [swap(pair, "ctx", sources, 2 * d) for d in range(1, sources // 2)]
         extra = -(-(batch + 1) // lane) * lane
         column = jnp.arange(extra, dtype=jnp.int32)
         limits = jnp.where(
@@ -558,7 +616,7 @@
             jnp.where(column == batch, -1, jnp.iinfo(jnp.int32).max),
         )
         parts, w_gate, w_up, w_down = attention(
-            everyone, limits[None], keys, values, sources, groups, (w_gate, w_up, w_down)
+            pieces, limits[None], keys, values, sources, groups, (w_gate, w_up, w_down)
         )
         parts = lax.all_to_all(parts, "ctx", split_axis=0, concat_axis=0)
         attended, copies = merge(parts, kv_local, groups)
@@ -567,29 +625,35 @@
         units = w_gate.shape[1]
         block = math.gcd(units, 640)
         blocks = units // block
-        cuts = (0, (blocks + 1) // 2, blocks)
+        cuts = sorted({0, blocks} | {blocks * part // 100 for part in (50,)})
         counts = tuple(end - begin for begin, end in zip(cuts, cuts[1:]))
-        terms = []
+        chunks = []
         for begin, end in zip(cuts, cuts[1:]):
             outs = gate_and_up(
                 mixed, residual, norm_gain, w_gate, w_up, block, begin, end, sources
             )
             if begin == 0:
                 stream = outs[0]
-            keep, give = outs[-2:]
-            theirs = swap(give, "ctx", sources, 1)
+            chunks.append(outs[-2:])
+        terms = []
+        for keep, give in chunks:
+            sums = pair_sums(keep, swap(give, "ctx", sources, 1))
             terms.append(
-                (keep.astype(jnp.float32) + theirs.astype(jnp.float32)).astype(jnp.bfloat16)
+                [sums[0]] + [swap(sums[d], "ctx", sources, 2 * d) for d in range(1, len(sums))]
             )
-        terms = lax.all_to_all(
-            jnp.concatenate(terms, axis=2),
-            "ctx",
-            split_axis=0,
-            concat_axis=0,
-            axis_index_groups=[[c for c in range(sources) if c % 2 == s] for s in range(2)],
-        )
-        hidden = spread(hidden_copies(terms, block, counts, width, sources))
-        ffn_out = down_and_scatter(hidden, w_down, block, heads)
+        total = None
+        for parts, begin, end in zip(terms, cuts, cuts[1:]):
+            own = hidden_units(parts, block, width)
+            mine = jnp.concatenate(
+                [own] + [swap(own, "ctx", sources, 2 * d) for d in range(1, sources // 2)], axis=0
+            )
+            theirs = swap(mine, "ctx", sources, 1)
+            total = down(
+                mine, theirs, w_down, total, block, begin, end == blocks, rows_local, heads // 2
+            )
+            if end < blocks:
+                (total,) = total
+        ffn_out = scatter_over_head(*total, heads)
         return (attended, stream, ffn_out.astype(jnp.bfloat16))
 
     return local

time: 291 us -> 270 us (0.928)
  starting transfers between devices: 142 us -> 33 us
  blocking collectives: 69.8 us -> 152 us
  waiting for transfers between devices: 30.5 us -> 34.7 us
    all_to_all x1, blocking collectives: 12.4 us -> 141 us  [local(): parts = lax.all_to_all(parts, 'ctx', split_axis=0, concat_axis=0)]
    ppermute x6 -> x24, starting transfers between devices: 135 us -> 33 us  [swap(): return lax.ppermute(block, axis, [(i, i ^ bit) for i in range(size)])]
    all_to_all x2 -> x1, blocking collectives: 34.9 us -> 10.7 us  [spread(): gathered = lax.all_to_all(copies, 'ctx', split_axis=0, concat_axis=0)]
    all_to_all x1 -> x0, blocking collectives: 22.5 us -> none  [local(): lax.all_to_all(jnp.concatenate(terms, axis=2), 'ctx', split_axis=0, conca...]
    ppermute x6 -> x24, waiting for transfers between devices: 23.4 us -> 34.7 us  [swap(): return lax.ppermute(block, axis, [(i, i ^ bit) for i in range(size)])]
    all_to_all x1 -> x0, starting transfers between devices: 7.25 us -> none  [spread(): gathered = lax.all_to_all(copies, 'ctx', split_axis=0, concat_axis=0)]
    all_to_all x1 -> x0, waiting for transfers between devices: 7.09 us -> none  [spread(): gathered = lax.all_to_all(copies, 'ctx', split_axis=0, concat_axis=0)]
  transfers between devices with their start and end apart: 7 -> 24, of which waited for: 7 -> 14; matrix products, arithmetic and copies ran while one was open for 0% -> 1% of each run, Pallas kernels for 1% -> 2%
where the time goes in v3:
time: 270 us; the launch traced here: 269 us
  blocking collectives  152 us (56%)
  Pallas kernels  44.3 us (16%)
  waiting for transfers between devices  34.7 us (13%)
  starting transfers between devices  33 us (12%)
    all_to_all x1, blocking collectives, local(): parts = lax.all_to_all(parts, 'ctx', split_axis=0, concat_axis=0)  141 us
    ppermute x24, waiting for transfers between devices, swap(): return lax.ppermute(block, axis, [(i, i ^ bit) for i in range(size)])  34.7 us
    ppermute x24, starting transfers between devices, swap(): return lax.ppermute(block, axis, [(i, i ^ bit) for i in range(size)])  33 us
    pallas_call x1, Pallas kernels, attention(): pl.pallas_call(functools.partial(attention_kernel, kv_local=kv_local, gro...  32.4 us
    all_to_all x1, blocking collectives, spread(): gathered = lax.all_to_all(copies, 'ctx', split_axis=0, concat_axis=0)  10.7 us
  transfers between devices with their start and end apart: 24, of which 14 were waited for; matrix products, arithmetic and copies ran while one was open for 1% of the time, Pallas kernels for 2%

profile of v3, /device:TPU:0, one launch (start us, length us, event | category | flops | bytes accessed | tf_op | source)
XLA Modules:
  0.0 269.2 jit_solution(12226327522504118056)
XLA Ops:
  0.6 3.0 %collective-permute-start = (bf16[8,2048]{1,0:T(8,128)(2,1)}, bf16[8,2048]{1,0:T(8,128)(2,1)S(1)}, u32[]{:S(2)}, u32[]{:S(2)}) collective-permute-start(bf16[8,2048]{1,0:T(8,128)(2,1)} %param.11), channel_id=1, source_target_pairs={{0,4},{4,0},{8,12},{12,8},{16,20},{20,16},{24,28},{28,24},{1,5},{5... | collective-permute-start | bytes 98312 | tf_op jit(solution)/shard_map/ppermute | solution.py:577
  5.8 2.1 collective-permute-start.1
  7.9 2.6 collective-permute-start.2
  11.6 2.8 %collective-permute-done.2.refs_2_ = bf16[16,2048]{1,0:T(8,128)(2,1)S(1)} collective-permute-done((bf16[16,2048]{1,0:T(8,128)(2,1)S(1)}, bf16[16,2048]{1,0:T(8,128)(2,1)S(1)}, u32[]{:S(2)}, u32[]{:S(2)}) %collective-permute-start.2) | collective-permute-done | bytes 65568 | tf_op jit(solution)/shard_map/ppermute | solution.py:577
  14.4 2.1 collective-permute-done.3.refs_3_
  17.1 2.5 shard_map.130
  19.6 32.4 %shard_map.131 = (bf16[8,144,128]{2,1,0:T(8,128)(2,1)}, bf16[640,6400]{1,0:T(8,128)(2,1)S(1)}, bf16[640,6400]{1,0:T(8,128)(2,1)S(1)}, bf16[6400,640]{1,0:T(8,128)(2,1)S(1)}) custom-call(bf16[2,256,512]{2,1,0:T(8,128)(2,1)} %get-tuple-element.28.query_cols, f32[2,1,512]{2,1,0:T(1,128)} %get-tuple-element.29.first_base, s32[1,128]{1,0:T(1,128)} %fusion.2.refs_4_.limit_ref, ...), custom_call_target="tpu_custom_call" | custom-call | flops 17179869184 | bytes 33554432 | tf_op jit(solution)/shard_map/pallas_call | solution.py:258
  52.0 141.2 %all_to_all.10.part_ref = bf16[8,144,128]{2,1,0:T(8,128)(2,1)S(1)} all-to-all(bf16[8,144,128]{2,1,0:T(8,128)(2,1)} %get-tuple-element.30), channel_id=1, replica_groups=mesh['ctx'=8,'head'=4] {'ctx'}, dimensions={0} | all-to-all | bytes 589824 | tf_op jit(solution)/shard_map/all_to_all | solution.py:621
  193.3 1.3 shard_map.132
  194.5 10.7 %all_to_all.11 = bf16[8,8,2048]{2,1,0:T(8,128)(2,1)S(1)} all-to-all(bf16[8,8,2048]{2,1,0:T(8,128)(2,1)S(1)} %get-tuple-element.32), channel_id=1, replica_groups=mesh['ctx'=8,'head'=4] {'ctx'}, dimensions={0} | all-to-all | bytes 524288 | tf_op jit(solution)/shard_map/all_to_all | solution.py:572
  205.8 1.4 collective-permute-done.4
  207.2 1.6 collective-permute-start.5
  208.8 3.0 %collective-permute-done.5 = bf16[64,640]{1,0:T(8,128)(2,1)S(1)} collective-permute-done((bf16[64,640]{1,0:T(8,128)(2,1)S(1)}, bf16[64,640]{1,0:T(8,128)(2,1)S(1)}, u32[]{:S(2)}, u32[]{:S(2)}) %collective-permute-start.5) | collective-permute-done | bytes 81952 | tf_op jit(solution)/shard_map/ppermute | solution.py:577
  211.8 2.4 shard_map.133
  214.3 2.1 shard_map.134
  216.4 2.1 collective-permute-start.6
  218.5 8.3 %collective-permute-done.14.theirs_ref = bf16[4,8,6528]{2,1,0:T(8,128)(2,1)S(1)} collective-permute-done((bf16[4,8,6528]{2,1,0:T(8,128)(2,1)S(1)}, bf16[4,8,6528]{2,1,0:T(8,128)(2,1)S(1)}, u32[]{:S(2)}, u32[]{:S(2)}) %collective-permute-start.14) | collective-permute-done | bytes 417824 | tf_op jit(solution)/shard_map/ppermute | solution.py:577
  228.1 3.3 %collective-permute-start.17 = (bf16[8,6528]{1,0:T(8,128)(2,1)S(1)}, bf16[8,6528]{1,0:T(8,128)(2,1)S(1)}, u32[]{:S(2)}, u32[]{:S(2)}) collective-permute-start(bf16[8,6528]{1,0:T(8,128)(2,1)S(1)} %get-tuple-element.48), channel_id=1, source_target_pairs={{0,24},{4,28},{8,16},{12,20},{16,8},{20,12},{24,0},{28,4},{1,25},{... | collective-permute-start | bytes 313352 | tf_op jit(solution)/shard_map/ppermute | solution.py:577
  231.4 2.7 collective-permute-done.6.theirs_ref
  235.4 3.3 %collective-permute-start.9 = (bf16[8,6528]{1,0:T(8,128)(2,1)S(1)}, bf16[8,6528]{1,0:T(8,128)(2,1)S(1)}, u32[]{:S(2)}, u32[]{:S(2)}) collective-permute-start(bf16[8,6528]{1,0:T(8,128)(2,1)S(1)} %get-tuple-element.41), channel_id=1, source_target_pairs={{0,24},{4,28},{8,16},{12,20},{16,8},{20,12},{24,0},{28,4},{1,25},{... | collective-permute-start | bytes 313352 | tf_op jit(solution)/shard_map/ppermute | solution.py:577
  240.0 3.3 %collective-permute-start.20 = (bf16[8,3200]{1,0:T(8,128)(2,1)S(1)}, bf16[8,3200]{1,0:T(8,128)(2,1)S(1)}, u32[]{:S(2)}, u32[]{:S(2)}) collective-permute-start(bf16[8,3200]{1,0:T(8,128)(2,1)S(1)} %shard_map.138), channel_id=1, source_target_pairs={{0,24},{4,28},{8,16},{12,20},{16,8},{20,12},{24,0},{28,4},{1,25},{... | collective-permute-start | bytes 153608 | tf_op jit(solution)/shard_map/ppermute | solution.py:577
  243.3 3.6 %collective-permute-done.8.refs_2_ = bf16[8,6528]{1,0:T(8,128)(2,1)S(1)} collective-permute-done((bf16[8,6528]{1,0:T(8,128)(2,1)S(1)}, bf16[8,6528]{1,0:T(8,128)(2,1)S(1)}, u32[]{:S(2)}, u32[]{:S(2)}) %collective-permute-start.8) | collective-permute-done | bytes 104480 | tf_op jit(solution)/shard_map/ppermute | solution.py:577
  247.1 2.3 collective-permute-start.10
  249.9 1.9 collective-permute-start.12
  253.0 1.4 collective-permute-done.11
  254.4 1.5 collective-permute-done.12
  257.8 1.5 shard_map.139.refs_0_
  259.3 2.5 collective-permute-done.13.theirs_ref
  261.7 1.5 shard_map.140
  263.3 1.6 collective-permute-start.22
  264.8 2.5 collective-permute-done.22.theirs_ref
  267.4 1.2 collective-permute-done.23
  (54 shorter events, 12.4 us)
Async XLA Ops:
  0.6 204.6 %copy-start = (bf16[2048,640]{1,0:T(8,128)(2,1)S(1)}, bf16[2048,640]{1,0:T(8,128)(2,1)}, u32[]{:S(2)}) copy-start(bf16[2048,640]{1,0:T(8,128)(2,1)} %param.17) | copy-start | bytes 7864324
  0.6 5.1 %collective-permute-start = (bf16[8,2048]{1,0:T(8,128)(2,1)}, bf16[8,2048]{1,0:T(8,128)(2,1)S(1)}, u32[]{:S(2)}, u32[]{:S(2)}) collective-permute-start(bf16[8,2048]{1,0:T(8,128)(2,1)} %param.11), channel_id=1, source_target_pairs={{0,4},{4,0},{8,12},{12,8},{16,20},{20,16},{24,28},{28,24},{1,5},{5... | collective-permute-start | bytes 98312 | tf_op jit(solution)/shard_map/ppermute | solution.py:577
  5.8 10.8 %copy-start.2 = (bf16[16,2048]{1,0:T(8,128)(2,1)}, bf16[16,2048]{1,0:T(8,128)(2,1)S(1)}, u32[]{:S(2)}) copy-start(bf16[16,2048]{1,0:T(8,128)(2,1)S(1)} %constant_dynamic-update-slice_fusion.refs_0_) | copy-start | bytes 196612
  5.8 5.9 %collective-permute-start.1 = (bf16[16,2048]{1,0:T(8,128)(2,1)S(1)}, bf16[16,2048]{1,0:T(8,128)(2,1)S(1)}, u32[]{:S(2)}, u32[]{:S(2)}) collective-permute-start(bf16[16,2048]{1,0:T(8,128)(2,1)S(1)} %constant_dynamic-update-slice_fusion.refs_0_), channel_id=1, source_target_pairs={{0,8},{4,12},{8,0},{12,4},{16,24},{20,28},{24,16},{28,20},{1,9},{5... | collective-permute-start | bytes 196616 | tf_op jit(solution)/shard_map/ppermute | solution.py:577
  7.9 6.6 %collective-permute-start.2 = (bf16[16,2048]{1,0:T(8,128)(2,1)S(1)}, bf16[16,2048]{1,0:T(8,128)(2,1)S(1)}, u32[]{:S(2)}, u32[]{:S(2)}) collective-permute-start(bf16[16,2048]{1,0:T(8,128)(2,1)S(1)} %constant_dynamic-update-slice_fusion.refs_0_), channel_id=1, source_target_pairs={{0,16},{4,20},{8,24},{12,28},{16,0},{20,4},{24,8},{28,12},{1,17},{... | collective-permute-start | bytes 196616 | tf_op jit(solution)/shard_map/ppermute | solution.py:577
  10.5 6.1 %collective-permute-start.3 = (bf16[16,2048]{1,0:T(8,128)(2,1)S(1)}, bf16[16,2048]{1,0:T(8,128)(2,1)S(1)}, u32[]{:S(2)}, u32[]{:S(2)}) collective-permute-start(bf16[16,2048]{1,0:T(8,128)(2,1)S(1)} %constant_dynamic-update-slice_fusion.refs_0_), channel_id=1, source_target_pairs={{0,24},{4,28},{8,16},{12,20},{16,8},{20,12},{24,0},{28,4},{1,25},{... | collective-permute-start | bytes 196616 | tf_op jit(solution)/shard_map/ppermute | solution.py:577
  11.6 4.9 %copy-start.3 = (bf16[16,2048]{1,0:T(8,128)(2,1)}, bf16[16,2048]{1,0:T(8,128)(2,1)S(1)}, u32[]{:S(2)}) copy-start(bf16[16,2048]{1,0:T(8,128)(2,1)S(1)} %collective-permute-done.1.refs_1_) | copy-start | bytes 196612
  14.4 2.1 copy-start.4
  16.5 0.6 copy-start.5
  19.6 189.2 %copy-start.6 = (f32[640]{0:T(1024)S(1)}, f32[640]{0:T(1024)}, u32[]{:S(2)}) copy-start(f32[640]{0:T(1024)} %param.18) | copy-start | bytes 7684
  19.6 192.2 %copy-start.1 = (bf16[64,640]{1,0:T(8,128)(2,1)S(1)}, bf16[64,640]{1,0:T(8,128)(2,1)}, u32[]{:S(2)}) copy-start(bf16[64,640]{1,0:T(8,128)(2,1)} %residual_ref.3) | copy-start | bytes 245764
  205.7 1.5 collective-permute-start.4
  207.2 4.6 %collective-permute-start.5 = (bf16[64,640]{1,0:T(8,128)(2,1)S(1)}, bf16[64,640]{1,0:T(8,128)(2,1)S(1)}, u32[]{:S(2)}, u32[]{:S(2)}) collective-permute-start(bf16[64,640]{1,0:T(8,128)(2,1)S(1)} %add_convert_fusion), channel_id=1, source_target_pairs={{0,2},{1,3},{2,0},{3,1},{4,6},{5,7},{6,4},{7,5},{8,10},{9,11},{10,... | collective-permute-start | bytes 245768 | tf_op jit(solution)/shard_map/ppermute | solution.py:577
  214.2 12.6 %collective-permute-start.14 = (bf16[4,8,6528]{2,1,0:T(8,128)(2,1)S(1)}, bf16[4,8,6528]{2,1,0:T(8,128)(2,1)S(1)}, u32[]{:S(2)}, u32[]{:S(2)}) collective-permute-start(bf16[4,8,6528]{2,1,0:T(8,128)(2,1)S(1)} %get-tuple-element.44), channel_id=1, source_target_pairs={{0,4},{4,0},{8,12},{12,8},{16,20},{20,16},{24,28},{28,24},{1,5},{5... | collective-permute-start | bytes 1253384 | tf_op jit(solution)/shard_map/ppermute | solution.py:577
  216.4 17.6 %collective-permute-start.6 = (bf16[4,8,6528]{2,1,0:T(8,128)(2,1)S(1)}, bf16[4,8,6528]{2,1,0:T(8,128)(2,1)S(1)}, u32[]{:S(2)}, u32[]{:S(2)}) collective-permute-start(bf16[4,8,6528]{2,1,0:T(8,128)(2,1)S(1)} %get-tuple-element.37), channel_id=1, source_target_pairs={{0,4},{4,0},{8,12},{12,8},{16,20},{20,16},{24,28},{28,24},{1,5},{5... | collective-permute-start | bytes 1253384 | tf_op jit(solution)/shard_map/ppermute | solution.py:577
  226.9 8.4 %collective-permute-start.15 = (bf16[8,6528]{1,0:T(8,128)(2,1)S(1)}, bf16[8,6528]{1,0:T(8,128)(2,1)S(1)}, u32[]{:S(2)}, u32[]{:S(2)}) collective-permute-start(bf16[8,6528]{1,0:T(8,128)(2,1)S(1)} %get-tuple-element.46), channel_id=1, source_target_pairs={{0,8},{4,12},{8,0},{12,4},{16,24},{20,28},{24,16},{28,20},{1,9},{5... | collective-permute-start | bytes 313352 | tf_op jit(solution)/shard_map/ppermute | solution.py:577
  227.0 11.6 %collective-permute-start.16 = (bf16[8,6528]{1,0:T(8,128)(2,1)S(1)}, bf16[8,6528]{1,0:T(8,128)(2,1)S(1)}, u32[]{:S(2)}, u32[]{:S(2)}) collective-permute-start(bf16[8,6528]{1,0:T(8,128)(2,1)S(1)} %get-tuple-element.47), channel_id=1, source_target_pairs={{0,16},{4,20},{8,24},{12,28},{16,0},{20,4},{24,8},{28,12},{1,17},{... | collective-permute-start | bytes 313352 | tf_op jit(solution)/shard_map/ppermute | solution.py:577
  228.1 10.5 %collective-permute-start.17 = (bf16[8,6528]{1,0:T(8,128)(2,1)S(1)}, bf16[8,6528]{1,0:T(8,128)(2,1)S(1)}, u32[]{:S(2)}, u32[]{:S(2)}) collective-permute-start(bf16[8,6528]{1,0:T(8,128)(2,1)S(1)} %get-tuple-element.48), channel_id=1, source_target_pairs={{0,24},{4,28},{8,16},{12,20},{16,8},{20,12},{24,0},{28,4},{1,25},{... | collective-permute-start | bytes 313352 | tf_op jit(solution)/shard_map/ppermute | solution.py:577
  234.2 5.9 %collective-permute-start.7 = (bf16[8,6528]{1,0:T(8,128)(2,1)S(1)}, bf16[8,6528]{1,0:T(8,128)(2,1)S(1)}, u32[]{:S(2)}, u32[]{:S(2)}) collective-permute-start(bf16[8,6528]{1,0:T(8,128)(2,1)S(1)} %get-tuple-element.39), channel_id=1, source_target_pairs={{0,8},{4,12},{8,0},{12,4},{16,24},{20,28},{24,16},{28,20},{1,9},{5... | collective-permute-start | bytes 313352 | tf_op jit(solution)/shard_map/ppermute | solution.py:577
  234.2 12.6 %collective-permute-start.8 = (bf16[8,6528]{1,0:T(8,128)(2,1)S(1)}, bf16[8,6528]{1,0:T(8,128)(2,1)S(1)}, u32[]{:S(2)}, u32[]{:S(2)}) collective-permute-start(bf16[8,6528]{1,0:T(8,128)(2,1)S(1)} %get-tuple-element.40), channel_id=1, source_target_pairs={{0,16},{4,20},{8,24},{12,28},{16,0},{20,4},{24,8},{28,12},{1,17},{... | collective-permute-start | bytes 313352 | tf_op jit(solution)/shard_map/ppermute | solution.py:577
  235.4 11.5 %collective-permute-start.9 = (bf16[8,6528]{1,0:T(8,128)(2,1)S(1)}, bf16[8,6528]{1,0:T(8,128)(2,1)S(1)}, u32[]{:S(2)}, u32[]{:S(2)}) collective-permute-start(bf16[8,6528]{1,0:T(8,128)(2,1)S(1)} %get-tuple-element.41), channel_id=1, source_target_pairs={{0,24},{4,28},{8,16},{12,20},{16,8},{20,12},{24,0},{28,4},{1,25},{... | collective-permute-start | bytes 313352 | tf_op jit(solution)/shard_map/ppermute | solution.py:577
  238.8 11.0 %collective-permute-start.18 = (bf16[8,3200]{1,0:T(8,128)(2,1)S(1)}, bf16[8,3200]{1,0:T(8,128)(2,1)S(1)}, u32[]{:S(2)}, u32[]{:S(2)}) collective-permute-start(bf16[8,3200]{1,0:T(8,128)(2,1)S(1)} %shard_map.138), channel_id=1, source_target_pairs={{0,8},{4,12},{8,0},{12,4},{16,24},{20,28},{24,16},{28,20},{1,9},{5... | collective-permute-start | bytes 153608 | tf_op jit(solution)/shard_map/ppermute | solution.py:577
  238.9 12.9 %collective-permute-start.19 = (bf16[8,3200]{1,0:T(8,128)(2,1)S(1)}, bf16[8,3200]{1,0:T(8,128)(2,1)S(1)}, u32[]{:S(2)}, u32[]{:S(2)}) collective-permute-start(bf16[8,3200]{1,0:T(8,128)(2,1)S(1)} %shard_map.138), channel_id=1, source_target_pairs={{0,16},{4,20},{8,24},{12,28},{16,0},{20,4},{24,8},{28,12},{1,17},{... | collective-permute-start | bytes 153608 | tf_op jit(solution)/shard_map/ppermute | solution.py:577
  240.0 11.8 %collective-permute-start.20 = (bf16[8,3200]{1,0:T(8,128)(2,1)S(1)}, bf16[8,3200]{1,0:T(8,128)(2,1)S(1)}, u32[]{:S(2)}, u32[]{:S(2)}) collective-permute-start(bf16[8,3200]{1,0:T(8,128)(2,1)S(1)} %shard_map.138), channel_id=1, source_target_pairs={{0,24},{4,28},{8,16},{12,20},{16,8},{20,12},{24,0},{28,4},{1,25},{... | collective-permute-start | bytes 153608 | tf_op jit(solution)/shard_map/ppermute | solution.py:577
  247.1 5.9 %collective-permute-start.10 = (bf16[8,3200]{1,0:T(8,128)(2,1)S(1)}, bf16[8,3200]{1,0:T(8,128)(2,1)S(1)}, u32[]{:S(2)}, u32[]{:S(2)}) collective-permute-start(bf16[8,3200]{1,0:T(8,128)(2,1)S(1)} %shard_map.136), channel_id=1, source_target_pairs={{0,8},{4,12},{8,0},{12,4},{16,24},{20,28},{24,16},{28,20},{1,9},{5... | collective-permute-start | bytes 153608 | tf_op jit(solution)/shard_map/ppermute | solution.py:577
  249.4 5.1 %collective-permute-start.11 = (bf16[8,3200]{1,0:T(8,128)(2,1)S(1)}, bf16[8,3200]{1,0:T(8,128)(2,1)S(1)}, u32[]{:S(2)}, u32[]{:S(2)}) collective-permute-start(bf16[8,3200]{1,0:T(8,128)(2,1)S(1)} %shard_map.136), channel_id=1, source_target_pairs={{0,16},{4,20},{8,24},{12,28},{16,0},{20,4},{24,8},{28,12},{1,17},{... | collective-permute-start | bytes 153608 | tf_op jit(solution)/shard_map/ppermute | solution.py:577
  249.9 6.0 %collective-permute-start.12 = (bf16[8,3200]{1,0:T(8,128)(2,1)S(1)}, bf16[8,3200]{1,0:T(8,128)(2,1)S(1)}, u32[]{:S(2)}, u32[]{:S(2)}) collective-permute-start(bf16[8,3200]{1,0:T(8,128)(2,1)S(1)} %shard_map.136), channel_id=1, source_target_pairs={{0,24},{4,28},{8,16},{12,20},{16,8},{20,12},{24,0},{28,4},{1,25},{... | collective-permute-start | bytes 153608 | tf_op jit(solution)/shard_map/ppermute | solution.py:577
  251.8 5.9 %collective-permute-start.21 = (bf16[32,3200]{1,0:T(8,128)(2,1)S(1)}, bf16[32,3200]{1,0:T(8,128)(2,1)S(1)}, u32[]{:S(2)}, u32[]{:S(2)}) collective-permute-start(bf16[32,3200]{1,0:T(8,128)(2,1)S(1)} %pad_maximum_fusion.1.mine_ref), channel_id=1, source_target_pairs={{0,4},{4,0},{8,12},{12,8},{16,20},{20,16},{24,28},{28,24},{1,5},{5... | collective-permute-start | bytes 614408 | tf_op jit(solution)/shard_map/ppermute | solution.py:577
  255.9 5.8 %collective-permute-start.13 = (bf16[32,3200]{1,0:T(8,128)(2,1)S(1)}, bf16[32,3200]{1,0:T(8,128)(2,1)S(1)}, u32[]{:S(2)}, u32[]{:S(2)}) collective-permute-start(bf16[32,3200]{1,0:T(8,128)(2,1)S(1)} %pad_maximum_fusion.mine_ref), channel_id=1, source_target_pairs={{0,4},{4,0},{8,12},{12,8},{16,20},{20,16},{24,28},{28,24},{1,5},{5... | collective-permute-start | bytes 614408 | tf_op jit(solution)/shard_map/ppermute | solution.py:577
  263.3 4.1 %collective-permute-start.22 = (bf16[32,640]{1,0:T(8,128)(2,1)S(1)}, bf16[32,640]{1,0:T(8,128)(2,1)S(1)}, u32[]{:S(2)}, u32[]{:S(2)}) collective-permute-start(bf16[32,640]{1,0:T(8,128)(2,1)S(1)} %get-tuple-element.50), channel_id=1, source_target_pairs={{0,2},{1,3},{2,0},{3,1},{4,6},{5,7},{6,4},{7,5},{8,10},{9,11},{10,... | collective-permute-start | bytes 122888 | tf_op jit(solution)/shard_map/ppermute | solution.py:577
  267.3 1.3 collective-permute-start.23

commit v4 on v3

--- a/solution.py
+++ b/solution.py
@@ -48,59 +48,22 @@
     return jnp.sum(weights.reshape(weights.shape[0] // 8, 8, weights.shape[1]), axis=0)
 
 
-def query_kernel(*refs, kv_local, groups, pieces):
-    piece_refs, (limit_ref, key_ref, cols_ref, base_ref, query_ref) = refs[:pieces], refs[pieces:]
-    me = lax.axis_index("ctx")
-    upper = lax.rem(me, 2) == 1
-    pair_rows = piece_refs[0].shape[0]
-    half = pair_rows // 2
-    for distance, piece_ref in enumerate(piece_refs):
-        piece = piece_ref[...].astype(jnp.float32)
-        low = jnp.where(upper, piece[half:], piece[:half])
-        high = jnp.where(upper, piece[:half], piece[half:])
-        place = pl.multiple_of(lax.bitwise_xor(lax.div(me, 2), distance) * pair_rows, pair_rows)
-        query_ref[pl.ds(place, pair_rows)] = jnp.concatenate([low, high], axis=0)
-    batch = query_ref.shape[0]
-    head_size = key_ref.shape[2]
-    columns = batch * groups
-    extra = limit_ref.shape[1]
-    row = lax.broadcasted_iota(jnp.int32, (extra, columns), 0)
-    column = lax.broadcasted_iota(jnp.int32, (extra, columns), 1)
-    mask_rows = jnp.where(lax.rem(column, batch) == row, hidden_score, 0.0)
-    hidden = hidden_slots(0, key_ref.shape[0], limit_ref[...])
-    keys = split_heads(key_ref[...], kv_local, head_size)
-    for h in range(kv_local):
-        rows = [
-            query_ref[:, (h * groups + g) * head_size : (h * groups + g + 1) * head_size]
-            for g in range(groups)
-        ]
-        turned = jnp.concatenate(rows, axis=0).T
-        cols_ref[h, :head_size] = turned.astype(jnp.bfloat16)
-        cols_ref[h, head_size:] = mask_rows.astype(jnp.bfloat16)
-        top = jnp.max(scores_of(keys[h], hidden, cols_ref[h]), axis=0, keepdims=True)
-        base = jnp.maximum(top, lowest_base).astype(jnp.bfloat16).astype(jnp.float32)
-        base_ref[h] = base
-        cols_ref[h, head_size:] = jnp.where(row == batch, -base, mask_rows).astype(jnp.bfloat16)
-
-
 def attention_kernel(
-    query_cols,
-    first_base,
-    limit_ref,
-    key_ref,
-    value_ref,
-    all_keys,
-    all_values,
-    *rest,
+    *refs,
+    pieces,
     kv_local,
     groups,
     sources,
     factor,
     carried,
 ):
+    piece_refs, rest = refs[:pieces], refs[pieces:]
+    probe_ref, length_ref, offset_ref, key_ref, value_ref, all_keys, all_values, *rest = rest
     weights_in, rest = rest[:carried], rest[carried:]
     out_ref, weights_out, rest = rest[0], rest[1 : 1 + carried], rest[1 + carried :]
     (
+    query_ref,
+    query_cols,
     base_ref,
     acc_ref,
     total_ref,
@@ -115,8 +78,12 @@
     block = key_ref.shape[0]
     columns = query_cols.shape[2]
     batch = columns // groups
-    extra = limit_ref.shape[1]
-    limits = limit_ref[...]
+    extra = query_cols.shape[1] - head_size
+    spot = lax.broadcasted_iota(jnp.int32, (1, extra), 1)
+    ends = jnp.concatenate(
+        [length_ref[...] - offset_ref[0], jnp.zeros((1, extra - batch), jnp.int32)], axis=1
+    )
+    limits = jnp.where(spot < batch, ends, jnp.where(spot == batch, -1, jnp.iinfo(jnp.int32).max))
     steps = all_keys.shape[0] // block
 
     turns = [
@@ -136,7 +103,33 @@
 
     @pl.when(step == 0)
     def start():
-        base_ref[...] = first_base[...]
+        me = lax.axis_index("ctx")
+        upper = lax.rem(me, 2) == 1
+        pair_rows = piece_refs[0].shape[0]
+        half = pair_rows // 2
+        for distance, piece_ref in enumerate(piece_refs):
+            piece = piece_ref[...].astype(jnp.float32)
+            low = jnp.where(upper, piece[half:], piece[:half])
+            high = jnp.where(upper, piece[:half], piece[half:])
+            place = pl.multiple_of(lax.bitwise_xor(lax.div(me, 2), distance) * pair_rows, pair_rows)
+            query_ref[pl.ds(place, pair_rows)] = jnp.concatenate([low, high], axis=0)
+        row = lax.broadcasted_iota(jnp.int32, (extra, columns), 0)
+        column = lax.broadcasted_iota(jnp.int32, (extra, columns), 1)
+        mask_rows = jnp.where(lax.rem(column, batch) == row, hidden_score, 0.0)
+        hidden = hidden_slots(0, probe_ref.shape[0], limits)
+        keys = split_heads(probe_ref[...], kv_local, head_size)
+        for h in range(kv_local):
+            rows = [
+                query_ref[:, (h * groups + g) * head_size : (h * groups + g + 1) * head_size]
+                for g in range(groups)
+            ]
+            turned = jnp.concatenate(rows, axis=0).T
+            query_cols[h, :head_size] = turned.astype(jnp.bfloat16)
+            query_cols[h, head_size:] = mask_rows.astype(jnp.bfloat16)
+            top = jnp.max(scores_of(keys[h], hidden, query_cols[h]), axis=0, keepdims=True)
+            base = jnp.maximum(top, lowest_base).astype(jnp.bfloat16).astype(jnp.float32)
+            base_ref[h] = base
+            query_cols[h, head_size:] = jnp.where(row == batch, -base, mask_rows).astype(jnp.bfloat16)
         acc_ref[...] = jnp.zeros_like(acc_ref)
         total_ref[...] = jnp.zeros_like(total_ref)
 
@@ -225,39 +218,22 @@
             )
 
 
-def attention(pieces, limits, keys, values, sources, groups, weights=()):
+def attention(pieces, lengths, offsets, keys, values, sources, groups, weights=()):
     span, kv_local, head_size = keys.shape
     batch = len(pieces) * pieces[0].shape[0]
     columns = batch * groups
     block = math.gcd(4096, span)
     piece = math.gcd(1024, span)
-    extra = limits.shape[1]
+    extra = -(-(batch + 1) // lane) * lane
     whole = lambda *shape: pl.BlockSpec(shape, lambda j: (0,) * len(shape))
     part = pl.BlockSpec((block, kv_local, head_size), lambda j: (j, 0, 0))
     out = (sources, kv_local * columns // sources + stat_rows, head_size)
     depth = head_size + extra
     probe = math.gcd(512, span)
-    query_cols, base = pl.pallas_call(
-        functools.partial(
-            query_kernel, kv_local=kv_local, groups=groups, pieces=len(pieces)
-        ),
-        grid=(1,),
-        in_specs=[
-            *[whole(*piece.shape) for piece in pieces],
-            whole(1, extra),
-            pl.BlockSpec((probe, kv_local, head_size), lambda j: (0, 0, 0)),
-        ],
-        out_specs=[whole(kv_local, depth, columns), whole(kv_local, 1, columns)],
-        out_shape=[
-            jax.ShapeDtypeStruct((kv_local, depth, columns), jnp.bfloat16),
-            jax.ShapeDtypeStruct((kv_local, 1, columns), jnp.float32),
-        ],
-        scratch_shapes=[pltpu.VMEM((batch, pieces[0].shape[1]), jnp.float32)],
-        compiler_params=pltpu.CompilerParams(vmem_limit_bytes=most_vmem),
-    )(*pieces, limits, keys)
     return pl.pallas_call(
         functools.partial(
             attention_kernel,
+            pieces=len(pieces),
             kv_local=kv_local,
             groups=groups,
             sources=sources,
@@ -266,9 +242,10 @@
         ),
         grid=(span // block,),
         in_specs=[
-            whole(kv_local, depth, columns),
-            whole(kv_local, 1, columns),
-            whole(1, extra),
+            *[whole(*piece.shape) for piece in pieces],
+            whole(probe, kv_local, head_size),
+            whole(1, batch),
+            pl.BlockSpec(memory_space=pltpu.SMEM),
             part,
             part,
             pl.BlockSpec(memory_space=pl.ANY),
@@ -279,6 +256,8 @@
         out_shape=[jax.ShapeDtypeStruct(out, jnp.bfloat16)]
         + [pltpu.VMEM(weight.shape, weight.dtype) for weight in weights],
         scratch_shapes=[
+            pltpu.VMEM((batch, pieces[0].shape[1]), jnp.float32),
+            pltpu.VMEM((kv_local, depth, columns), jnp.bfloat16),
             pltpu.VMEM((kv_local, 1, columns), jnp.float32),
             pltpu.VMEM((kv_local, head_size, columns), jnp.float32),
             pltpu.VMEM((kv_local, 8, columns), jnp.float32),
@@ -296,7 +275,7 @@
             bytes_accessed=4 * span * kv_local * head_size,
             transcendentals=span * columns * kv_local,
         ),
-    )(query_cols, base, limits, keys, values, keys, values, *weights)
+    )(*pieces, keys, lengths[None], offsets, keys, values, keys, values, *weights)
 
 
 def merge_kernel(part_ref, out_ref, copies_ref, *, kv_local, groups):
@@ -337,8 +316,9 @@
     width = kv_local * groups * head_size
     return pl.pallas_call(
         functools.partial(merge_kernel, kv_local=kv_local, groups=groups),
+        out_specs=[pl.BlockSpec(memory_space=pltpu.VMEM)] * 2,
         out_shape=[
-            jax.ShapeDtypeStruct((rows_local, width), jnp.bfloat16),
+            pltpu.VMEM((rows_local, width), jnp.bfloat16),
             jax.ShapeDtypeStruct((sources, rows_local, width), jnp.bfloat16),
         ],
         compiler_params=pltpu.CompilerParams(vmem_limit_bytes=small_vmem),
@@ -396,8 +376,8 @@
     out_shape = [jax.ShapeDtypeStruct(half, jnp.bfloat16)] * 2
     out_specs = [whole(*half)] * 2
     if first:
-        out_shape.insert(0, jax.ShapeDtypeStruct((rows, depth), jnp.bfloat16))
-        out_specs.insert(0, whole(rows, depth))
+        out_shape.insert(0, pltpu.VMEM((rows, depth), jnp.bfloat16))
+        out_specs.insert(0, pl.BlockSpec(memory_space=pltpu.VMEM))
     return pl.pallas_call(
         functools.partial(
             terms_kernel, first=first, block=block, offset=begin, sources=sources
@@ -608,15 +588,8 @@
         width = residual.shape[1] * sources
         pair = jnp.concatenate([queries, swap(queries, "ctx", sources, 1)], axis=0)
         pieces = [pair] + [swap(pair, "ctx", sources, 2 * d) for d in range(1, sources // 2)]
-        extra = -(-(batch + 1) // lane) * lane
-        column = jnp.arange(extra, dtype=jnp.int32)
-        limits = jnp.where(
-            column < batch,
-            jnp.pad(lengths, (0, extra - batch)) - offsets[0],
-            jnp.where(column == batch, -1, jnp.iinfo(jnp.int32).max),
-        )
         parts, w_gate, w_up, w_down = attention(
-            pieces, limits[None], keys, values, sources, groups, (w_gate, w_up, w_down)
+            pieces, lengths, offsets, keys, values, sources, groups, (w_gate, w_up, w_down)
         )
         parts = lax.all_to_all(parts, "ctx", split_axis=0, concat_axis=0)
         attended, copies = merge(parts, kv_local, groups)

time: 270 us -> 269 us (level)
  blocking collectives: 152 us -> 22.8 us
  starting transfers between devices: 33 us -> 162 us
    ppermute x24, starting transfers between devices: 33 us -> 162 us  [swap(): return lax.ppermute(block, axis, [(i, i ^ bit) for i in range(size)])]
    all_to_all x1, blocking collectives: 141 us -> 12.1 us  [local(): parts = lax.all_to_all(parts, 'ctx', split_axis=0, concat_axis=0)]
    pallas_call x2 -> x1, Pallas kernels: 34.9 us -> 33.9 us  [attention(): pl.pallas_call(functools.partial(attention_kernel, pieces=len(pieces), kv...]
  transfers between devices with their start and end apart: 24 -> 24, of which waited for: 14 -> 13; matrix products, arithmetic and copies ran while one was open for 1% -> 1% of each run, Pallas kernels for 2% -> 2%
where the time goes in v4:
time: 269 us; the launch traced here: 268 us
  starting transfers between devices  162 us (60%)
  Pallas kernels  42.5 us (16%)
  waiting for transfers between devices  34.6 us (13%)
  blocking collectives  22.8 us (8%)
  local copies, waits for them, and re-layouts  2.7 us (1%)
    ppermute x24, starting transfers between devices, swap(): return lax.ppermute(block, axis, [(i, i ^ bit) for i in range(size)])  162 us
    ppermute x24, waiting for transfers between devices, swap(): return lax.ppermute(block, axis, [(i, i ^ bit) for i in range(size)])  34.6 us
    pallas_call x1, Pallas kernels, attention(): pl.pallas_call(functools.partial(attention_kernel, pieces=len(pieces), kv...  33.9 us
    all_to_all x1, blocking collectives, local(): parts = lax.all_to_all(parts, 'ctx', split_axis=0, concat_axis=0)  12.1 us
    all_to_all x1, blocking collectives, spread(): gathered = lax.all_to_all(copies, 'ctx', split_axis=0, concat_axis=0)  10.7 us
  transfers between devices with their start and end apart: 24, of which 13 were waited for; matrix products, arithmetic and copies ran while one was open for 1% of the time, Pallas kernels for 2%

profile of v4, /device:TPU:0, one launch (start us, length us, event | category | flops | bytes accessed | tf_op | source)
XLA Modules:
  0.0 267.8 jit_solution(6410966879126260823)
XLA Ops:
  0.6 3.0 %collective-permute-start = (bf16[8,2048]{1,0:T(8,128)(2,1)}, bf16[8,2048]{1,0:T(8,128)(2,1)S(1)}, u32[]{:S(2)}, u32[]{:S(2)}) collective-permute-start(bf16[8,2048]{1,0:T(8,128)(2,1)} %param.11), channel_id=1, source_target_pairs={{0,4},{4,0},{8,12},{12,8},{16,20},{20,16},{24,28},{28,24},{1,5},{5... | collective-permute-start | bytes 98312 | tf_op jit(solution)/shard_map/ppermute | solution.py:557
  4.4 1.3 collective-permute-done
  5.8 2.1 collective-permute-start.1
  7.9 2.6 collective-permute-start.2
  11.1 3.3 %collective-permute-done.2.refs_2_ = bf16[16,2048]{1,0:T(8,128)(2,1)S(1)} collective-permute-done((bf16[16,2048]{1,0:T(8,128)(2,1)S(1)}, bf16[16,2048]{1,0:T(8,128)(2,1)S(1)}, u32[]{:S(2)}, u32[]{:S(2)}) %collective-permute-start.2) | collective-permute-done | bytes 65568 | tf_op jit(solution)/shard_map/ppermute | solution.py:557
  14.4 2.1 collective-permute-done.3.refs_3_
  17.2 33.9 %shard_map.130 = (bf16[8,144,128]{2,1,0:T(8,128)(2,1)}, bf16[640,6400]{1,0:T(8,128)(2,1)S(1)}, bf16[640,6400]{1,0:T(8,128)(2,1)S(1)}, bf16[6400,640]{1,0:T(8,128)(2,1)S(1)}) custom-call(bf16[16,2048]{1,0:T(8,128)(2,1)} %copy-done.2, bf16[16,2048]{1,0:T(8,128)(2,1)} %copy-done.3, bf16[16,2048]{1,0:T(8,128)(2,1)} %copy-done.4, bf16[16,2048]{1,0:T(8,128)(2,1)} %copy-done.5, ...), custom_call_target="tpu_custom_call" | custom-call | flops 17179869184 | bytes 33554432 | tf_op jit(solution)/shard_map/pallas_call | solution.py:233
  51.1 12.1 %all_to_all.10.part_ref = bf16[8,144,128]{2,1,0:T(8,128)(2,1)S(1)} all-to-all(bf16[8,144,128]{2,1,0:T(8,128)(2,1)} %get-tuple-element.26), channel_id=1, replica_groups=mesh['ctx'=8,'head'=4] {'ctx'}, dimensions={0} | all-to-all | bytes 589824 | tf_op jit(solution)/shard_map/all_to_all | solution.py:594
  63.9 10.7 %all_to_all.11 = bf16[8,8,2048]{2,1,0:T(8,128)(2,1)S(1)} all-to-all(bf16[8,8,2048]{2,1,0:T(8,128)(2,1)S(1)} %get-tuple-element.28), channel_id=1, replica_groups=mesh['ctx'=8,'head'=4] {'ctx'}, dimensions={0} | all-to-all | bytes 524288 | tf_op jit(solution)/shard_map/all_to_all | solution.py:552
  75.1 123.9 %collective-permute-start.4 = (f32[64,640]{1,0:T(8,128)S(1)}, f32[64,640]{1,0:T(8,128)S(1)}, u32[]{:S(2)}, u32[]{:S(2)}) collective-permute-start(f32[64,640]{1,0:T(8,128)S(1)} %fusion), channel_id=1, source_target_pairs={{0,1},{1,0},{2,3},{3,2},{4,5},{5,4},{6,7},{7,6},{8,9},{9,8},{10,11... | collective-permute-start | bytes 491528 | tf_op jit(solution)/shard_map/ppermute | solution.py:557
  200.0 7.3 %collective-permute-start.5 = (bf16[64,640]{1,0:T(8,128)(2,1)S(1)}, bf16[64,640]{1,0:T(8,128)(2,1)S(1)}, u32[]{:S(2)}, u32[]{:S(2)}) collective-permute-start(bf16[64,640]{1,0:T(8,128)(2,1)S(1)} %add_convert_fusion), channel_id=1, source_target_pairs={{0,2},{1,3},{2,0},{3,1},{4,6},{5,7},{6,4},{7,5},{8,10},{9,11},{10,... | collective-permute-start | bytes 245768 | tf_op jit(solution)/shard_map/ppermute | solution.py:557
  207.3 2.7 %collective-permute-done.5 = bf16[64,640]{1,0:T(8,128)(2,1)S(1)} collective-permute-done((bf16[64,640]{1,0:T(8,128)(2,1)S(1)}, bf16[64,640]{1,0:T(8,128)(2,1)S(1)}, u32[]{:S(2)}, u32[]{:S(2)}) %collective-permute-start.5) | collective-permute-done | bytes 81952 | tf_op jit(solution)/shard_map/ppermute | solution.py:557
  210.1 2.2 shard_map.132
  212.4 2.2 shard_map.133
  214.5 2.1 collective-permute-start.6
  216.6 8.3 %collective-permute-done.14.theirs_ref = bf16[4,8,6528]{2,1,0:T(8,128)(2,1)S(1)} collective-permute-done((bf16[4,8,6528]{2,1,0:T(8,128)(2,1)S(1)}, bf16[4,8,6528]{2,1,0:T(8,128)(2,1)S(1)}, u32[]{:S(2)}, u32[]{:S(2)}) %collective-permute-start.14) | collective-permute-done | bytes 417824 | tf_op jit(solution)/shard_map/ppermute | solution.py:557
  226.2 3.3 %collective-permute-start.17 = (bf16[8,6528]{1,0:T(8,128)(2,1)S(1)}, bf16[8,6528]{1,0:T(8,128)(2,1)S(1)}, u32[]{:S(2)}, u32[]{:S(2)}) collective-permute-start(bf16[8,6528]{1,0:T(8,128)(2,1)S(1)} %get-tuple-element.44), channel_id=1, source_target_pairs={{0,24},{4,28},{8,16},{12,20},{16,8},{20,12},{24,0},{28,4},{1,25},{... | collective-permute-start | bytes 313352 | tf_op jit(solution)/shard_map/ppermute | solution.py:557
  229.5 3.0 %collective-permute-done.6.theirs_ref = bf16[4,8,6528]{2,1,0:T(8,128)(2,1)S(1)} collective-permute-done((bf16[4,8,6528]{2,1,0:T(8,128)(2,1)S(1)}, bf16[4,8,6528]{2,1,0:T(8,128)(2,1)S(1)}, u32[]{:S(2)}, u32[]{:S(2)}) %collective-permute-start.6) | collective-permute-done | bytes 417824 | tf_op jit(solution)/shard_map/ppermute | solution.py:557
  233.8 3.3 %collective-permute-start.9 = (bf16[8,6528]{1,0:T(8,128)(2,1)S(1)}, bf16[8,6528]{1,0:T(8,128)(2,1)S(1)}, u32[]{:S(2)}, u32[]{:S(2)}) collective-permute-start(bf16[8,6528]{1,0:T(8,128)(2,1)S(1)} %get-tuple-element.37), channel_id=1, source_target_pairs={{0,24},{4,28},{8,16},{12,20},{16,8},{20,12},{24,0},{28,4},{1,25},{... | collective-permute-start | bytes 313352 | tf_op jit(solution)/shard_map/ppermute | solution.py:557
  237.3 1.1 collective-permute-start.19
  238.4 3.3 %collective-permute-start.20 = (bf16[8,3200]{1,0:T(8,128)(2,1)S(1)}, bf16[8,3200]{1,0:T(8,128)(2,1)S(1)}, u32[]{:S(2)}, u32[]{:S(2)}) collective-permute-start(bf16[8,3200]{1,0:T(8,128)(2,1)S(1)} %shard_map.137), channel_id=1, source_target_pairs={{0,24},{4,28},{8,16},{12,20},{16,8},{20,12},{24,0},{28,4},{1,25},{... | collective-permute-start | bytes 153608 | tf_op jit(solution)/shard_map/ppermute | solution.py:557
  241.7 3.9 %collective-permute-done.8.refs_2_ = bf16[8,6528]{1,0:T(8,128)(2,1)S(1)} collective-permute-done((bf16[8,6528]{1,0:T(8,128)(2,1)S(1)}, bf16[8,6528]{1,0:T(8,128)(2,1)S(1)}, u32[]{:S(2)}, u32[]{:S(2)}) %collective-permute-start.8) | collective-permute-done | bytes 104480 | tf_op jit(solution)/shard_map/ppermute | solution.py:557
  245.8 2.3 collective-permute-start.10
  248.4 2.2 collective-permute-start.12
  251.7 1.5 collective-permute-done.11
  253.2 1.2 collective-permute-done.12
  255.2 1.6 collective-permute-done.21.theirs_ref
  256.9 1.5 shard_map.138.refs_0_
  258.4 1.9 collective-permute-done.13.theirs_ref
  260.3 1.5 shard_map.139
  261.8 1.4 collective-permute-start.22
  263.2 2.7 %collective-permute-done.22.theirs_ref = bf16[32,640]{1,0:T(8,128)(2,1)S(1)} collective-permute-done((bf16[32,640]{1,0:T(8,128)(2,1)S(1)}, bf16[32,640]{1,0:T(8,128)(2,1)S(1)}, u32[]{:S(2)}, u32[]{:S(2)}) %collective-permute-start.22) | collective-permute-done | bytes 40992 | tf_op jit(solution)/shard_map/ppermute | solution.py:557
  (54 shorter events, 11.0 us)
Async XLA Ops:
  0.6 73.9 %copy-start = (bf16[2048,640]{1,0:T(8,128)(2,1)S(1)}, bf16[2048,640]{1,0:T(8,128)(2,1)}, u32[]{:S(2)}) copy-start(bf16[2048,640]{1,0:T(8,128)(2,1)} %param.17) | copy-start | bytes 7864324
  0.6 5.1 %collective-permute-start = (bf16[8,2048]{1,0:T(8,128)(2,1)}, bf16[8,2048]{1,0:T(8,128)(2,1)S(1)}, u32[]{:S(2)}, u32[]{:S(2)}) collective-permute-start(bf16[8,2048]{1,0:T(8,128)(2,1)} %param.11), channel_id=1, source_target_pairs={{0,4},{4,0},{8,12},{12,8},{16,20},{20,16},{24,28},{28,24},{1,5},{5... | collective-permute-start | bytes 98312 | tf_op jit(solution)/shard_map/ppermute | solution.py:557
  5.8 10.8 %copy-start.2 = (bf16[16,2048]{1,0:T(8,128)(2,1)}, bf16[16,2048]{1,0:T(8,128)(2,1)S(1)}, u32[]{:S(2)}) copy-start(bf16[16,2048]{1,0:T(8,128)(2,1)S(1)} %constant_dynamic-update-slice_fusion.refs_0_) | copy-start | bytes 196612
  5.8 5.4 %collective-permute-start.1 = (bf16[16,2048]{1,0:T(8,128)(2,1)S(1)}, bf16[16,2048]{1,0:T(8,128)(2,1)S(1)}, u32[]{:S(2)}, u32[]{:S(2)}) collective-permute-start(bf16[16,2048]{1,0:T(8,128)(2,1)S(1)} %constant_dynamic-update-slice_fusion.refs_0_), channel_id=1, source_target_pairs={{0,8},{4,12},{8,0},{12,4},{16,24},{20,28},{24,16},{28,20},{1,9},{5... | collective-permute-start | bytes 196616 | tf_op jit(solution)/shard_map/ppermute | solution.py:557
  7.9 6.6 %collective-permute-start.2 = (bf16[16,2048]{1,0:T(8,128)(2,1)S(1)}, bf16[16,2048]{1,0:T(8,128)(2,1)S(1)}, u32[]{:S(2)}, u32[]{:S(2)}) collective-permute-start(bf16[16,2048]{1,0:T(8,128)(2,1)S(1)} %constant_dynamic-update-slice_fusion.refs_0_), channel_id=1, source_target_pairs={{0,16},{4,20},{8,24},{12,28},{16,0},{20,4},{24,8},{28,12},{1,17},{... | collective-permute-start | bytes 196616 | tf_op jit(solution)/shard_map/ppermute | solution.py:557
  10.5 6.1 %collective-permute-start.3 = (bf16[16,2048]{1,0:T(8,128)(2,1)S(1)}, bf16[16,2048]{1,0:T(8,128)(2,1)S(1)}, u32[]{:S(2)}, u32[]{:S(2)}) collective-permute-start(bf16[16,2048]{1,0:T(8,128)(2,1)S(1)} %constant_dynamic-update-slice_fusion.refs_0_), channel_id=1, source_target_pairs={{0,24},{4,28},{8,16},{12,20},{16,8},{20,12},{24,0},{28,4},{1,25},{... | collective-permute-start | bytes 196616 | tf_op jit(solution)/shard_map/ppermute | solution.py:557
  11.1 5.4 %copy-start.3 = (bf16[16,2048]{1,0:T(8,128)(2,1)}, bf16[16,2048]{1,0:T(8,128)(2,1)S(1)}, u32[]{:S(2)}) copy-start(bf16[16,2048]{1,0:T(8,128)(2,1)S(1)} %collective-permute-done.1.refs_1_) | copy-start | bytes 196612
  14.4 2.1 copy-start.4
  16.5 0.6 copy-start.5
  17.2 190.2 %copy-start.6 = (f32[640]{0:T(1024)S(1)}, f32[640]{0:T(1024)}, u32[]{:S(2)}) copy-start(f32[640]{0:T(1024)} %param.18) | copy-start | bytes 7684
  17.2 192.9 %copy-start.1 = (bf16[64,640]{1,0:T(8,128)(2,1)S(1)}, bf16[64,640]{1,0:T(8,128)(2,1)}, u32[]{:S(2)}) copy-start(bf16[64,640]{1,0:T(8,128)(2,1)} %residual_ref.3) | copy-start | bytes 245764
  75.1 124.9 %collective-permute-start.4 = (f32[64,640]{1,0:T(8,128)S(1)}, f32[64,640]{1,0:T(8,128)S(1)}, u32[]{:S(2)}, u32[]{:S(2)}) collective-permute-start(f32[64,640]{1,0:T(8,128)S(1)} %fusion), channel_id=1, source_target_pairs={{0,1},{1,0},{2,3},{3,2},{4,5},{5,4},{6,7},{7,6},{8,9},{9,8},{10,11... | collective-permute-start | bytes 491528 | tf_op jit(solution)/shard_map/ppermute | solution.py:557
  200.0 10.0 %collective-permute-start.5 = (bf16[64,640]{1,0:T(8,128)(2,1)S(1)}, bf16[64,640]{1,0:T(8,128)(2,1)S(1)}, u32[]{:S(2)}, u32[]{:S(2)}) collective-permute-start(bf16[64,640]{1,0:T(8,128)(2,1)S(1)} %add_convert_fusion), channel_id=1, source_target_pairs={{0,2},{1,3},{2,0},{3,1},{4,6},{5,7},{6,4},{7,5},{8,10},{9,11},{10,... | collective-permute-start | bytes 245768 | tf_op jit(solution)/shard_map/ppermute | solution.py:557
  212.3 12.6 %collective-permute-start.14 = (bf16[4,8,6528]{2,1,0:T(8,128)(2,1)S(1)}, bf16[4,8,6528]{2,1,0:T(8,128)(2,1)S(1)}, u32[]{:S(2)}, u32[]{:S(2)}) collective-permute-start(bf16[4,8,6528]{2,1,0:T(8,128)(2,1)S(1)} %get-tuple-element.40), channel_id=1, source_target_pairs={{0,4},{4,0},{8,12},{12,8},{16,20},{20,16},{24,28},{28,24},{1,5},{5... | collective-permute-start | bytes 1253384 | tf_op jit(solution)/shard_map/ppermute | solution.py:557
  214.5 17.9 %collective-permute-start.6 = (bf16[4,8,6528]{2,1,0:T(8,128)(2,1)S(1)}, bf16[4,8,6528]{2,1,0:T(8,128)(2,1)S(1)}, u32[]{:S(2)}, u32[]{:S(2)}) collective-permute-start(bf16[4,8,6528]{2,1,0:T(8,128)(2,1)S(1)} %get-tuple-element.33), channel_id=1, source_target_pairs={{0,4},{4,0},{8,12},{12,8},{16,20},{20,16},{24,28},{28,24},{1,5},{5... | collective-permute-start | bytes 1253384 | tf_op jit(solution)/shard_map/ppermute | solution.py:557
  225.0 8.8 %collective-permute-start.15 = (bf16[8,6528]{1,0:T(8,128)(2,1)S(1)}, bf16[8,6528]{1,0:T(8,128)(2,1)S(1)}, u32[]{:S(2)}, u32[]{:S(2)}) collective-permute-start(bf16[8,6528]{1,0:T(8,128)(2,1)S(1)} %get-tuple-element.42), channel_id=1, source_target_pairs={{0,8},{4,12},{8,0},{12,4},{16,24},{20,28},{24,16},{28,20},{1,9},{5... | collective-permute-start | bytes 313352 | tf_op jit(solution)/shard_map/ppermute | solution.py:557
  225.1 12.0 %collective-permute-start.16 = (bf16[8,6528]{1,0:T(8,128)(2,1)S(1)}, bf16[8,6528]{1,0:T(8,128)(2,1)S(1)}, u32[]{:S(2)}, u32[]{:S(2)}) collective-permute-start(bf16[8,6528]{1,0:T(8,128)(2,1)S(1)} %get-tuple-element.43), channel_id=1, source_target_pairs={{0,16},{4,20},{8,24},{12,28},{16,0},{20,4},{24,8},{28,12},{1,17},{... | collective-permute-start | bytes 313352 | tf_op jit(solution)/shard_map/ppermute | solution.py:557
  226.2 10.9 %collective-permute-start.17 = (bf16[8,6528]{1,0:T(8,128)(2,1)S(1)}, bf16[8,6528]{1,0:T(8,128)(2,1)S(1)}, u32[]{:S(2)}, u32[]{:S(2)}) collective-permute-start(bf16[8,6528]{1,0:T(8,128)(2,1)S(1)} %get-tuple-element.44), channel_id=1, source_target_pairs={{0,24},{4,28},{8,16},{12,20},{16,8},{20,12},{24,0},{28,4},{1,25},{... | collective-permute-start | bytes 313352 | tf_op jit(solution)/shard_map/ppermute | solution.py:557
  232.6 5.9 %collective-permute-start.7 = (bf16[8,6528]{1,0:T(8,128)(2,1)S(1)}, bf16[8,6528]{1,0:T(8,128)(2,1)S(1)}, u32[]{:S(2)}, u32[]{:S(2)}) collective-permute-start(bf16[8,6528]{1,0:T(8,128)(2,1)S(1)} %get-tuple-element.35), channel_id=1, source_target_pairs={{0,8},{4,12},{8,0},{12,4},{16,24},{20,28},{24,16},{28,20},{1,9},{5... | collective-permute-start | bytes 313352 | tf_op jit(solution)/shard_map/ppermute | solution.py:557
  232.7 12.9 %collective-permute-start.8 = (bf16[8,6528]{1,0:T(8,128)(2,1)S(1)}, bf16[8,6528]{1,0:T(8,128)(2,1)S(1)}, u32[]{:S(2)}, u32[]{:S(2)}) collective-permute-start(bf16[8,6528]{1,0:T(8,128)(2,1)S(1)} %get-tuple-element.36), channel_id=1, source_target_pairs={{0,16},{4,20},{8,24},{12,28},{16,0},{20,4},{24,8},{28,12},{1,17},{... | collective-permute-start | bytes 313352 | tf_op jit(solution)/shard_map/ppermute | solution.py:557
  233.8 11.8 %collective-permute-start.9 = (bf16[8,6528]{1,0:T(8,128)(2,1)S(1)}, bf16[8,6528]{1,0:T(8,128)(2,1)S(1)}, u32[]{:S(2)}, u32[]{:S(2)}) collective-permute-start(bf16[8,6528]{1,0:T(8,128)(2,1)S(1)} %get-tuple-element.37), channel_id=1, source_target_pairs={{0,24},{4,28},{8,16},{12,20},{16,8},{20,12},{24,0},{28,4},{1,25},{... | collective-permute-start | bytes 313352 | tf_op jit(solution)/shard_map/ppermute | solution.py:557
  237.2 11.1 %collective-permute-start.18 = (bf16[8,3200]{1,0:T(8,128)(2,1)S(1)}, bf16[8,3200]{1,0:T(8,128)(2,1)S(1)}, u32[]{:S(2)}, u32[]{:S(2)}) collective-permute-start(bf16[8,3200]{1,0:T(8,128)(2,1)S(1)} %shard_map.137), channel_id=1, source_target_pairs={{0,8},{4,12},{8,0},{12,4},{16,24},{20,28},{24,16},{28,20},{1,9},{5... | collective-permute-start | bytes 153608 | tf_op jit(solution)/shard_map/ppermute | solution.py:557
  237.3 13.2 %collective-permute-start.19 = (bf16[8,3200]{1,0:T(8,128)(2,1)S(1)}, bf16[8,3200]{1,0:T(8,128)(2,1)S(1)}, u32[]{:S(2)}, u32[]{:S(2)}) collective-permute-start(bf16[8,3200]{1,0:T(8,128)(2,1)S(1)} %shard_map.137), channel_id=1, source_target_pairs={{0,16},{4,20},{8,24},{12,28},{16,0},{20,4},{24,8},{28,12},{1,17},{... | collective-permute-start | bytes 153608 | tf_op jit(solution)/shard_map/ppermute | solution.py:557
  238.4 12.1 %collective-permute-start.20 = (bf16[8,3200]{1,0:T(8,128)(2,1)S(1)}, bf16[8,3200]{1,0:T(8,128)(2,1)S(1)}, u32[]{:S(2)}, u32[]{:S(2)}) collective-permute-start(bf16[8,3200]{1,0:T(8,128)(2,1)S(1)} %shard_map.137), channel_id=1, source_target_pairs={{0,24},{4,28},{8,16},{12,20},{16,8},{20,12},{24,0},{28,4},{1,25},{... | collective-permute-start | bytes 153608 | tf_op jit(solution)/shard_map/ppermute | solution.py:557
  245.8 5.9 %collective-permute-start.10 = (bf16[8,3200]{1,0:T(8,128)(2,1)S(1)}, bf16[8,3200]{1,0:T(8,128)(2,1)S(1)}, u32[]{:S(2)}, u32[]{:S(2)}) collective-permute-start(bf16[8,3200]{1,0:T(8,128)(2,1)S(1)} %shard_map.135), channel_id=1, source_target_pairs={{0,8},{4,12},{8,0},{12,4},{16,24},{20,28},{24,16},{28,20},{1,9},{5... | collective-permute-start | bytes 153608 | tf_op jit(solution)/shard_map/ppermute | solution.py:557
  248.1 5.1 %collective-permute-start.11 = (bf16[8,3200]{1,0:T(8,128)(2,1)S(1)}, bf16[8,3200]{1,0:T(8,128)(2,1)S(1)}, u32[]{:S(2)}, u32[]{:S(2)}) collective-permute-start(bf16[8,3200]{1,0:T(8,128)(2,1)S(1)} %shard_map.135), channel_id=1, source_target_pairs={{0,16},{4,20},{8,24},{12,28},{16,0},{20,4},{24,8},{28,12},{1,17},{... | collective-permute-start | bytes 153608 | tf_op jit(solution)/shard_map/ppermute | solution.py:557
  248.4 6.0 %collective-permute-start.12 = (bf16[8,3200]{1,0:T(8,128)(2,1)S(1)}, bf16[8,3200]{1,0:T(8,128)(2,1)S(1)}, u32[]{:S(2)}, u32[]{:S(2)}) collective-permute-start(bf16[8,3200]{1,0:T(8,128)(2,1)S(1)} %shard_map.135), channel_id=1, source_target_pairs={{0,24},{4,28},{8,16},{12,20},{16,8},{20,12},{24,0},{28,4},{1,25},{... | collective-permute-start | bytes 153608 | tf_op jit(solution)/shard_map/ppermute | solution.py:557
  250.6 6.3 %collective-permute-start.21 = (bf16[32,3200]{1,0:T(8,128)(2,1)S(1)}, bf16[32,3200]{1,0:T(8,128)(2,1)S(1)}, u32[]{:S(2)}, u32[]{:S(2)}) collective-permute-start(bf16[32,3200]{1,0:T(8,128)(2,1)S(1)} %pad_maximum_fusion.1.mine_ref), channel_id=1, source_target_pairs={{0,4},{4,0},{8,12},{12,8},{16,20},{20,16},{24,28},{28,24},{1,5},{5... | collective-permute-start | bytes 614408 | tf_op jit(solution)/shard_map/ppermute | solution.py:557
  254.4 5.8 %collective-permute-start.13 = (bf16[32,3200]{1,0:T(8,128)(2,1)S(1)}, bf16[32,3200]{1,0:T(8,128)(2,1)S(1)}, u32[]{:S(2)}, u32[]{:S(2)}) collective-permute-start(bf16[32,3200]{1,0:T(8,128)(2,1)S(1)} %pad_maximum_fusion.mine_ref), channel_id=1, source_target_pairs={{0,4},{4,0},{8,12},{12,8},{16,20},{20,16},{24,28},{28,24},{1,5},{5... | collective-permute-start | bytes 614408 | tf_op jit(solution)/shard_map/ppermute | solution.py:557
  261.8 4.1 %collective-permute-start.22 = (bf16[32,640]{1,0:T(8,128)(2,1)S(1)}, bf16[32,640]{1,0:T(8,128)(2,1)S(1)}, u32[]{:S(2)}, u32[]{:S(2)}) collective-permute-start(bf16[32,640]{1,0:T(8,128)(2,1)S(1)} %get-tuple-element.46), channel_id=1, source_target_pairs={{0,2},{1,3},{2,0},{3,1},{4,6},{5,7},{6,4},{7,5},{8,10},{9,11},{10,... | collective-permute-start | bytes 122888 | tf_op jit(solution)/shard_map/ppermute | solution.py:557
  265.9 1.3 collective-permute-start.23

commit v5 on v4

--- a/solution.py
+++ b/solution.py
@@ -443,27 +443,25 @@
     )(*parts)
 
 
-def give_half(total, keep_ref, give_ref, bit):
-    upper = lax.rem(lax.div(lax.axis_index("head"), bit), 2) == 1
-    half = keep_ref.shape[0]
-    low, high = total[:half], total[half:]
-    keep_ref[...] = jnp.where(upper, high, low)
-    give_ref[...] = jnp.where(upper, low, high).astype(give_ref.dtype)
-
-
-def halves(rows, columns, bit):
-    sent = jnp.bfloat16 if bit > 1 else jnp.float32
+def give_parts(total, keep_ref, give_refs):
+    me = lax.axis_index("head")
+    keep_ref[...] = total[me]
+    for distance, give_ref in enumerate(give_refs, 1):
+        give_ref[...] = total[lax.bitwise_xor(me, distance)].astype(give_ref.dtype)
+
+
+def head_parts(rows, columns, size):
     return [
-        jax.ShapeDtypeStruct((rows // 2, columns), jnp.float32),
-        jax.ShapeDtypeStruct((rows // 2, columns), sent),
+        jax.ShapeDtypeStruct((rows // size, columns), jnp.float32 if d < 2 else jnp.bfloat16)
+        for d in range(size)
     ]
 
 
-def down_kernel(mine_ref, theirs_ref, weight_ref, *refs, offset, started, finished, rows_local, bit):
+def down_kernel(mine_ref, theirs_ref, weight_ref, *refs, offset, started, finished, rows_local, size):
     if started:
         before_ref, refs = refs[0], refs[1:]
     if finished:
-        keep_ref, give_ref, total_ref, ordered_ref = refs
+        keep_ref, *give_refs, total_ref, ordered_ref, split_ref = refs
     else:
         (total_ref,) = refs
     step = pl.program_id(0)
@@ -492,10 +490,11 @@
                     pair = lax.bitwise_xor(lax.div(me, 2), distance)
                     begin = (other * pairs + distance) * rows_local
                     ordered_ref[2 * pair + side] = total_ref[begin : begin + rows_local]
-            give_half(ordered_ref[...].reshape(total_ref.shape), keep_ref, give_ref, bit)
-
-
-def down(mine, theirs, w_down, before, block, begin, finished, rows_local, bit):
+            split_ref[...] = ordered_ref[...].reshape(split_ref.shape)
+            give_parts(split_ref, keep_ref, give_refs)
+
+
+def down(mine, theirs, w_down, before, block, begin, finished, rows_local, size):
     half, depth = mine.shape
     rows, columns = 2 * half, w_down.shape[1]
     operands = [mine, theirs, w_down]
@@ -505,10 +504,11 @@
         operands.append(before)
         in_specs.append(pl.BlockSpec((rows, columns), lambda j: (0, 0)))
     if finished:
-        out = halves(rows, columns, bit)
+        out = head_parts(rows, columns, size)
         scratch = [
             pltpu.VMEM((rows, columns), jnp.float32),
             pltpu.VMEM((rows // rows_local, rows_local, columns), jnp.float32),
+            pltpu.VMEM((size, rows // size, columns), jnp.float32),
         ]
     else:
         out = [jax.ShapeDtypeStruct((rows, columns), jnp.float32)]
@@ -520,7 +520,7 @@
             started=before is not None,
             finished=finished,
             rows_local=rows_local,
-            bit=bit,
+            size=size,
         ),
         grid=(depth // block,),
         in_specs=in_specs,
@@ -534,18 +534,6 @@
             flops=2 * rows * depth * columns, bytes_accessed=2 * depth * columns, transcendentals=0
         ),
     )(*operands)
-
-
-def add_kernel(mine_ref, theirs_ref, keep_ref, give_ref, *, bit):
-    give_half(mine_ref[...] + theirs_ref[...].astype(jnp.float32), keep_ref, give_ref, bit)
-
-
-def add_and_split(mine, theirs, bit):
-    return pl.pallas_call(
-        functools.partial(add_kernel, bit=bit),
-        out_shape=halves(*mine.shape, bit),
-        compiler_params=pltpu.CompilerParams(vmem_limit_bytes=small_vmem),
-    )(mine, theirs)
 
 
 def spread(copies):
@@ -567,13 +555,9 @@
     return block
 
 
-def scatter_over_head(keep, give, size):
-    bit = size // 2
-    while bit > 1:
-        theirs = swap(give, "head", size, bit)
-        bit //= 2
-        keep, give = add_and_split(keep, theirs, bit)
-    return keep + swap(give, "head", size, bit)
+def scatter_over_head(keep, *gives, size):
+    theirs = [swap(give, "head", size, d) for d, give in enumerate(gives, 1)]
+    return keep + sum(part.astype(jnp.float32) for part in theirs)
 
 
 def local_step(sources, heads):
@@ -622,11 +606,11 @@
             )
             theirs = swap(mine, "ctx", sources, 1)
             total = down(
-                mine, theirs, w_down, total, block, begin, end == blocks, rows_local, heads // 2
+                mine, theirs, w_down, total, block, begin, end == blocks, rows_local, heads
             )
             if end < blocks:
                 (total,) = total
-        ffn_out = scatter_over_head(*total, heads)
+        ffn_out = scatter_over_head(*total, size=heads)
         return (attended, stream, ffn_out.astype(jnp.bfloat16))
 
     return local

time: 269 us -> 264 us (0.981); the launches traced: 268 us -> 266 us
    ppermute x24 -> x25, waiting for transfers between devices: 34.6 us -> 33.8 us  [swap(): return lax.ppermute(block, axis, [(i, i ^ bit) for i in range(size)])]
    ppermute x24 -> x25, starting transfers between devices: 162 us -> 162 us  [swap(): return lax.ppermute(block, axis, [(i, i ^ bit) for i in range(size)])]
  transfers between devices with their start and end apart: 24 -> 25, of which waited for: 13 -> 14; matrix products, arithmetic and copies ran while one was open for 1% -> 1% of each run, Pallas kernels for 2% -> 2%
where the time goes in v5:
time: 264 us; the launch traced here: 266 us
  starting transfers between devices  162 us (61%)
  Pallas kernels  42.5 us (16%)
  waiting for transfers between devices  33.8 us (13%)
  blocking collectives  22.8 us (9%)
  local copies, waits for them, and re-layouts  2.7 us (1%)
    ppermute x25, starting transfers between devices, swap(): return lax.ppermute(block, axis, [(i, i ^ bit) for i in range(size)])  162 us
    pallas_call x1, Pallas kernels, attention(): pl.pallas_call(functools.partial(attention_kernel, pieces=len(pieces), kv...  33.9 us
    ppermute x25, waiting for transfers between devices, swap(): return lax.ppermute(block, axis, [(i, i ^ bit) for i in range(size)])  33.8 us
    all_to_all x1, blocking collectives, local(): parts = lax.all_to_all(parts, 'ctx', split_axis=0, concat_axis=0)  12.1 us
    all_to_all x1, blocking collectives, spread(): gathered = lax.all_to_all(copies, 'ctx', split_axis=0, concat_axis=0)  10.7 us
  transfers between devices with their start and end apart: 25, of which 14 were waited for; matrix products, arithmetic and copies ran while one was open for 1% of the time, Pallas kernels for 2%

profile of v5, /device:TPU:0, one launch (start us, length us, event | category | flops | bytes accessed | tf_op | source)
XLA Modules:
  0.0 266.3 jit_solution(17555853385770585376)
XLA Ops:
  0.6 3.0 %collective-permute-start = (bf16[8,2048]{1,0:T(8,128)(2,1)}, bf16[8,2048]{1,0:T(8,128)(2,1)S(1)}, u32[]{:S(2)}, u32[]{:S(2)}) collective-permute-start(bf16[8,2048]{1,0:T(8,128)(2,1)} %param.11), channel_id=1, source_target_pairs={{0,4},{4,0},{8,12},{12,8},{16,20},{20,16},{24,28},{28,24},{1,5},{5... | collective-permute-start | bytes 98312 | tf_op jit(solution)/shard_map/ppermute | solution.py:545
  4.4 1.3 collective-permute-done
  5.8 2.1 collective-permute-start.1
  7.9 2.6 collective-permute-start.2
  11.1 3.3 %collective-permute-done.2.refs_2_ = bf16[16,2048]{1,0:T(8,128)(2,1)S(1)} collective-permute-done((bf16[16,2048]{1,0:T(8,128)(2,1)S(1)}, bf16[16,2048]{1,0:T(8,128)(2,1)S(1)}, u32[]{:S(2)}, u32[]{:S(2)}) %collective-permute-start.2) | collective-permute-done | bytes 65568 | tf_op jit(solution)/shard_map/ppermute | solution.py:545
  14.4 2.1 collective-permute-done.3.refs_3_
  17.2 33.9 %shard_map.130 = (bf16[8,144,128]{2,1,0:T(8,128)(2,1)}, bf16[640,6400]{1,0:T(8,128)(2,1)S(1)}, bf16[640,6400]{1,0:T(8,128)(2,1)S(1)}, bf16[6400,640]{1,0:T(8,128)(2,1)S(1)}) custom-call(bf16[16,2048]{1,0:T(8,128)(2,1)} %copy-done.2, bf16[16,2048]{1,0:T(8,128)(2,1)} %copy-done.3, bf16[16,2048]{1,0:T(8,128)(2,1)} %copy-done.4, bf16[16,2048]{1,0:T(8,128)(2,1)} %copy-done.5, ...), custom_call_target="tpu_custom_call" | custom-call | flops 17179869184 | bytes 33554432 | tf_op jit(solution)/shard_map/pallas_call | solution.py:233
  51.1 12.1 %all_to_all.10.part_ref = bf16[8,144,128]{2,1,0:T(8,128)(2,1)S(1)} all-to-all(bf16[8,144,128]{2,1,0:T(8,128)(2,1)} %get-tuple-element.26), channel_id=1, replica_groups=mesh['ctx'=8,'head'=4] {'ctx'}, dimensions={0} | all-to-all | bytes 589824 | tf_op jit(solution)/shard_map/all_to_all | solution.py:578
  63.9 10.7 %all_to_all.11 = bf16[8,8,2048]{2,1,0:T(8,128)(2,1)S(1)} all-to-all(bf16[8,8,2048]{2,1,0:T(8,128)(2,1)S(1)} %get-tuple-element.28), channel_id=1, replica_groups=mesh['ctx'=8,'head'=4] {'ctx'}, dimensions={0} | all-to-all | bytes 524288 | tf_op jit(solution)/shard_map/all_to_all | solution.py:540
  75.2 1.4 collective-permute-done.4
  76.6 130.0 %collective-permute-start.5 = (bf16[64,640]{1,0:T(8,128)(2,1)S(1)}, bf16[64,640]{1,0:T(8,128)(2,1)S(1)}, u32[]{:S(2)}, u32[]{:S(2)}) collective-permute-start(bf16[64,640]{1,0:T(8,128)(2,1)S(1)} %add_convert_fusion), channel_id=1, source_target_pairs={{0,2},{1,3},{2,0},{3,1},{4,6},{5,7},{6,4},{7,5},{8,10},{9,11},{10,... | collective-permute-start | bytes 245768 | tf_op jit(solution)/shard_map/ppermute | solution.py:545
  206.6 2.7 %collective-permute-done.5 = bf16[64,640]{1,0:T(8,128)(2,1)S(1)} collective-permute-done((bf16[64,640]{1,0:T(8,128)(2,1)S(1)}, bf16[64,640]{1,0:T(8,128)(2,1)S(1)}, u32[]{:S(2)}, u32[]{:S(2)}) %collective-permute-start.5) | collective-permute-done | bytes 81952 | tf_op jit(solution)/shard_map/ppermute | solution.py:545
  209.3 2.2 shard_map.132
  211.6 2.2 shard_map.133
  213.8 2.1 collective-permute-start.6
  215.8 8.3 %collective-permute-done.14.theirs_ref = bf16[4,8,6528]{2,1,0:T(8,128)(2,1)S(1)} collective-permute-done((bf16[4,8,6528]{2,1,0:T(8,128)(2,1)S(1)}, bf16[4,8,6528]{2,1,0:T(8,128)(2,1)S(1)}, u32[]{:S(2)}, u32[]{:S(2)}) %collective-permute-start.14) | collective-permute-done | bytes 417824 | tf_op jit(solution)/shard_map/ppermute | solution.py:545
  225.4 3.3 %collective-permute-start.17 = (bf16[8,6528]{1,0:T(8,128)(2,1)S(1)}, bf16[8,6528]{1,0:T(8,128)(2,1)S(1)}, u32[]{:S(2)}, u32[]{:S(2)}) collective-permute-start(bf16[8,6528]{1,0:T(8,128)(2,1)S(1)} %get-tuple-element.44), channel_id=1, source_target_pairs={{0,24},{4,28},{8,16},{12,20},{16,8},{20,12},{24,0},{28,4},{1,25},{... | collective-permute-start | bytes 313352 | tf_op jit(solution)/shard_map/ppermute | solution.py:545
  228.7 3.0 %collective-permute-done.6.theirs_ref = bf16[4,8,6528]{2,1,0:T(8,128)(2,1)S(1)} collective-permute-done((bf16[4,8,6528]{2,1,0:T(8,128)(2,1)S(1)}, bf16[4,8,6528]{2,1,0:T(8,128)(2,1)S(1)}, u32[]{:S(2)}, u32[]{:S(2)}) %collective-permute-start.6) | collective-permute-done | bytes 417824 | tf_op jit(solution)/shard_map/ppermute | solution.py:545
  231.9 1.1 collective-permute-start.8
  233.0 3.3 %collective-permute-start.9 = (bf16[8,6528]{1,0:T(8,128)(2,1)S(1)}, bf16[8,6528]{1,0:T(8,128)(2,1)S(1)}, u32[]{:S(2)}, u32[]{:S(2)}) collective-permute-start(bf16[8,6528]{1,0:T(8,128)(2,1)S(1)} %get-tuple-element.37), channel_id=1, source_target_pairs={{0,24},{4,28},{8,16},{12,20},{16,8},{20,12},{24,0},{28,4},{1,25},{... | collective-permute-start | bytes 313352 | tf_op jit(solution)/shard_map/ppermute | solution.py:545
  236.6 1.1 collective-permute-start.19
  237.7 3.3 %collective-permute-start.20 = (bf16[8,3200]{1,0:T(8,128)(2,1)S(1)}, bf16[8,3200]{1,0:T(8,128)(2,1)S(1)}, u32[]{:S(2)}, u32[]{:S(2)}) collective-permute-start(bf16[8,3200]{1,0:T(8,128)(2,1)S(1)} %shard_map.137), channel_id=1, source_target_pairs={{0,24},{4,28},{8,16},{12,20},{16,8},{20,12},{24,0},{28,4},{1,25},{... | collective-permute-start | bytes 153608 | tf_op jit(solution)/shard_map/ppermute | solution.py:545
  240.9 3.9 %collective-permute-done.8.refs_2_ = bf16[8,6528]{1,0:T(8,128)(2,1)S(1)} collective-permute-done((bf16[8,6528]{1,0:T(8,128)(2,1)S(1)}, bf16[8,6528]{1,0:T(8,128)(2,1)S(1)}, u32[]{:S(2)}, u32[]{:S(2)}) %collective-permute-start.8) | collective-permute-done | bytes 104480 | tf_op jit(solution)/shard_map/ppermute | solution.py:545
  245.0 2.3 collective-permute-start.10
  247.6 2.2 collective-permute-start.12
  250.9 1.5 collective-permute-done.11
  252.4 1.2 collective-permute-done.12
  254.5 1.6 collective-permute-done.21.theirs_ref
  256.1 1.5 shard_map.138.refs_0_
  257.6 1.9 collective-permute-done.13.theirs_ref
  259.5 1.5 shard_map.139
  261.1 1.4 collective-permute-start.23
  (55 shorter events, 10.9 us)
Async XLA Ops:
  0.6 73.9 %copy-start = (bf16[2048,640]{1,0:T(8,128)(2,1)S(1)}, bf16[2048,640]{1,0:T(8,128)(2,1)}, u32[]{:S(2)}) copy-start(bf16[2048,640]{1,0:T(8,128)(2,1)} %param.17) | copy-start | bytes 7864324
  0.6 5.1 %collective-permute-start = (bf16[8,2048]{1,0:T(8,128)(2,1)}, bf16[8,2048]{1,0:T(8,128)(2,1)S(1)}, u32[]{:S(2)}, u32[]{:S(2)}) collective-permute-start(bf16[8,2048]{1,0:T(8,128)(2,1)} %param.11), channel_id=1, source_target_pairs={{0,4},{4,0},{8,12},{12,8},{16,20},{20,16},{24,28},{28,24},{1,5},{5... | collective-permute-start | bytes 98312 | tf_op jit(solution)/shard_map/ppermute | solution.py:545
  5.8 10.8 %copy-start.2 = (bf16[16,2048]{1,0:T(8,128)(2,1)}, bf16[16,2048]{1,0:T(8,128)(2,1)S(1)}, u32[]{:S(2)}) copy-start(bf16[16,2048]{1,0:T(8,128)(2,1)S(1)} %constant_dynamic-update-slice_fusion.refs_0_) | copy-start | bytes 196612
  5.8 5.4 %collective-permute-start.1 = (bf16[16,2048]{1,0:T(8,128)(2,1)S(1)}, bf16[16,2048]{1,0:T(8,128)(2,1)S(1)}, u32[]{:S(2)}, u32[]{:S(2)}) collective-permute-start(bf16[16,2048]{1,0:T(8,128)(2,1)S(1)} %constant_dynamic-update-slice_fusion.refs_0_), channel_id=1, source_target_pairs={{0,8},{4,12},{8,0},{12,4},{16,24},{20,28},{24,16},{28,20},{1,9},{5... | collective-permute-start | bytes 196616 | tf_op jit(solution)/shard_map/ppermute | solution.py:545
  7.9 6.6 %collective-permute-start.2 = (bf16[16,2048]{1,0:T(8,128)(2,1)S(1)}, bf16[16,2048]{1,0:T(8,128)(2,1)S(1)}, u32[]{:S(2)}, u32[]{:S(2)}) collective-permute-start(bf16[16,2048]{1,0:T(8,128)(2,1)S(1)} %constant_dynamic-update-slice_fusion.refs_0_), channel_id=1, source_target_pairs={{0,16},{4,20},{8,24},{12,28},{16,0},{20,4},{24,8},{28,12},{1,17},{... | collective-permute-start | bytes 196616 | tf_op jit(solution)/shard_map/ppermute | solution.py:545
  10.5 6.1 %collective-permute-start.3 = (bf16[16,2048]{1,0:T(8,128)(2,1)S(1)}, bf16[16,2048]{1,0:T(8,128)(2,1)S(1)}, u32[]{:S(2)}, u32[]{:S(2)}) collective-permute-start(bf16[16,2048]{1,0:T(8,128)(2,1)S(1)} %constant_dynamic-update-slice_fusion.refs_0_), channel_id=1, source_target_pairs={{0,24},{4,28},{8,16},{12,20},{16,8},{20,12},{24,0},{28,4},{1,25},{... | collective-permute-start | bytes 196616 | tf_op jit(solution)/shard_map/ppermute | solution.py:545
  11.1 5.4 %copy-start.3 = (bf16[16,2048]{1,0:T(8,128)(2,1)}, bf16[16,2048]{1,0:T(8,128)(2,1)S(1)}, u32[]{:S(2)}) copy-start(bf16[16,2048]{1,0:T(8,128)(2,1)S(1)} %collective-permute-done.1.refs_1_) | copy-start | bytes 196612
  14.4 2.1 copy-start.4
  16.5 0.6 copy-start.5
  17.2 189.4 %copy-start.6 = (f32[640]{0:T(1024)S(1)}, f32[640]{0:T(1024)}, u32[]{:S(2)}) copy-start(f32[640]{0:T(1024)} %param.18) | copy-start | bytes 7684
  17.2 192.2 %copy-start.1 = (bf16[64,640]{1,0:T(8,128)(2,1)S(1)}, bf16[64,640]{1,0:T(8,128)(2,1)}, u32[]{:S(2)}) copy-start(bf16[64,640]{1,0:T(8,128)(2,1)} %residual_ref.3) | copy-start | bytes 245764
  75.1 1.5 collective-permute-start.4
  76.6 132.7 %collective-permute-start.5 = (bf16[64,640]{1,0:T(8,128)(2,1)S(1)}, bf16[64,640]{1,0:T(8,128)(2,1)S(1)}, u32[]{:S(2)}, u32[]{:S(2)}) collective-permute-start(bf16[64,640]{1,0:T(8,128)(2,1)S(1)} %add_convert_fusion), channel_id=1, source_target_pairs={{0,2},{1,3},{2,0},{3,1},{4,6},{5,7},{6,4},{7,5},{8,10},{9,11},{10,... | collective-permute-start | bytes 245768 | tf_op jit(solution)/shard_map/ppermute | solution.py:545
  211.5 12.6 %collective-permute-start.14 = (bf16[4,8,6528]{2,1,0:T(8,128)(2,1)S(1)}, bf16[4,8,6528]{2,1,0:T(8,128)(2,1)S(1)}, u32[]{:S(2)}, u32[]{:S(2)}) collective-permute-start(bf16[4,8,6528]{2,1,0:T(8,128)(2,1)S(1)} %get-tuple-element.40), channel_id=1, source_target_pairs={{0,4},{4,0},{8,12},{12,8},{16,20},{20,16},{24,28},{28,24},{1,5},{5... | collective-permute-start | bytes 1253384 | tf_op jit(solution)/shard_map/ppermute | solution.py:545
  213.8 17.9 %collective-permute-start.6 = (bf16[4,8,6528]{2,1,0:T(8,128)(2,1)S(1)}, bf16[4,8,6528]{2,1,0:T(8,128)(2,1)S(1)}, u32[]{:S(2)}, u32[]{:S(2)}) collective-permute-start(bf16[4,8,6528]{2,1,0:T(8,128)(2,1)S(1)} %get-tuple-element.33), channel_id=1, source_target_pairs={{0,4},{4,0},{8,12},{12,8},{16,20},{20,16},{24,28},{28,24},{1,5},{5... | collective-permute-start | bytes 1253384 | tf_op jit(solution)/shard_map/ppermute | solution.py:545
  224.2 8.8 %collective-permute-start.15 = (bf16[8,6528]{1,0:T(8,128)(2,1)S(1)}, bf16[8,6528]{1,0:T(8,128)(2,1)S(1)}, u32[]{:S(2)}, u32[]{:S(2)}) collective-permute-start(bf16[8,6528]{1,0:T(8,128)(2,1)S(1)} %get-tuple-element.42), channel_id=1, source_target_pairs={{0,8},{4,12},{8,0},{12,4},{16,24},{20,28},{24,16},{28,20},{1,9},{5... | collective-permute-start | bytes 313352 | tf_op jit(solution)/shard_map/ppermute | solution.py:545
  224.3 12.0 %collective-permute-start.16 = (bf16[8,6528]{1,0:T(8,128)(2,1)S(1)}, bf16[8,6528]{1,0:T(8,128)(2,1)S(1)}, u32[]{:S(2)}, u32[]{:S(2)}) collective-permute-start(bf16[8,6528]{1,0:T(8,128)(2,1)S(1)} %get-tuple-element.43), channel_id=1, source_target_pairs={{0,16},{4,20},{8,24},{12,28},{16,0},{20,4},{24,8},{28,12},{1,17},{... | collective-permute-start | bytes 313352 | tf_op jit(solution)/shard_map/ppermute | solution.py:545
  225.4 10.8 %collective-permute-start.17 = (bf16[8,6528]{1,0:T(8,128)(2,1)S(1)}, bf16[8,6528]{1,0:T(8,128)(2,1)S(1)}, u32[]{:S(2)}, u32[]{:S(2)}) collective-permute-start(bf16[8,6528]{1,0:T(8,128)(2,1)S(1)} %get-tuple-element.44), channel_id=1, source_target_pairs={{0,24},{4,28},{8,16},{12,20},{16,8},{20,12},{24,0},{28,4},{1,25},{... | collective-permute-start | bytes 313352 | tf_op jit(solution)/shard_map/ppermute | solution.py:545
  231.8 5.9 %collective-permute-start.7 = (bf16[8,6528]{1,0:T(8,128)(2,1)S(1)}, bf16[8,6528]{1,0:T(8,128)(2,1)S(1)}, u32[]{:S(2)}, u32[]{:S(2)}) collective-permute-start(bf16[8,6528]{1,0:T(8,128)(2,1)S(1)} %get-tuple-element.35), channel_id=1, source_target_pairs={{0,8},{4,12},{8,0},{12,4},{16,24},{20,28},{24,16},{28,20},{1,9},{5... | collective-permute-start | bytes 313352 | tf_op jit(solution)/shard_map/ppermute | solution.py:545
  231.9 12.9 %collective-permute-start.8 = (bf16[8,6528]{1,0:T(8,128)(2,1)S(1)}, bf16[8,6528]{1,0:T(8,128)(2,1)S(1)}, u32[]{:S(2)}, u32[]{:S(2)}) collective-permute-start(bf16[8,6528]{1,0:T(8,128)(2,1)S(1)} %get-tuple-element.36), channel_id=1, source_target_pairs={{0,16},{4,20},{8,24},{12,28},{16,0},{20,4},{24,8},{28,12},{1,17},{... | collective-permute-start | bytes 313352 | tf_op jit(solution)/shard_map/ppermute | solution.py:545
  233.0 11.8 %collective-permute-start.9 = (bf16[8,6528]{1,0:T(8,128)(2,1)S(1)}, bf16[8,6528]{1,0:T(8,128)(2,1)S(1)}, u32[]{:S(2)}, u32[]{:S(2)}) collective-permute-start(bf16[8,6528]{1,0:T(8,128)(2,1)S(1)} %get-tuple-element.37), channel_id=1, source_target_pairs={{0,24},{4,28},{8,16},{12,20},{16,8},{20,12},{24,0},{28,4},{1,25},{... | collective-permute-start | bytes 313352 | tf_op jit(solution)/shard_map/ppermute | solution.py:545
  236.5 11.1 %collective-permute-start.18 = (bf16[8,3200]{1,0:T(8,128)(2,1)S(1)}, bf16[8,3200]{1,0:T(8,128)(2,1)S(1)}, u32[]{:S(2)}, u32[]{:S(2)}) collective-permute-start(bf16[8,3200]{1,0:T(8,128)(2,1)S(1)} %shard_map.137), channel_id=1, source_target_pairs={{0,8},{4,12},{8,0},{12,4},{16,24},{20,28},{24,16},{28,20},{1,9},{5... | collective-permute-start | bytes 153608 | tf_op jit(solution)/shard_map/ppermute | solution.py:545
  236.6 13.2 %collective-permute-start.19 = (bf16[8,3200]{1,0:T(8,128)(2,1)S(1)}, bf16[8,3200]{1,0:T(8,128)(2,1)S(1)}, u32[]{:S(2)}, u32[]{:S(2)}) collective-permute-start(bf16[8,3200]{1,0:T(8,128)(2,1)S(1)} %shard_map.137), channel_id=1, source_target_pairs={{0,16},{4,20},{8,24},{12,28},{16,0},{20,4},{24,8},{28,12},{1,17},{... | collective-permute-start | bytes 153608 | tf_op jit(solution)/shard_map/ppermute | solution.py:545
  237.7 12.1 %collective-permute-start.20 = (bf16[8,3200]{1,0:T(8,128)(2,1)S(1)}, bf16[8,3200]{1,0:T(8,128)(2,1)S(1)}, u32[]{:S(2)}, u32[]{:S(2)}) collective-permute-start(bf16[8,3200]{1,0:T(8,128)(2,1)S(1)} %shard_map.137), channel_id=1, source_target_pairs={{0,24},{4,28},{8,16},{12,20},{16,8},{20,12},{24,0},{28,4},{1,25},{... | collective-permute-start | bytes 153608 | tf_op jit(solution)/shard_map/ppermute | solution.py:545
  245.0 5.9 %collective-permute-start.10 = (bf16[8,3200]{1,0:T(8,128)(2,1)S(1)}, bf16[8,3200]{1,0:T(8,128)(2,1)S(1)}, u32[]{:S(2)}, u32[]{:S(2)}) collective-permute-start(bf16[8,3200]{1,0:T(8,128)(2,1)S(1)} %shard_map.135), channel_id=1, source_target_pairs={{0,8},{4,12},{8,0},{12,4},{16,24},{20,28},{24,16},{28,20},{1,9},{5... | collective-permute-start | bytes 153608 | tf_op jit(solution)/shard_map/ppermute | solution.py:545
  247.3 5.1 %collective-permute-start.11 = (bf16[8,3200]{1,0:T(8,128)(2,1)S(1)}, bf16[8,3200]{1,0:T(8,128)(2,1)S(1)}, u32[]{:S(2)}, u32[]{:S(2)}) collective-permute-start(bf16[8,3200]{1,0:T(8,128)(2,1)S(1)} %shard_map.135), channel_id=1, source_target_pairs={{0,16},{4,20},{8,24},{12,28},{16,0},{20,4},{24,8},{28,12},{1,17},{... | collective-permute-start | bytes 153608 | tf_op jit(solution)/shard_map/ppermute | solution.py:545
  247.6 6.0 %collective-permute-start.12 = (bf16[8,3200]{1,0:T(8,128)(2,1)S(1)}, bf16[8,3200]{1,0:T(8,128)(2,1)S(1)}, u32[]{:S(2)}, u32[]{:S(2)}) collective-permute-start(bf16[8,3200]{1,0:T(8,128)(2,1)S(1)} %shard_map.135), channel_id=1, source_target_pairs={{0,24},{4,28},{8,16},{12,20},{16,8},{20,12},{24,0},{28,4},{1,25},{... | collective-permute-start | bytes 153608 | tf_op jit(solution)/shard_map/ppermute | solution.py:545
  249.8 6.3 %collective-permute-start.21 = (bf16[32,3200]{1,0:T(8,128)(2,1)S(1)}, bf16[32,3200]{1,0:T(8,128)(2,1)S(1)}, u32[]{:S(2)}, u32[]{:S(2)}) collective-permute-start(bf16[32,3200]{1,0:T(8,128)(2,1)S(1)} %pad_maximum_fusion.1.mine_ref), channel_id=1, source_target_pairs={{0,4},{4,0},{8,12},{12,8},{16,20},{20,16},{24,28},{28,24},{1,5},{5... | collective-permute-start | bytes 614408 | tf_op jit(solution)/shard_map/ppermute | solution.py:545
  253.7 5.8 %collective-permute-start.13 = (bf16[32,3200]{1,0:T(8,128)(2,1)S(1)}, bf16[32,3200]{1,0:T(8,128)(2,1)S(1)}, u32[]{:S(2)}, u32[]{:S(2)}) collective-permute-start(bf16[32,3200]{1,0:T(8,128)(2,1)S(1)} %pad_maximum_fusion.mine_ref), channel_id=1, source_target_pairs={{0,4},{4,0},{8,12},{12,8},{16,20},{20,16},{24,28},{28,24},{1,5},{5... | collective-permute-start | bytes 614408 | tf_op jit(solution)/shard_map/ppermute | solution.py:545
  261.0 4.7 %collective-permute-start.22 = (f32[16,640]{1,0:T(8,128)S(1)}, f32[16,640]{1,0:T(8,128)S(1)}, u32[]{:S(2)}, u32[]{:S(2)}) collective-permute-start(f32[16,640]{1,0:T(8,128)S(1)} %get-tuple-element.46), channel_id=1, source_target_pairs={{0,1},{1,0},{2,3},{3,2},{4,5},{5,4},{6,7},{7,6},{8,9},{9,8},{10,11... | collective-permute-start | bytes 122888 | tf_op jit(solution)/shard_map/ppermute | solution.py:545
  261.1 3.8 %collective-permute-start.23 = (bf16[16,640]{1,0:T(8,128)(2,1)S(1)}, bf16[16,640]{1,0:T(8,128)(2,1)S(1)}, u32[]{:S(2)}, u32[]{:S(2)}) collective-permute-start(bf16[16,640]{1,0:T(8,128)(2,1)S(1)} %get-tuple-element.47), channel_id=1, source_target_pairs={{0,2},{1,3},{2,0},{3,1},{4,6},{5,7},{6,4},{7,5},{8,10},{9,11},{10,... | collective-permute-start | bytes 61448 | tf_op jit(solution)/shard_map/ppermute | solution.py:545
  262.5 3.2 %collective-permute-start.24 = (bf16[16,640]{1,0:T(8,128)(2,1)S(1)}, bf16[16,640]{1,0:T(8,128)(2,1)S(1)}, u32[]{:S(2)}, u32[]{:S(2)}) collective-permute-start(bf16[16,640]{1,0:T(8,128)(2,1)S(1)} %get-tuple-element.48), channel_id=1, source_target_pairs={{0,3},{1,2},{2,1},{3,0},{4,7},{5,6},{6,5},{7,4},{8,11},{9,10},{10,... | collective-permute-start | bytes 61448 | tf_op jit(solution)/shard_map/ppermute | solution.py:545
